TPU v7x, 32 devices: a whole 2x2x4 slice. The times are simulated.
32 devices in a mesh: dp: 16 (over z, x, core), tensor: 2 (over y).
Axes of the slice: x: 2, y: 2, z: 4, core: 2. Of those that a mesh axis runs over, the one named last changes fastest.
Arguments:
- tokens: bfloat16 [8192, 2048], P('dp'), may hold values from -6 to 6
- out_grad: bfloat16 [8192, 2048], P('dp'), may hold values from -6 to 6
- lengths: int32 [8], replicated, may hold values from 1 to 4096, 8192 in all
- attn_gain: float32 [2048], replicated, may hold values from 0.5 to 1.5
- q_weight: bfloat16 [2048, 2048], P('dp', 'tensor'), may hold values from -0.125 to 0.125
- key_matrix: bfloat16 [2048, 1024], P('dp', 'tensor'), may hold values from -0.125 to 0.125
- value_matrix: bfloat16 [2048, 1024], P('dp', 'tensor'), may hold values from -0.125 to 0.125
- o_weight: bfloat16 [2048, 2048], P('dp', 'tensor'), may hold values from -0.5 to 0.5
- q_gain: float32 [128], replicated, may hold values from 1 to 2
- k_gain: float32 [128], replicated, may hold values from 0.75 to 1.5
- mlp_gain: float32 [2048], replicated, may hold values from 0.5 to 1.5
- gate_weight: bfloat16 [2048, 6144], P('dp', 'tensor'), may hold values from -0.125 to 0.125
- up_weight: bfloat16 [2048, 6144], P('dp', 'tensor'), may hold values from -0.125 to 0.125
- down_weight: bfloat16 [2048, 6144], P('dp', 'tensor'), may hold values from -0.078125 to 0.078125
Outputs:
- output: bfloat16 [8192, 2048], P('dp')
- input_grad: float32 [8192, 2048], P('dp')
- grad_attn_gain: float32 [2048], replicated
- grad_q_weight: float32 [2048, 2048], P('dp', 'tensor')
- grad_k_weight: float32 [2048, 1024], P('dp', 'tensor')
- grad_v_weight: float32 [2048, 1024], P('dp', 'tensor')
- grad_o_weight: float32 [2048, 2048], P('dp', 'tensor')
- grad_q_gain: float32 [128], replicated
- grad_k_gain: float32 [128], replicated
- grad_mlp_gain: float32 [2048], replicated
- grad_gate_weight: float32 [2048, 6144], P('dp', 'tensor')
- grad_up_weight: float32 [2048, 6144], P('dp', 'tensor')
- grad_down_weight: float32 [2048, 6144], P('dp', 'tensor')
Inputs may be any that keep to these rules, and one draw needn't show every extreme that they name: Sequence lengths in pack order; they sum to 8192 and the longest is exactly 4096.
All inputs are finite; a program needn't handle non-finite values.
Results may differ from a plain program's by a relative error of at most 0.02.
Values may be sent and summed in bfloat16 or wider, within the bound.
A program may use at most 320 MiB of HBM per device.

v0:
```python
from functools import partial
import math

import jax
import jax.numpy as jnp
from jax import lax
from jax.sharding import PartitionSpec as P

REACH = 8


EPS = 1e-06
THETA = 1000000.0
MASKED = -1e30


def shifted(value, axis, by):
    devices = lax.axis_size(axis)
    pairs = [(i, i + by) for i in range(devices) if 0 <= i + by < devices]
    return lax.ppermute(value, axis, pairs)


def rms_rows(values, gain_vec):
    return values * lax.rsqrt(jnp.mean(values * values, axis=-1, keepdims=True) + EPS) * gain_vec


def rotate(values):
    half_size = values.shape[-1] // 2
    return jnp.concatenate([-values[..., half_size:], values[..., :half_size]], axis=-1)


def head_prep(projected, gain_vec, cosine, sine_vals):
    heads_view = projected.reshape(projected.shape[0], -1, gain_vec.shape[0])
    normed = rms_rows(heads_view, gain_vec)
    return normed * cosine[:, None, :] + rotate(normed) * sine_vals[:, None, :]


def place_info(index, lengths):
    ends = jnp.cumsum(lengths)
    starts = ends - lengths
    seg_id = jnp.sum((index[:, None] >= ends[None, :]).astype(jnp.int32), axis=1)
    inside = (index[:, None] >= starts[None, :]) & (index[:, None] < ends[None, :])
    position = index - jnp.sum(jnp.where(inside, starts[None, :], 0), axis=1)
    return (seg_id, position)


def angles(position, head_dim):
    freq = THETA ** (-(jnp.arange(0, head_dim, 2, dtype=jnp.float32) / head_dim))
    turn = position.astype(jnp.float32)[:, None] * freq[None, :]
    turn = jnp.concatenate([turn, turn], axis=-1)
    return (jnp.cos(turn), jnp.sin(turn))


def local(
    tokens,
    out_grad,
    lengths,
    attn_gain,
    q_weight,
    key_matrix,
    value_matrix,
    o_weight,
    q_gain,
    k_gain,
    mlp_gain,
    gate_weight,
    up_weight,
    down_weight,
):
    row_count = tokens.shape[0]
    head_dim = q_gain.shape[0]
    score_factor_scale = 1.0 / math.sqrt(head_dim)
    devices = lax.axis_size("dp")
    my_index = lax.axis_index("dp")
    q_full, k_full, v_full, o_full = (
        lax.all_gather(q_weight, "dp", axis=0, tiled=True),
        lax.all_gather(key_matrix, "dp", axis=0, tiled=True),
        lax.all_gather(value_matrix, "dp", axis=0, tiled=True),
        lax.all_gather(o_weight, "dp", axis=0, tiled=True),
    )
    gate_full, up_full, down_full = (
        lax.all_gather(gate_weight, "dp", axis=0, tiled=True),
        lax.all_gather(up_weight, "dp", axis=0, tiled=True),
        lax.all_gather(down_weight, "dp", axis=0, tiled=True),
    )
    kv_heads = k_full.shape[1] // head_dim
    q_heads = q_full.shape[1] // head_dim
    query_group_width = q_heads // kv_heads
    local_ids = jnp.arange(row_count, dtype=jnp.int32)
    q_index = my_index * row_count + local_ids
    q_seg, q_pos = place_info(q_index, lengths)
    cosine, sine_vals = angles(q_pos, head_dim)
    prep = partial(head_prep, cosine=cosine, sine_vals=sine_vals)
    tokens_wide = tokens.astype(jnp.float32)
    first_low = rms_rows(tokens_wide, attn_gain).astype(jnp.bfloat16)
    q_proj = jnp.dot(first_low, q_full, preferred_element_type=jnp.float32)
    k_proj = jnp.dot(first_low, k_full, preferred_element_type=jnp.float32)
    value_projected = jnp.dot(first_low, v_full, preferred_element_type=jnp.float32)
    query_reduced = (
        prep(q_proj, q_gain)
        .astype(jnp.bfloat16)
        .reshape(row_count, kv_heads, query_group_width, head_dim)
    )
    key_reduced = prep(k_proj, k_gain).astype(jnp.bfloat16)
    value_reduced = value_projected.astype(jnp.bfloat16).reshape(row_count, kv_heads, head_dim)
    key_pair = jnp.stack([key_reduced, value_reduced])

    def forward_hop(retained_rows, unused):
        arrived = shifted(retained_rows, "dp", 1)
        return (arrived, arrived)

    unused_last, earlier = lax.scan(forward_hop, key_pair, None, length=REACH)
    window = jnp.concatenate([key_pair[None], earlier], axis=0)
    hop_ids = jnp.arange(REACH + 1, dtype=jnp.int32)

    def score_block(hop_id, key_tile_rows):
        source = (my_index - hop_id) % devices
        k_index = source * row_count + local_ids
        k_seg, unused_pos = place_info(k_index, lengths)
        allowed = (q_seg[:, None] == k_seg[None, :]) & (k_index[None, :] <= q_index[:, None])
        unscaled_score = (
            jnp.einsum(
                "cmyx,imx->myci", query_reduced, key_tile_rows, preferred_element_type=jnp.float32
            )
            * score_factor_scale
        )
        return jnp.where(allowed[None, None], unscaled_score, MASKED)

    def stat_step(carry, scan_item):
        row_top, row_total = carry
        hop_id, retained_rows = scan_item
        score_now = score_block(hop_id, retained_rows[0])
        new_top = jnp.maximum(row_top, jnp.max(score_now, axis=-1))
        row_total = row_total * jnp.exp(row_top - new_top) + jnp.sum(
            jnp.exp(score_now - new_top[..., None]), axis=-1
        )
        return ((new_top, row_total), None)

    stat_init = (
        jnp.full((kv_heads, query_group_width, row_count), MASKED, jnp.float32),
        jnp.zeros((kv_heads, query_group_width, row_count), jnp.float32),
    )
    (row_top, row_total), unused_stats = lax.scan(stat_step, stat_init, (hop_ids, window))
    log_total = row_top + jnp.log(row_total)

    def value_step(heads_sum, scan_item):
        hop_id, retained_rows = scan_item
        prob_reduced = jnp.exp(score_block(hop_id, retained_rows[0]) - log_total[..., None]).astype(
            jnp.bfloat16
        )
        return (
            heads_sum
            + jnp.einsum(
                "nlcu,une->cnle", prob_reduced, retained_rows[1], preferred_element_type=jnp.float32
            ),
            None,
        )

    heads_zero = jnp.zeros((row_count, kv_heads, query_group_width, head_dim), jnp.float32)
    heads_out, unused_vals = lax.scan(value_step, heads_zero, (hop_ids, window))
    attn_low = heads_out.reshape(row_count, -1).astype(jnp.bfloat16)
    attn_part = jnp.einsum("tk,dk->td", attn_low, o_full, preferred_element_type=jnp.float32)
    attn_out = lax.psum(attn_part.astype(jnp.bfloat16), "tensor").astype(jnp.float32)
    middle = tokens_wide + attn_out
    second_low = rms_rows(middle, mlp_gain).astype(jnp.bfloat16)
    gate_pre = jnp.dot(second_low, gate_full, preferred_element_type=jnp.float32)
    up_pre = jnp.dot(second_low, up_full, preferred_element_type=jnp.float32)
    act_low = (jax.nn.silu(gate_pre) * up_pre).astype(jnp.bfloat16)
    mlp_part = jnp.einsum("tf,df->td", act_low, down_full, preferred_element_type=jnp.float32)
    mlp_out = lax.psum(mlp_part.astype(jnp.bfloat16), "tensor").astype(jnp.float32)
    output = (middle + mlp_out).astype(jnp.bfloat16)
    grad_down = jnp.einsum("td,tf->df", out_grad, act_low, preferred_element_type=jnp.float32)
    d_act = jnp.dot(out_grad, down_full, preferred_element_type=jnp.float32)
    sigmoid_gate = jax.nn.sigmoid(gate_pre)
    d_gate = (d_act * up_pre * sigmoid_gate * (1.0 + gate_pre * (1.0 - sigmoid_gate))).astype(
        jnp.bfloat16
    )
    d_up = (d_act * gate_pre * sigmoid_gate).astype(jnp.bfloat16)
    grad_gate = jnp.einsum("td,tf->df", second_low, d_gate, preferred_element_type=jnp.float32)
    grad_up = jnp.einsum("td,tf->df", second_low, d_up, preferred_element_type=jnp.float32)
    d_second_part = jnp.einsum(
        "tf,df->td", d_gate, gate_full, preferred_element_type=jnp.float32
    ) + jnp.einsum("tf,df->td", d_up, up_full, preferred_element_type=jnp.float32)
    d_second = lax.psum(d_second_part.astype(jnp.bfloat16), "tensor").astype(jnp.float32)
    unused_mid, norm_back_mid = jax.vjp(rms_rows, middle, mlp_gain)
    d_middle_norm, grad_mlp_gain = norm_back_mid(d_second)
    d_middle = out_grad.astype(jnp.float32) + d_middle_norm
    d_attn = d_middle.astype(jnp.bfloat16)
    grad_o = jnp.einsum("td,tk->dk", d_attn, attn_low, preferred_element_type=jnp.float32)
    heads_gradient = jnp.dot(d_attn, o_full, preferred_element_type=jnp.float32).astype(
        jnp.bfloat16
    )
    heads_gradient = heads_gradient.reshape(row_count, kv_heads, query_group_width, head_dim)
    row_dot = jnp.transpose(
        jnp.sum(heads_gradient.astype(jnp.float32) * heads_out, axis=-1), (1, 2, 0)
    )

    def grad_step(d_query, scan_item):
        hop_id, retained_rows = scan_item
        prob_full = jnp.exp(score_block(hop_id, retained_rows[0]) - log_total[..., None])
        prob_reduced = prob_full.astype(jnp.bfloat16)
        d_value = jnp.einsum(
            "ivah,aivc->hic", prob_reduced, heads_gradient, preferred_element_type=jnp.float32
        )
        prob_gradient = jnp.einsum(
            "cmyx,imx->myci", heads_gradient, retained_rows[1], preferred_element_type=jnp.float32
        )
        score_gradient = (prob_full * (prob_gradient - row_dot[..., None])).astype(jnp.bfloat16)
        d_query = (
            d_query
            + jnp.einsum(
                "nlcu,une->cnle",
                score_gradient,
                retained_rows[0],
                preferred_element_type=jnp.float32,
            )
            * score_factor_scale
        )
        d_key = (
            jnp.einsum(
                "ivah,aivc->hic", score_gradient, query_reduced, preferred_element_type=jnp.float32
            )
            * score_factor_scale
        )
        return (d_query, jnp.stack([d_key, d_value]))

    d_query, key_grads = lax.scan(grad_step, heads_zero, (hop_ids, window))

    def back_hop(carried, own_part):
        arrived = shifted(carried.astype(jnp.bfloat16), "dp", -1).astype(carried.dtype)
        return (arrived + own_part, None)

    home_grads, unused_back = lax.scan(back_hop, key_grads[REACH], key_grads[:REACH][::-1])
    unused_q, q_back = jax.vjp(prep, q_proj, q_gain)
    d_q_proj, q_gain_part = q_back(d_query.reshape(row_count, q_heads, head_dim))
    unused_k, k_back = jax.vjp(prep, k_proj, k_gain)
    d_k_proj, k_gain_part = k_back(home_grads[0])
    dq_low = d_q_proj.astype(jnp.bfloat16)
    dk_low = d_k_proj.astype(jnp.bfloat16)
    dv_low = home_grads[1].reshape(row_count, -1).astype(jnp.bfloat16)
    grad_q = jnp.einsum("td,tk->dk", first_low, dq_low, preferred_element_type=jnp.float32)
    grad_k = jnp.einsum("td,tk->dk", first_low, dk_low, preferred_element_type=jnp.float32)
    grad_v = jnp.einsum("td,tk->dk", first_low, dv_low, preferred_element_type=jnp.float32)
    d_first_part = (
        jnp.einsum("tk,dk->td", dq_low, q_full, preferred_element_type=jnp.float32)
        + jnp.einsum("tk,dk->td", dk_low, k_full, preferred_element_type=jnp.float32)
        + jnp.einsum("tk,dk->td", dv_low, v_full, preferred_element_type=jnp.float32)
    )
    d_first, q_gain_local, k_gain_local = (
        lax.psum(d_first_part.astype(jnp.bfloat16), "tensor").astype(jnp.float32),
        lax.psum(q_gain_part.astype(jnp.bfloat16), "tensor").astype(jnp.float32),
        lax.psum(k_gain_part.astype(jnp.bfloat16), "tensor").astype(jnp.float32),
    )
    unused_in, norm_back_in = jax.vjp(rms_rows, tokens_wide, attn_gain)
    d_tokens_norm, grad_attn_local = norm_back_in(d_first)
    input_grad = d_middle + d_tokens_norm
    gain_grads = lax.psum((grad_attn_local, q_gain_local, k_gain_local, grad_mlp_gain), "dp")
    weight_grads = (
        lax.psum_scatter(grad_q, "dp", scatter_dimension=0, tiled=True),
        lax.psum_scatter(grad_k, "dp", scatter_dimension=0, tiled=True),
        lax.psum_scatter(grad_v, "dp", scatter_dimension=0, tiled=True),
        lax.psum_scatter(grad_o, "dp", scatter_dimension=0, tiled=True),
        lax.psum_scatter(grad_gate, "dp", scatter_dimension=0, tiled=True),
        lax.psum_scatter(grad_up, "dp", scatter_dimension=0, tiled=True),
        lax.psum_scatter(grad_down, "dp", scatter_dimension=0, tiled=True),
    )
    return (
        output,
        input_grad,
        gain_grads[0],
        weight_grads[0],
        weight_grads[1],
        weight_grads[2],
        weight_grads[3],
        gain_grads[1],
        gain_grads[2],
        gain_grads[3],
        weight_grads[4],
        weight_grads[5],
        weight_grads[6],
    )


def solution(mesh):
    placed = (
        P("dp", None),
        P("dp", None),
        P(),
        P(),
        P("dp", "tensor"),
        P("dp", "tensor"),
        P("dp", "tensor"),
        P("dp", "tensor"),
        P(),
        P(),
        P(),
        P("dp", "tensor"),
        P("dp", "tensor"),
        P("dp", "tensor"),
    )
    return jax.shard_map(
        local,
        mesh=mesh,
        in_specs=placed,
        out_specs=(
            P("dp", None),
            P("dp", None),
            P(),
            P("dp", "tensor"),
            P("dp", "tensor"),
            P("dp", "tensor"),
            P("dp", "tensor"),
            P(),
            P(),
            P(),
            P("dp", "tensor"),
            P("dp", "tensor"),
            P("dp", "tensor"),
        ),
        check_vma=False,
    )
```

profile of v0, /device:TPU:0, one launch (start us, length us, event | category | flops | bytes accessed | tf_op | source)
XLA Modules:
  0.0 2535.7 jit_solution(4320080775099622056)
XLA Ops:
  17.2 37.1 %all-gather.8.cloned.1.call-done = bf16[2048,512]{1,0:T(8,128)(2,1)} async-done(((bf16[128,512]{1,0:T(8,128)(2,1)}), bf16[2048,512]{1,0:T(8,128)(2,1)}) %all-gather.8.cloned.1.call-update) | async-done | bytes 2097168 | tf_op jit(solution)/shard_map/all_gather | solution.py:77
  59.5 37.2 %all-gather.10.cloned.1.call-done = bf16[2048,512]{1,0:T(8,128)(2,1)} async-done(((bf16[128,512]{1,0:T(8,128)(2,1)}), bf16[2048,512]{1,0:T(8,128)(2,1)}) %all-gather.10.cloned.1.call-update) | async-done | bytes 2097168 | tf_op jit(solution)/shard_map/all_gather | solution.py:78
  104.6 160.8 %while.65 = (s32[]{:T(128)}, bf16[2,512,4,128]{3,2,1,0:T(4,128)(2,1)}, bf16[8,2,512,4,128]{4,2,3,1,0:T(8,128)(2,1)}, s32[]{:T(128)}) while((s32[]{:T(128)}, bf16[2,512,4,128]{3,2,1,0:T(4,128)(2,1)}, bf16[8,2,512,4,128]{4,2,3,1,0:T(8,128)(2,1)}, s32[]{:T(128)}) %tuple.157), condition=%wide.region_5.6_spmd, body=%wide.region_4.5_spmd.sunk | while | flops 2 | bytes 8388713 | solution.py:112
  111.3 13.2 collective-permute-start
  129.0 23.4 collective-permute-start
  157.0 16.2 collective-permute-start
  177.7 18.8 collective-permute-start
  201.0 13.9 collective-permute-start
  219.4 22.1 collective-permute-start
  246.0 14.8 collective-permute-start
  265.4 8.0 pad_maximum_fusion
  300.5 54.8 %while.67 = (s32[]{:T(128)}, f32[4,2,512]{2,1,0:T(2,128)S(1)}, f32[4,2,512]{2,1,0:T(2,128)S(1)}, s32[512]{0:T(512)S(1)}, s32[9]{0:T(128)S(1)}, /*index=5*/s32[]{...) while((s32[]{:T(128)}, f32[4,2,512]{2,1,0:T(2,128)S(1)}, ...), condition=%wide.region_13.14_spmd.clone, body=%wide.region_9.13_spmd.clone.sunk | while | flops 552370688 | bytes 19366236 | solution.py:143
  355.4 68.6 %while.68 = (s32[]{:T(128)}, f32[512,4,2,128]{0,3,2,1:T(8,128)}, bf16[9,2,512,4,128]{4,2,3,1,0:T(8,128)(2,1)}, s32[512]{0:T(512)S(1)}, s32[9]{0:T(128)S(1)}, /*i...) while((s32[]{:T(128)}, f32[512,4,2,128]{0,3,2,1:T(8,128)}, ...), condition=%wide.region_16.17_spmd.clone, body=%wide.region_14.16_spmd.clone.sunk | while | flops 1083978240 | bytes 6850923 | solution.py:160
  435.0 90.0 %all-reduce.11.cloned.1.call-done = bf16[512,2048]{1,0:T(8,128)(2,1)} async-done(((bf16[512,2048]{1,0:T(8,128)(2,1)}), bf16[512,2048]{1,0:T(8,128)(2,1)}) %all-reduce.11.cloned.1.call-update) | async-done | bytes 2097168 | tf_op jit(solution)/shard_map/psum | solution.py:163
  529.9 98.3 %all-gather.18.cloned.1.call-done = bf16[2048,3072]{1,0:T(8,128)(2,1)} async-done(((bf16[128,3072]{1,0:T(8,128)(2,1)}), bf16[2048,3072]{1,0:T(8,128)(2,1)}) %all-gather.18.cloned.1.call-update) | async-done | bytes 12582928 | tf_op jit(solution)/shard_map/all_gather | solution.py:83
  628.2 12.1 fusion.109
  640.3 89.4 %all-gather.16.cloned.1.call-done = bf16[2048,3072]{1,0:T(8,128)(2,1)} async-done(((bf16[128,3072]{1,0:T(8,128)(2,1)}), bf16[2048,3072]{1,0:T(8,128)(2,1)}) %all-gather.16.cloned.1.call-update) | async-done | bytes 12582928 | tf_op jit(solution)/shard_map/all_gather | solution.py:82
  729.7 11.9 fusion.108
  741.6 89.6 %all-gather.20.cloned.1.call-done = bf16[2048,3072]{1,0:T(8,128)(2,1)} async-done(((bf16[128,3072]{1,0:T(8,128)(2,1)}), bf16[2048,3072]{1,0:T(8,128)(2,1)}) %all-gather.20.cloned.1.call-update) | async-done | bytes 12582928 | tf_op jit(solution)/shard_map/all_gather | solution.py:84
  831.2 16.2 multiply_convert_fusion
  847.4 13.3 fusion.110
  860.7 13.3 add_convert_fusion.1
  874.1 11.7 convolution_convert_fusion
  885.8 49.5 %all-reduce.13.cloned.1.call-done = bf16[512,2048]{1,0:T(8,128)(2,1)} async-done(((bf16[512,2048]{1,0:T(8,128)(2,1)}), bf16[512,2048]{1,0:T(8,128)(2,1)}) %all-reduce.13.cloned.1.call-update) | async-done | bytes 2097168 | tf_op jit(solution)/shard_map/psum | solution.py:184
  957.3 137.6 %while.69 = (s32[]{:T(128)}, f32[512,4,2,128]{0,3,2,1:T(8,128)S(1)}, f32[9,2,512,4,128]{4,2,3,1,0:T(8,128)}, bf16[9,2,512,4,128]{4,2,3,1,0:T(8,128)(2,1)}, s32[5...) while((s32[]{:T(128)}, ...), condition=%wide.region_25.26_spmd.clone, body=%wide.region_23.25_spmd.clone.sunk | while | flops 2708484608 | bytes 59048368 | solution.py:227
  1098.7 11.5 slice.66
  1110.2 11.5 rev.3
  1124.7 143.7 %while.66 = (s32[]{:T(128)}, f32[2,512,4,128]{3,2,1,0:T(4,128)S(1)}, f32[8,2,512,4,128]{4,2,3,1,0:T(8,128)}, s32[]{:T(128)}) while((s32[]{:T(128)}, f32[2,512,4,128]{3,2,1,0:T(4,128)S(1)}, f32[8,2,512,4,128]{4,2,3,1,0:T(8,128)}, s32[]{:T(128)}) %tuple.169), condition=%wide.region_28.29_spmd, body=%wide.region_27.28_spmd.sunk | while | flops 1572866 | bytes 16777320 | solution.py:233
  1136.1 12.5 collective-permute-done.1
  1154.9 13.2 collective-permute-done.1
  1174.4 13.2 collective-permute-done.1
  1193.9 13.2 collective-permute-done.1
  1213.3 13.2 collective-permute-done.1
  1232.8 13.2 collective-permute-done.1
  1252.3 13.2 collective-permute-done.1
  1288.4 13.7 convolution_bitcast_fusion.1
  1312.9 10.0 fusion.76
  1330.4 14.2 fusion.114
  1344.6 13.9 fusion.113
  1363.5 49.7 %all-reduce.15.cloned.1.call-done = (bf16[512,2048]{1,0:T(8,128)(2,1)}, bf16[512,2048]{1,0:T(8,128)(2,1)}) async-done(((bf16[512,2048]{1,0:T(8,128)(2,1)}, bf16[512,2048]{1,0:T(8,128)(2,1)}), (bf16[512,2048]{1,0:T(8,128)(2,1)}, bf16[512,2048]{1,0:T(8,128)(2,1)})) %all-reduce.15.cloned.1.call-update) | async-done | bytes 4194320 | tf_op jit(solution)/shard_map/psum | solution.py:170
  1416.5 62.0 %all-reduce.4 = (f32[2048]{0:T(1024)}, f32[128]{0:T(128)}, f32[128]{0:T(128)}, f32[2048]{0:T(1024)}) all-reduce(f32[2048]{0:T(1024)S(1)} %get-tuple-element.785, bf16[128]{0:T(256)(128)(2,1)S(1)} %get-tuple-element.875, bf16[128]{0:T(256)(128)(2,1)S(1)} %get-tuple-element.876, ...), channel_id=1, replica_groups=mesh['dp'=16,'tensor'=2] {'dp'}, use_global_device_ids=true, to_apply=%region_33.34 | all-reduce | flops 4352 | bytes 34304 | tf_op jit(solution)/shard_map/psum | solution.py:257
  1486.5 175.1 %reduce-scatter.20.cloned.1.call-done = f32[128,3072]{0,1:T(8,128)} async-done(((f32[2048,3072]{0,1:T(8,128)}), f32[128,3072]{0,1:T(8,128)}) %reduce-scatter.20.cloned.1.call-update) | async-done | bytes 1572880 | tf_op jit(solution)/shard_map/reduce_scatter | solution.py:265
  1664.6 73.4 %reduce-scatter.12.cloned.1.call-done = f32[128,512]{1,0:T(8,128)} async-done(((f32[2048,512]{1,0:T(8,128)}), f32[128,512]{1,0:T(8,128)}) %reduce-scatter.12.cloned.1.call-update) | async-done | bytes 262160 | tf_op jit(solution)/shard_map/reduce_scatter | solution.py:261
  1738.0 75.8 %reduce-scatter.10.cloned.1.call-done = f32[128,512]{1,0:T(8,128)} async-done(((f32[2048,512]{1,0:T(8,128)}), f32[128,512]{1,0:T(8,128)}) %reduce-scatter.10.cloned.1.call-update) | async-done | bytes 262160 | tf_op jit(solution)/shard_map/reduce_scatter | solution.py:260
  1813.8 108.8 %reduce-scatter.14.cloned.1.call-done = f32[128,1024]{1,0:T(8,128)} async-done(((f32[2048,1024]{1,0:T(8,128)}), f32[128,1024]{1,0:T(8,128)}) %reduce-scatter.14.cloned.1.call-update) | async-done | bytes 524304 | tf_op jit(solution)/shard_map/reduce_scatter | solution.py:262
  1922.6 109.4 %reduce-scatter.8.cloned.1.call-done = f32[128,1024]{1,0:T(8,128)} async-done(((f32[2048,1024]{1,0:T(8,128)}), f32[128,1024]{1,0:T(8,128)}) %reduce-scatter.8.cloned.1.call-update) | async-done | bytes 524304 | tf_op jit(solution)/shard_map/reduce_scatter | solution.py:259
  2032.0 248.6 %reduce-scatter.18.cloned.1.call-done = f32[128,3072]{1,0:T(8,128)} async-done(((f32[2048,3072]{1,0:T(8,128)}), f32[128,3072]{1,0:T(8,128)}) %reduce-scatter.18.cloned.1.call-update) | async-done | bytes 1572880 | tf_op jit(solution)/shard_map/reduce_scatter | solution.py:264
  2280.6 248.0 %reduce-scatter.16.cloned.1.call-done = f32[128,3072]{1,0:T(8,128)} async-done(((f32[2048,3072]{1,0:T(8,128)}), f32[128,3072]{1,0:T(8,128)}) %reduce-scatter.16.cloned.1.call-update) | async-done | bytes 1572880 | tf_op jit(solution)/shard_map/reduce_scatter | solution.py:263
  (518 shorter events, 482.8 us)
Async XLA Ops:
  7.2 47.2 %copy-start = (bf16[512,2048]{1,0:T(8,128)(2,1)S(1)}, bf16[512,2048]{1,0:T(8,128)(2,1)}, u32[]{:S(2)}) copy-start(bf16[512,2048]{1,0:T(8,128)(2,1)} %param.24) | copy-start | bytes 6291460
  7.2 47.1 %copy-start.30 = (f32[2048]{0:T(1024)S(1)}, f32[2048]{0:T(1024)}, u32[]{:S(2)}) copy-start(f32[2048]{0:T(1024)} %param.27) | copy-start | bytes 24580
  7.2 47.1 %all-gather.8.cloned.1.call-start = ((), (), s32[]{:S(2)}) async-start(), calls=%async_computation.7 | async-start | bytes 2228224 | tf_op jit(solution)/shard_map/all_gather | solution.py:77
  7.9 88.8 %all-gather.10.cloned.1.call-start = ((), (), s32[]{:S(2)}) async-start(), calls=%async_computation.8 | async-start | bytes 2228224 | tf_op jit(solution)/shard_map/all_gather | solution.py:78
  8.7 264.8 %all-gather.12.cloned.1.call-start = ((), (), s32[]{:S(2)}) async-start(), calls=%async_computation.9 | async-start | bytes 4456448 | tf_op jit(solution)/shard_map/all_gather | solution.py:76
  9.4 417.2 %all-gather.14.cloned.1.call-start = ((), (), s32[]{:S(2)}) async-start(), calls=%async_computation.10 | async-start | bytes 4456448 | tf_op jit(solution)/shard_map/all_gather | solution.py:79
  10.0 515.0 %all-reduce.11.cloned.1.call-start = ((), (), s32[]{:S(2)}) async-start(), calls=%async_computation.11 | async-start | bytes 4194304 | tf_op jit(solution)/shard_map/psum | solution.py:163
  14.5 258.9 %copy-start.38 = (f32[512]{0:T(512)}, f32[512]{0:T(512)S(1)}, u32[]{:S(2)}) copy-start(f32[512]{0:T(512)S(1)} %fusion.90) | copy-start | bytes 6148
  16.2 41.5 %copy-start.12 = (f32[512,128]{0,1:T(8,128)}, f32[512,128]{0,1:T(8,128)S(1)}, u32[]{:S(2)}) copy-start(f32[512,128]{0,1:T(8,128)S(1)} %get-tuple-element.904) | copy-start | bytes 786436
  16.2 41.5 %copy-start.14 = (f32[512,128]{0,1:T(8,128)}, f32[512,128]{0,1:T(8,128)S(1)}, u32[]{:S(2)}) copy-start(f32[512,128]{0,1:T(8,128)S(1)} %get-tuple-element.905) | copy-start | bytes 786436
  17.2 40.1 %copy-start.49 = (f32[128]{0:T(128)S(1)}, f32[128]{0:T(128)}, u32[]{:S(2)}) copy-start(f32[128]{0:T(128)} %param.33) | copy-start | bytes 1540
  57.3 42.4 %copy-start.43 = (f32[512,4]{0,1:T(4,128)}, f32[512,4]{0,1:T(4,128)S(1)}, u32[]{:S(2)}) copy-start(f32[512,4]{0,1:T(4,128)S(1)} %get-tuple-element.906) | copy-start | bytes 24580
  57.4 42.4 %copy-start.32 = (f32[512,4]{0,1:T(4,128)}, f32[512,4]{0,1:T(4,128)S(1)}, u32[]{:S(2)}) copy-start(f32[512,4]{0,1:T(4,128)S(1)} %fusion.89) | copy-start | bytes 24580
  104.6 4.6 collective-permute-start
  111.3 15.6 collective-permute-start
  129.0 25.9 %collective-permute-start = (bf16[2,512,4,128]{3,2,1,0:T(4,128)(2,1)}, bf16[2,512,4,128]{3,2,1,0:T(4,128)(2,1)S(1)}, u32[]{:S(2)}, u32[]{:S(2)}) collective-permute-start(bf16[2,512,4,128]{3,2,1,0:T(4,128)(2,1)} %get-tuple-element.1168), channel_id=1, source_target_pairs={{0,2},{2,4},{4,6},{6,8},{8,10},{10,12},{12,14},{14,16},{16,18},{18... | collective-permute-start | bytes 3145736 | tf_op jit(solution)/shard_map/while/body/eval_jaxpr/ppermute | solution.py:20
  157.0 18.6 collective-permute-start
  177.7 21.2 collective-permute-start
  201.0 16.3 collective-permute-start
  219.4 24.5 collective-permute-start
  246.0 17.2 collective-permute-start
  432.9 94.7 %copy-start.36 = (f32[2048]{0:T(1024)S(1)}, f32[2048]{0:T(1024)}, u32[]{:S(2)}) copy-start(f32[2048]{0:T(1024)} %param.34) | copy-start | bytes 24580
  432.9 195.3 %all-gather.18.cloned.1.call-start = ((), (), s32[]{:S(2)}) async-start(), calls=%async_computation.13 | async-start | bytes 13369344 | tf_op jit(solution)/shard_map/all_gather | solution.py:83
  433.5 296.2 %all-gather.16.cloned.1.call-start = ((), (), s32[]{:S(2)}) async-start(), calls=%async_computation.12 | async-start | bytes 13369344 | tf_op jit(solution)/shard_map/all_gather | solution.py:82
  434.2 397.0 %all-gather.20.cloned.1.call-start = ((), (), s32[]{:S(2)}) async-start(), calls=%async_computation.14 | async-start | bytes 13369344 | tf_op jit(solution)/shard_map/all_gather | solution.py:84
  435.0 500.3 %all-reduce.13.cloned.1.call-start = ((), (), s32[]{:S(2)}) async-start(), calls=%async_computation.15 | async-start | bytes 4194304 | tf_op jit(solution)/shard_map/psum | solution.py:184
  527.5 412.5 %copy-start.40 = (f32[512]{0:T(512)}, f32[512]{0:T(512)S(1)}, u32[]{:S(2)}) copy-start(f32[512]{0:T(512)S(1)} %fusion.91) | copy-start | bytes 6148
  847.4 13.3 copy-start.54
  847.4 13.3 copy-start.55
  874.1 539.2 %all-reduce.15.cloned.1.call-start = ((), (), s32[]{:S(2)}) async-start(), calls=%async_computation.23 | async-start | bytes 8388608 | tf_op jit(solution)/shard_map/psum | solution.py:170
  1094.9 15.4 copy-start.3
  1125.1 4.7 collective-permute-start.1
  1133.0 15.6 collective-permute-start.1
  1151.8 16.2 collective-permute-start.1
  1171.3 16.2 collective-permute-start.1
  1190.8 16.2 collective-permute-start.1
  1210.3 16.2 collective-permute-start.1
  1229.8 16.2 collective-permute-start.1
  1249.3 16.2 collective-permute-start.1
  1286.8 374.8 %reduce-scatter.20.cloned.1.call-start = ((), (), s32[]{:S(2)}) async-start(), calls=%async_computation.22 | async-start | bytes 26738688 | tf_op jit(solution)/shard_map/reduce_scatter | solution.py:265
  1302.2 435.8 %reduce-scatter.12.cloned.1.call-start = ((), (), s32[]{:S(2)}) async-start(), calls=%async_computation.18 | async-start | bytes 4456448 | tf_op jit(solution)/shard_map/reduce_scatter | solution.py:261
  1307.2 506.6 %reduce-scatter.10.cloned.1.call-start = ((), (), s32[]{:S(2)}) async-start(), calls=%async_computation.17 | async-start | bytes 4456448 | tf_op jit(solution)/shard_map/reduce_scatter | solution.py:260
  1311.7 610.9 %reduce-scatter.14.cloned.1.call-start = ((), (), s32[]{:S(2)}) async-start(), calls=%async_computation.19 | async-start | bytes 8912896 | tf_op jit(solution)/shard_map/reduce_scatter | solution.py:262
  1322.9 709.1 %reduce-scatter.8.cloned.1.call-start = ((), (), s32[]{:S(2)}) async-start(), calls=%async_computation.16 | async-start | bytes 8912896 | tf_op jit(solution)/shard_map/reduce_scatter | solution.py:259
  1330.1 950.6 %reduce-scatter.18.cloned.1.call-start = ((), (), s32[]{:S(2)}) async-start(), calls=%async_computation.21 | async-start | bytes 26738688 | tf_op jit(solution)/shard_map/reduce_scatter | solution.py:264
  1344.6 1184.1 %reduce-scatter.16.cloned.1.call-start = ((), (), s32[]{:S(2)}) async-start(), calls=%async_computation.20 | async-start | bytes 26738688 | tf_op jit(solution)/shard_map/reduce_scatter | solution.py:263
  1358.5 58.0 %copy-start.42 = (f32[2048]{0:T(1024)S(1)}, f32[2048]{0:T(1024)}, u32[]{:S(2)}) copy-start(f32[2048]{0:T(1024)} %get-tuple-element.783) | copy-start | bytes 24580
  1358.5 120.0 %copy-start.46 = (f32[512]{0:T(512)S(1)}, f32[512]{0:T(512)}, u32[]{:S(2)}) copy-start(f32[512]{0:T(512)} %copy-done.45) | copy-start | bytes 6148
  (49 other events, 123.3 us)
Sparse Core Ops, SparseCore 0:
  10.2 44.0 all-gather.7
  56.5 40.1 all-gather.9
  98.9 54.6 all-gather.11
  155.6 56.2 all-gather.13
  433.0 91.9 all-reduce.10
  527.4 100.7 all-gather.17
  630.7 98.9 all-gather.15
  732.2 98.9 all-gather.19
  874.2 61.0 all-reduce.12
  1287.0 126.2 all-reduce.14
  1417.9 243.6 reduce-scatter.19
  1666.4 71.5 reduce-scatter.11
  1742.4 71.2 reduce-scatter.9
  1818.8 103.7 reduce-scatter.13
  1927.6 104.3 reduce-scatter.7
  2037.1 243.5 reduce-scatter.17
  2285.7 242.9 reduce-scatter.15
where the time goes:
time: 2550 us; the launch traced here: 2540 us
  waiting for transfers between devices  1700 us (67%)
  matrix products  359 us (14%)
  starting transfers between devices  136 us (5%)
  other arithmetic  121 us (5%)
  local copies, waits for them, and re-layouts  120 us (5%)
  blocking collectives  66.9 us (3%)
    reduce_scatter x1, waiting for transfers between devices, local(): lax.psum_scatter(grad_up, 'dp', scatter_dimension=0, tiled=True)  249 us
    reduce_scatter x1, waiting for transfers between devices, local(): lax.psum_scatter(grad_gate, 'dp', scatter_dimension=0, tiled=True)  248 us
    reduce_scatter x1, waiting for transfers between devices, local(): lax.psum_scatter(grad_down, 'dp', scatter_dimension=0, tiled=True)  175 us
    ppermute x16, starting transfers between devices, shifted(): return lax.ppermute(value, axis, pairs)  135 us
    ppermute x16, waiting for transfers between devices, shifted(): return lax.ppermute(value, axis, pairs)  113 us
    reduce_scatter x1, waiting for transfers between devices, local(): lax.psum_scatter(grad_q, 'dp', scatter_dimension=0, tiled=True)  109 us
    reduce_scatter x1, waiting for transfers between devices, local(): lax.psum_scatter(grad_o, 'dp', scatter_dimension=0, tiled=True)  109 us
    all_gather x1, waiting for transfers between devices, local(): lax.all_gather(up_weight, 'dp', axis=0, tiled=True)  98.3 us
  transfers between devices with their start and end apart: 33, of which 31 were waited for; matrix products, arithmetic and copies ran while one was open for 12% of the time, Pallas kernels for 0%

commit v1 on v0

v1 whole, which is shorter than its diff:
```python
from functools import partial
import math

import jax
import jax.numpy as jnp
from jax import lax
from jax.experimental import pallas as pl
from jax.experimental.pallas import tpu as pltpu
from jax.sharding import PartitionSpec as P

REACH = 8
EPS = 1e-06
THETA = 1000000.0
LOG2E = 1.4426950408889634
F32 = jnp.float32
BF16 = jnp.bfloat16
VMEM_LIMIT = 60 * 1024 * 1024

NT = (((1,), (1,)), ((), ()))
NN = (((1,), (0,)), ((), ()))
TN = (((0,), (0,)), ((), ()))
MESH = pl.DeviceIdType.MESH


def dot(a, b, dims=NN):
    return lax.dot_general(a, b, dims, preferred_element_type=F32)


def over_quads(value, by):
    n = lax.axis_size("dp")
    return lax.ppermute(value, "dp", [(i, (i + 4 * by) % n) for i in range(n)])


def shift_quads(value, by):
    n = lax.axis_size("dp")
    return lax.ppermute(
        value, "dp", [(i, i + 4 * by) for i in range(n) if 0 <= i + 4 * by < n]
    )


def swap_x(value):
    return lax.ppermute(value, "dp", [(i, i ^ 2) for i in range(lax.axis_size("dp"))])


def swap_core(value):
    return lax.ppermute(value, "dp", [(i, i ^ 1) for i in range(lax.axis_size("dp"))])


def swap_tensor(value):
    return lax.ppermute(value, "tensor", [(0, 1), (1, 0)])


def tensor_sum(part):
    low = part.astype(BF16)
    return low.astype(F32) + swap_tensor(low).astype(F32)


def rms_rows(values, gain_vec):
    return values * lax.rsqrt(jnp.mean(values * values, axis=-1, keepdims=True) + EPS) * gain_vec


def rotate(values):
    half_size = values.shape[-1] // 2
    return jnp.concatenate([-values[..., half_size:], values[..., :half_size]], axis=-1)


def head_prep(heads_view, gain_vec, cosine, sine_vals):
    normed = rms_rows(heads_view, gain_vec)
    return normed * cosine[:, None, :] + rotate(normed) * sine_vals[:, None, :]


def starts_of(index, lengths):
    ends = jnp.cumsum(lengths)
    starts = ends - lengths
    inside = (index[:, None] >= starts[None, :]) & (index[:, None] < ends[None, :])
    return jnp.sum(jnp.where(inside, starts[None, :], 0), axis=1)


def angles(position, head_dim):
    freq = THETA ** (-(jnp.arange(0, head_dim, 2, dtype=F32) / head_dim))
    turn = position.astype(F32)[:, None] * freq[None, :]
    turn = jnp.concatenate([turn, turn], axis=-1)
    return (jnp.cos(turn), jnp.sin(turn))


def attn_bwd_kernel(
    rows, blocks, info, q_ref, g_ref, k_ref, v_ref, start_ref, l_ref, r_ref, dq_ref, dk_ref, dv_ref
):
    i = pl.program_id(0)
    d = k_ref.shape[1]
    scale = 1.0 / math.sqrt(d)

    @pl.when(i == 0)
    def _():
        dk_ref[...] = jnp.zeros_like(dk_ref)
        dv_ref[...] = jnp.zeros_like(dv_ref)

    dq_ref[...] = jnp.zeros_like(dq_ref)
    q2 = jnp.concatenate([q_ref[:, :d], q_ref[:, d:]], axis=0)
    g2 = jnp.concatenate([g_ref[:, :d], g_ref[:, d:]], axis=0)
    log_total = jnp.concatenate([l_ref[0:1, :], l_ref[1:2, :]], axis=1)
    row_dot = jnp.concatenate([r_ref[0:1, :], r_ref[1:2, :]], axis=1)
    q_block = info[0, i]

    def step(j, carry):
        k_block = info[1, j]
        need = (k_block <= q_block) & (k_block >= 0) & (k_block * rows + rows - 1 >= info[2, i])
        whole = (k_block < q_block) & (k_block * rows >= info[3, i])
        at = pl.ds(pl.multiple_of(j * rows, rows), rows)

        def part(masked):
            k_now = k_ref[at, :]
            score = dot(k_now, q2, NT)
            prob = jnp.exp2(score * (scale * LOG2E) - log_total)
            if masked:
                k_pos = k_block * rows + lax.broadcasted_iota(jnp.int32, (rows, rows), 0)
                q_pos = q_block * rows + lax.broadcasted_iota(jnp.int32, (rows, rows), 1)
                keep = (k_pos <= q_pos) & (k_pos >= start_ref[...])
                prob = jnp.where(jnp.concatenate([keep, keep], axis=1), prob, 0.0)
            d_prob = dot(v_ref[at, :], g2, NT)
            d_score = (prob * (d_prob - row_dot)).astype(BF16)
            dv_ref[at, :] += dot(prob.astype(BF16), g2)
            dk_ref[at, :] += dot(d_score, q2)
            d_q = dot(d_score, k_now, TN)
            dq_ref[:, :d] += d_q[:rows]
            dq_ref[:, d:] += d_q[rows:]

        pl.when(need & whole)(lambda: part(False))
        pl.when(need & jnp.logical_not(whole))(lambda: part(True))
        return carry

    lax.fori_loop(0, blocks, step, 0)


def attn_bwd(info, q, g, k, v, start, log_total, row_dot, rows):
    n_q, width = q.shape[0] // rows, q.shape[1]
    blocks = k.shape[0] // rows
    whole = lambda i, s: (0, 0)
    part = lambda i, s: (i, 0)
    row = lambda i, s: (0, i)
    return pl.pallas_call(
        partial(attn_bwd_kernel, rows, blocks),
        grid_spec=pltpu.PrefetchScalarGridSpec(
            num_scalar_prefetch=1,
            grid=(n_q,),
            in_specs=[
                pl.BlockSpec((rows, width), part),
                pl.BlockSpec((rows, width), part),
                pl.BlockSpec(k.shape, whole),
                pl.BlockSpec(v.shape, whole),
                pl.BlockSpec((1, rows), row),
                pl.BlockSpec((2, rows), row),
                pl.BlockSpec((2, rows), row),
            ],
            out_specs=[
                pl.BlockSpec((rows, width), part),
                pl.BlockSpec(k.shape, whole),
                pl.BlockSpec(k.shape, whole),
            ],
        ),
        out_shape=[
            jax.ShapeDtypeStruct(q.shape, F32),
            jax.ShapeDtypeStruct(k.shape, F32),
            jax.ShapeDtypeStruct(k.shape, F32),
        ],
        compiler_params=pltpu.CompilerParams(vmem_limit_bytes=VMEM_LIMIT),
        cost_estimate=pl.CostEstimate(flops=50 * 10**9, bytes_accessed=10**7, transcendentals=10**7),
        name="attn_bwd",
    )(info, q, g, k, v, start, log_total, row_dot)


def ffn_kernel(pieces, block, offs, s_ref, g_ref, st_ref, gt_ref, w_gate, w_up, w_down, mlp_ref, ds_ref, *grads):
    f = pl.program_id(0)

    @pl.when(f == 0)
    def _():
        mlp_ref[...] = jnp.zeros_like(mlp_ref)
        ds_ref[...] = jnp.zeros_like(ds_ref)

    s, g = s_ref[...], g_ref[...]
    gate = dot(s, w_gate[...])
    up = dot(s, w_up[...])
    d_act = dot(g, w_down[...])
    sig = 1.0 / (1.0 + jnp.exp(-gate))
    silu = gate * sig
    act = (silu * up).astype(BF16)
    d_gate = (d_act * up * sig * (1.0 + gate * (1.0 - sig))).astype(BF16)
    d_up = (d_act * silu).astype(BF16)
    mlp_ref[...] += dot(act, w_down[...], NT)
    ds_ref[...] += dot(d_gate, w_gate[...], NT) + dot(d_up, w_up[...], NT)
    half = pieces // 2
    for k, (left, right) in enumerate(((st_ref, d_gate), (st_ref, d_up), (gt_ref, act))):
        for j in range(pieces):
            at = pl.ds(pl.multiple_of(offs[j], block), block)
            grads[2 * k + j // half][j % half] = dot(left[at, :], right).astype(BF16)


def ffn_chunk(offs, s, g, st, gt, full_w, block):
    units = full_w.shape[1] // 3
    ft = min(256, units)
    n = offs.shape[0]
    tokens, width = s.shape
    steps = units // ft
    whole = lambda a: pl.BlockSpec(a.shape, lambda f, o: (0, 0))
    w_specs = [pl.BlockSpec((width, ft), lambda f, o, k=kind: (0, k * steps + f)) for kind in range(3)]
    grad_spec = pl.BlockSpec((n // 2, block, ft), lambda f, o: (0, 0, f))
    return pl.pallas_call(
        partial(ffn_kernel, n, block),
        grid_spec=pltpu.PrefetchScalarGridSpec(
            num_scalar_prefetch=1,
            grid=(steps,),
            in_specs=[whole(a) for a in (s, g, st, gt)] + w_specs,
            out_specs=[whole(s)] * 2 + [grad_spec] * 6,
        ),
        out_shape=[jax.ShapeDtypeStruct(s.shape, F32)] * 2
        + [jax.ShapeDtypeStruct((n // 2, block, units), BF16)] * 6,
        compiler_params=pltpu.CompilerParams(vmem_limit_bytes=VMEM_LIMIT),
        cost_estimate=pl.CostEstimate(
            flops=18 * tokens * width * units, bytes_accessed=10**7, transcendentals=tokens * units
        ),
        name="ffn",
    )(offs, s, g, st, gt, full_w, full_w, full_w)


class Net:
    def __init__(self, sems):
        me = lax.axis_index("dp")
        self.me, self.tensor = me, lax.axis_index("tensor")
        self.core = lax.rem(me, 2)
        self.x = lax.rem(lax.div(me, 2), 2)
        self.quad = lax.div(me, 4)
        self.quads = lax.axis_size("dp") // 4
        self.sems, self.used = sems, 0
        self.pending = []

    def sem(self):
        self.used += 1
        return self.sems.at[self.used - 1]

    def at(self, quad=None, x=None, core=None, tensor=None):
        quad = self.quad if quad is None else quad
        x = self.x if x is None else x
        core = self.core if core is None else core
        tensor = self.tensor if tensor is None else tensor
        return (quad * 4 + x * 2 + core, tensor)

    def other_core(self):
        return self.at(core=1 - self.core)

    def other_x(self):
        return self.at(x=1 - self.x)

    def other_tensor(self):
        return self.at(tensor=1 - self.tensor)

    def greet(self):
        targets = [self.other_core(), self.other_x(), self.other_tensor()]
        for s in range(1, self.quads):
            for c in range(2):
                targets.append(self.at(quad=lax.rem(self.quad + s, self.quads), core=c))
        barrier = pltpu.get_barrier_semaphore()
        for t in targets:
            pl.semaphore_signal(barrier, inc=1, device_id=t, device_id_type=MESH)
        pl.semaphore_wait(barrier, len(targets))

    def copy(self, src, dst, to, send=None, recv=None):
        return pltpu.make_async_remote_copy(
            src_ref=src,
            dst_ref=dst,
            send_sem=self.sem() if send is None else send,
            recv_sem=self.sem() if recv is None else recv,
            device_id=to,
            device_id_type=MESH,
        )

    def send(self, src, dst, to):
        c = self.copy(src, dst, to)
        c.start()
        self.pending.append(c.wait_send)
        return c

    def keep(self, src, dst):
        c = pltpu.make_async_copy(src, dst, self.sem())
        c.start()
        self.pending.append(c.wait)
        return c

    def finish(self):
        for wait in self.pending:
            wait()
        self.pending = []


def wait_bytes(ref, sem):
    pltpu.make_async_copy(ref, ref, sem).wait()


class Gather:
    def __init__(self, net, full, shard, kinds):
        self.net, self.full, self.shard, self.kinds = net, full, shard, kinds
        self.z_sem = [net.sem() for _ in range(net.quads)]
        self.x_sem = [net.sem() for _ in range(net.quads)]
        self.z_sent, self.x_sent, self.own = net.sem(), net.sem(), net.sem()

    def rows(self, s, x):
        n = self.net
        at = (lax.rem(n.quad + n.quads - s, n.quads) * 4 + 2 * x) * self.shard
        return self.full.at[pl.ds(pl.multiple_of(at, self.shard), 2 * self.shard)]

    def start(self):
        n = self.net
        mine = pl.ds(pl.multiple_of(n.me * self.shard, self.shard), self.shard)
        for arr, first, wide, into in self.kinds:
            half = arr.shape[1] // 2
            there = self.full.at[mine, pl.ds(into, wide)]

            def cut(core):
                return arr.at[:, pl.ds(pl.multiple_of(core * half + first, 128), wide)]

            pltpu.make_async_copy(cut(n.core), there, self.own).start()
            n.copy(cut(1 - n.core), there, n.other_core(), self.z_sent, self.z_sem[0]).start()
            for s in range(1, n.quads):
                to = lax.rem(n.quad + s, n.quads)
                for c in range(2):
                    n.copy(cut(c), there, n.at(quad=to, core=c), self.z_sent, self.z_sem[s]).start()

    def forward(self, s):
        n = self.net
        if s == 0:
            half = self.full.at[pl.ds(0, self.shard)]
            wait_bytes(half, self.own)
            wait_bytes(half, self.z_sem[0])
        else:
            wait_bytes(self.rows(s, n.x), self.z_sem[s])
        block = self.rows(s, n.x)
        n.copy(block, block, n.other_x(), self.x_sent, self.x_sem[s]).start()

    def forward_all(self):
        for s in range(self.net.quads):
            self.forward(s)

    def arrived(self):
        n = self.net
        for s in range(n.quads):
            wait_bytes(self.rows(s, 1 - n.x), self.x_sem[s])

    def finish(self):
        q = self.net.quads
        wait_bytes(self.full.at[pl.ds(0, (2 * q - 1) * self.shard)], self.z_sent)
        wait_bytes(self.full.at[pl.ds(0, 2 * q * self.shard)], self.x_sent)


def forward_kernel(
    tokens,
    out_grad,
    attn_gain,
    mlp_gain,
    q_gain,
    k_gain,
    cosine,
    sine,
    start,
    wq,
    wk,
    wv,
    wo,
    wg,
    wu,
    wd,
    first_out,
    grad_out,
    proj_out,
    plane_out,
    k_out,
    v_out,
    heads_out,
    stat_out,
    attn_out,
    middle_out,
    second_out,
    qkv_full,
    o_full,
    ff0,
    ff1,
    ff2,
    sems,
    first,
    w_qkv,
    proj,
    low,
    plane,
    kx,
    vx,
    acc,
    heads,
    stat,
    attn,
    w_o,
    core_send,
    core_recv,
    low_send,
    low_recv,
    middle,
    second,
):
    n = Net(sems)
    rows, width = tokens.shape
    d = q_gain.shape[1]
    shard = wq.shape[0]
    units = ff0.shape[1] // 3
    my_rows = pl.ds(pl.multiple_of(n.core * rows, rows), rows)
    chip_rows = pl.ds(pl.multiple_of(n.x * 2 * rows, 2 * rows), 2 * rows)
    back = kx.shape[0] - 1
    n.greet()

    qkv = Gather(n, qkv_full, shard, [(wq, 0, 4 * d, 0), (wk, 0, 2 * d, 4 * d), (wv, 0, 2 * d, 6 * d)])
    o_w = Gather(n, o_full, shard, [(wo, 0, 4 * d, 0)])
    ff = [
        Gather(
            n,
            full,
            shard,
            [(wg, i * units, units, 0), (wu, i * units, units, units), (wd, i * units, units, 2 * units)],
        )
        for i, full in enumerate((ff0, ff1, ff2))
    ]
    qkv.start()
    o_w.start()

    step = 128

    def norm_first(i, carry):
        at = pl.ds(pl.multiple_of(i * step, step), step)
        to = pl.ds(pl.multiple_of(n.core * rows + i * step, step), step)
        first[to, :] = rms_rows(tokens[at, :].astype(F32), attn_gain[...]).astype(BF16)
        return carry

    lax.fori_loop(0, rows // step, norm_first, 0)
    first_copy = n.send(first.at[my_rows], first.at[my_rows], n.other_core())
    grad_copy = n.send(out_grad, grad_out.at[my_rows], n.other_core())
    n.keep(out_grad, grad_out.at[my_rows])
    vx[:, :, d:] = jnp.ones(vx.shape[:2] + (d,), BF16)
    acc[...] = jnp.zeros_like(acc)

    qkv.forward_all()
    first_copy.wait_recv()
    o_w.forward_all()
    ff[0].start()
    qkv.arrived()
    load = pltpu.make_async_copy(qkv_full, w_qkv, n.sem())
    load.start()
    load.wait()

    tall = 256

    def project(i, carry):
        at = pl.ds(pl.multiple_of(i * tall, tall), tall)
        proj[at, :] = dot(first[at, :], w_qkv[...])
        cos, sin = cosine[at, :], sine[at, :]

        def prep(col, gain):
            u = proj[at, pl.ds(col, d)]
            u = rms_rows(u, gain[...])
            return (u * cos + pltpu.roll(u, d // 2, 1) * sin).astype(BF16)

        for h in range(2):
            for g in range(2):
                low[h, at, pl.ds(g * d, d)] = prep((2 * h + g) * d, q_gain)
            low[h, at, pl.ds(2 * d, d)] = prep((4 + h) * d, k_gain)
            low[h, at, pl.ds(3 * d, d)] = proj[at, pl.ds((6 + h) * d, d)].astype(BF16)
        return carry

    lax.fori_loop(0, 2 * rows // tall, project, 0)
    head_copy = n.send(low.at[1 - n.x], plane.at[chip_rows], n.other_x())
    n.keep(proj, proj_out)
    plane[chip_rows, :] = low[n.x]
    head_copy.wait_recv()
    kx[0] = plane[:, 2 * d : 3 * d]
    vx[0, :, :d] = plane[:, 3 * d :]
    n.keep(plane, plane_out)

    ahead = n.at(quad=jnp.minimum(n.quad + 1, n.quads - 1))
    hops = []
    for h in range(back):
        hops.append(
            [
                n.copy(kx.at[h], kx.at[h + 1], ahead),
                n.copy(vx.at[h, :, pl.ds(0, d)], vx.at[h + 1, :, pl.ds(0, d)], ahead),
            ]
        )

    def hop_start(h):
        @pl.when((n.quad >= h) & (n.quad < n.quads - 1))
        def _():
            for c in hops[h]:
                c.start()

    def hop_sent(h):
        @pl.when((n.quad >= h) & (n.quad < n.quads - 1))
        def _():
            for c in hops[h]:
                c.wait_send()

    def hop_arrived(h):
        @pl.when(n.quad >= h + 1)
        def _():
            for c in hops[h]:
                c.wait_recv()

    factor = LOG2E / math.sqrt(d)

    def attend(h, i, j):
        q_at = pl.ds(pl.multiple_of(i * rows, rows), rows)
        k_at = pl.ds(pl.multiple_of(j * rows, rows), rows)
        q2 = jnp.concatenate([plane[q_at, pl.ds(0, d)], plane[q_at, pl.ds(d, d)]], axis=0)
        prob = jnp.exp2(dot(q2, kx[h, k_at, :], NT) * factor)
        k_pos = (4 * (n.quad - h) + j) * rows + lax.broadcasted_iota(jnp.int32, (rows, rows), 1)
        keep = k_pos >= start[q_at, :]
        if h == 0:
            q_pos = (4 * n.quad + i) * rows + lax.broadcasted_iota(jnp.int32, (rows, rows), 0)
            keep = keep & (k_pos <= q_pos)
        prob = jnp.where(jnp.concatenate([keep, keep], axis=0), prob, 0.0)
        acc[i] += dot(prob.astype(BF16), vx[h, k_at, :])

    def sweep(h, i, lo, hi):
        def body(j, carry):
            attend(h, i, j)
            return carry

        lax.fori_loop(lo, hi, body, 0)

    def over_q(fn):
        def body(i, carry):
            fn(i)
            return carry

        lax.fori_loop(0, 4, body, 0)

    hop_start(0)
    over_q(lambda i: sweep(0, i, 0, i + 1))
    hop_arrived(0)
    hop_start(1)

    @pl.when(n.quad >= 1)
    def _():
        over_q(lambda i: sweep(1, i, 0, 4))

    ff[0].forward_all()
    ff[1].start()
    hop_arrived(1)

    @pl.when(n.quad >= 2)
    def _():
        over_q(lambda i: sweep(2, i, i, 4))

    for i in range(4):
        at = pl.ds(i * rows, rows)
        total = acc[i, :, d:]
        done = acc[i, :, :d] / total
        heads[at, pl.ds(0, d)] = done[:rows]
        heads[at, pl.ds(d, d)] = done[rows:]
        logs = jnp.log2(total)
        stat[0:1, pl.ds(i * rows, rows)] = logs[:rows].T[0:1]
        stat[1:2, pl.ds(i * rows, rows)] = logs[rows:].T[0:1]
    theirs = pl.ds(pl.multiple_of((1 - n.x) * 2 * rows, 2 * rows), 2 * rows)
    plane_attn = low.at[0, :, pl.ds(0, 2 * d)]
    head_copy.wait_send()
    n.pending.remove(head_copy.wait_send)
    low[0, :, : 2 * d] = heads[theirs, :].astype(BF16)
    attn_copy = n.send(plane_attn, attn.at[n.x], n.other_x())
    attn[n.x] = heads[chip_rows, :].astype(BF16)
    n.keep(heads, heads_out)
    n.keep(stat, stat_out)
    for h in range(back + 1):
        n.keep(kx.at[h], k_out.at[pl.ds(h * 4 * rows, 4 * rows)])
        n.keep(vx.at[h, :, pl.ds(0, d)], v_out.at[pl.ds(h * 4 * rows, 4 * rows)])
    o_w.arrived()
    load_o = pltpu.make_async_copy(o_full, w_o, n.sem())
    load_o.start()
    load_o.wait()
    attn_copy.wait_recv()
    n.keep(attn, attn_out)

    def o_rows(at):
        return dot(attn[0, at, :], w_o[:, : 2 * d], NT) + dot(attn[1, at, :], w_o[:, 2 * d :], NT)

    parts = rows // step
    core_copies, low_copies, second_copies = [], [], []
    for i in range(parts):
        at = pl.ds(i * step, step)
        core_send[at, :] = o_rows(
            pl.ds(pl.multiple_of((1 - n.core) * rows + i * step, step), step)
        ).astype(BF16)
        core_copies.append(n.send(core_send.at[at], core_recv.at[at], n.other_core()))
    for i in range(parts):
        at = pl.ds(i * step, step)
        part = o_rows(pl.ds(pl.multiple_of(n.core * rows + i * step, step), step))
        core_copies[i].wait_recv()
        low_send[at, :] = (part + core_recv[at, :].astype(F32)).astype(BF16)
        low_copies.append(n.send(low_send.at[at], low_recv.at[at], n.other_tensor()))
    ff[1].forward_all()
    ff[2].start()
    for i in range(parts):
        at = pl.ds(i * step, step)
        low_copies[i].wait_recv()
        mid = tokens[at, :].astype(F32) + (low_send[at, :].astype(F32) + low_recv[at, :].astype(F32))
        middle[at, :] = mid
        to = pl.ds(pl.multiple_of(n.core * rows + i * step, step), step)
        second[to, :] = rms_rows(mid, mlp_gain[...]).astype(BF16)
        second_copies.append(n.send(second.at[to], second.at[to], n.other_core()))
    n.keep(middle, middle_out)
    n.keep(first, first_out)
    for c in second_copies:
        c.wait_recv()
    n.keep(second, second_out)
    grad_copy.wait_recv()
    ff[2].forward_all()
    for g in ff:
        g.arrived()
    for h in range(back):
        hop_sent(h)
    n.finish()
    for g in [qkv, o_w] + ff:
        g.finish()


def forward(tokens, out_grad, attn_gain, mlp_gain, q_gain, k_gain, cosine, sine, start, *weights):
    rows, width = tokens.shape
    d = q_gain.shape[0]
    wq, wg = weights[0], weights[4]
    quads = lax.axis_size("dp") // 4
    back = REACH // 4
    units = wg.shape[1] // 2 // 3
    vmem = pl.BlockSpec(memory_space=pltpu.VMEM)
    hbm = pl.BlockSpec(memory_space=pl.ANY)
    shape = jax.ShapeDtypeStruct
    return pl.pallas_call(
        forward_kernel,
        in_specs=[vmem, hbm] + [vmem] * 7 + [hbm] * 7,
        out_specs=[hbm] * 16,
        out_shape=[
            shape((2 * rows, width), BF16),
            shape((2 * rows, width), BF16),
            shape((2 * rows, 8 * d), F32),
            shape((4 * rows, 4 * d), BF16),
            shape((4 * rows * (back + 1), d), BF16),
            shape((4 * rows * (back + 1), d), BF16),
            shape((4 * rows, 2 * d), F32),
            shape((2, 4 * rows), F32),
            shape((2, 2 * rows, 2 * d), BF16),
            shape((rows, width), F32),
            shape((2 * rows, width), BF16),
            shape((width, 8 * d), BF16),
            shape((width, 4 * d), BF16),
        ]
        + [shape((width, 3 * units), BF16)] * 3,
        scratch_shapes=[
            pltpu.SemaphoreType.DMA((80 + 5 * (2 * quads + 3),)),
            pltpu.VMEM((2 * rows, width), BF16),
            pltpu.VMEM((width, 8 * d), BF16),
            pltpu.VMEM((2 * rows, 8 * d), F32),
            pltpu.VMEM((2, 2 * rows, 4 * d), BF16),
            pltpu.VMEM((4 * rows, 4 * d), BF16),
            pltpu.VMEM((back + 1, 4 * rows, d), BF16),
            pltpu.VMEM((back + 1, 4 * rows, 2 * d), BF16),
            pltpu.VMEM((4, 2 * rows, 2 * d), F32),
            pltpu.VMEM((4 * rows, 2 * d), F32),
            pltpu.VMEM((2, 4 * rows), F32),
            pltpu.VMEM((2, 2 * rows, 2 * d), BF16),
            pltpu.VMEM((width, 4 * d), BF16),
            pltpu.VMEM((rows, width), BF16),
            pltpu.VMEM((rows, width), BF16),
            pltpu.VMEM((rows, width), BF16),
            pltpu.VMEM((rows, width), BF16),
            pltpu.VMEM((rows, width), F32),
            pltpu.VMEM((2 * rows, width), BF16),
        ],
        compiler_params=pltpu.CompilerParams(
            collective_id=0, has_side_effects=True, vmem_limit_bytes=VMEM_LIMIT
        ),
        name="forward",
    )(
        tokens,
        out_grad,
        attn_gain[None],
        mlp_gain[None],
        q_gain[None],
        k_gain[None],
        cosine,
        sine,
        start,
        *weights,
    )


def local(
    tokens,
    out_grad,
    lengths,
    attn_gain,
    q_weight,
    key_matrix,
    value_matrix,
    o_weight,
    q_gain,
    k_gain,
    mlp_gain,
    gate_weight,
    up_weight,
    down_weight,
):
    rows, width = tokens.shape
    d = q_gain.shape[0]
    devices = lax.axis_size("dp")
    quads = devices // 4
    me = lax.axis_index("dp")
    quad, x, core = me // 4, (me // 2) % 2, me % 2
    shard = q_weight.shape[0]
    block = 2 * shard
    kv_here = key_matrix.shape[1] // d
    group = q_weight.shape[1] // key_matrix.shape[1]
    assert kv_here == 4 and group == 2

    def pick(arr, index, count, axis):
        size = arr.shape[axis] // count
        return lax.dynamic_slice_in_dim(arr, index * size, size, axis)

    def ordered(mine, other, flag, axis):
        return jnp.where(
            flag == 0,
            jnp.concatenate([mine, other], axis),
            jnp.concatenate([other, mine], axis),
        )

    offs = jnp.stack(
        [
            ((quad - s) % quads) * 2 * block + jnp.where(xr == 0, x, 1 - x) * block
            for xr in range(2)
            for s in range(quads)
        ]
    ).astype(jnp.int32)

    def both(mine_rows):
        return ordered(mine_rows, swap_core(mine_rows), core, 0)

    chip_index = (me // 2) * 2 * rows + jnp.arange(2 * rows, dtype=jnp.int32)
    cosine, sine_vals = angles(chip_index - starts_of(chip_index, lengths), d)
    sine_signed = jnp.concatenate([-sine_vals[:, : d // 2], sine_vals[:, d // 2 :]], 1)
    q_index = quad * 4 * rows + jnp.arange(4 * rows, dtype=jnp.int32)
    q_start = starts_of(q_index, lengths)
    tokens_wide = tokens.astype(F32)
    (
        first_chip,
        grad_chip,
        proj,
        plane,
        k_all,
        v_all,
        heads_out,
        log_total,
        attn_halves,
        middle,
        second_chip,
        qkv_full,
        o_full,
        *ff_full,
    ) = forward(
        tokens,
        out_grad,
        attn_gain,
        mlp_gain,
        q_gain,
        k_gain,
        cosine,
        sine_signed,
        q_start[:, None],
        q_weight,
        key_matrix,
        value_matrix,
        o_weight,
        gate_weight,
        up_weight,
        down_weight,
    )
    q_plane = plane[:, : group * d]
    attn_low = jnp.concatenate([attn_halves[0], attn_halves[1]], 1)
    back_hops = REACH // 4
    q_blocks = 4 * quad + jnp.arange(4)
    k_blocks = jnp.concatenate([q_blocks - 4 * h for h in range(back_hops + 1)])
    by_block = q_start.reshape(-1, rows)
    lanes = k_blocks.shape[0]
    info = jnp.stack(
        [
            jnp.pad(v, (0, lanes - v.shape[0]))
            for v in (q_blocks, k_blocks, by_block[:, 0], by_block[:, -1])
        ]
    ).astype(jnp.int32)

    def prep_q(p, gain):
        return head_prep(p.reshape(2 * rows, 2 * group, d), gain, cosine, sine_vals)

    def prep_k(p, gain):
        return head_prep(p.reshape(2 * rows, 2, d), gain, cosine, sine_vals)

    q_in, k_in = proj[:, : 4 * d], proj[:, 4 * d : 6 * d]

    def core_sum(part):
        low_part = pick(part, 1 - core, 2, 0).astype(BF16)
        return pick(part, core, 2, 0) + swap_core(low_part).astype(F32)

    second_t, grad_t = second_chip.T, grad_chip.T

    def scatter(keep, send):
        got = swap_x(send)
        sums = [
            (keep[s].astype(F32) + got[s].astype(F32)).astype(BF16) for s in range(quads)
        ]
        total = sums[0].astype(F32)
        for s in range(1, quads):
            total = total + over_quads(sums[s], -s).astype(F32)
        return total

    def to_cores(total):
        own = pick(total, core, 2, 0)
        return ordered(own, swap_core(pick(total, 1 - core, 2, 0)), core, 1)

    ff_grads = [[], [], []]
    mlp_part, d_second_part = 0.0, 0.0
    for full_w in ff_full:
        got = ffn_chunk(offs, second_chip, grad_chip, second_t, grad_t, full_w, block)
        mlp_part, d_second_part = mlp_part + got[0], d_second_part + got[1]
        for n in range(3):
            ff_grads[n].append(scatter(got[2 + 2 * n], got[3 + 2 * n]))
    grad_gate, grad_up, grad_down = (to_cores(jnp.concatenate(g, 1)) for g in ff_grads)

    d_second = tensor_sum(core_sum(d_second_part))
    mlp_out = tensor_sum(core_sum(mlp_part))
    output = (middle + mlp_out).astype(BF16)
    unused_mid, norm_back_mid = jax.vjp(rms_rows, middle, mlp_gain)
    d_middle_norm, grad_mlp_local = norm_back_mid(d_second)
    d_middle = out_grad.astype(F32) + d_middle_norm
    d_attn = both(d_middle.astype(BF16))

    def split_rows(grad):
        by = grad.reshape(quads, 2, block, -1)
        order = (quad - jnp.arange(quads)) % quads
        keep = lax.dynamic_index_in_dim(by, x, 1, False)
        send = lax.dynamic_index_in_dim(by, 1 - x, 1, False)

        def rel(a):
            return [lax.dynamic_index_in_dim(a, order[s], 0, False) for s in range(quads)]

        return jnp.stack(rel(keep)), jnp.stack(rel(send))

    grad_o = to_cores(scatter(*split_rows(dot(d_attn, attn_low, TN).astype(BF16))))
    d_heads = dot(d_attn, o_full).astype(BF16)
    d_heads_plane = ordered(pick(d_heads, x, 2, 1), swap_x(pick(d_heads, 1 - x, 2, 1)), x, 0)
    row_dot = jnp.sum(
        (d_heads_plane.astype(F32) * heads_out).reshape(4 * rows, group, d), axis=-1
    ).T
    d_q, d_k, d_v = attn_bwd(
        info, q_plane, d_heads_plane, k_all, v_all, q_start[None, :], log_total, row_dot, rows
    )
    scale = 1.0 / math.sqrt(d)
    d_kv = jnp.concatenate([d_k * scale, d_v], 1).reshape(back_hops + 1, 4 * rows, 2 * d)
    carried = d_kv[back_hops]
    for h in reversed(range(back_hops)):
        carried = d_kv[h] + shift_quads(carried.astype(BF16), -1).astype(F32)
    d_plane = jnp.concatenate([d_q * scale, carried], 1)
    d_mine = pick(d_plane, x, 2, 0)
    d_back = swap_x(pick(d_plane, 1 - x, 2, 0).astype(BF16)).astype(F32)
    d_low = jnp.where(x == 0, jnp.stack([d_mine, d_back], 1), jnp.stack([d_back, d_mine], 1))
    unused_q, q_back = jax.vjp(prep_q, q_in, q_gain)
    d_q_proj, q_gain_local = q_back(d_low[:, :, : group * d].reshape(2 * rows, 2 * group, d))
    unused_k, k_back = jax.vjp(prep_k, k_in, k_gain)
    d_k_proj, k_gain_local = k_back(d_low[:, :, group * d : (group + 1) * d])
    d_proj = jnp.concatenate(
        [d_q_proj, d_k_proj, d_low[:, :, (group + 1) * d :].reshape(2 * rows, -1)], 1
    ).astype(BF16)
    grad_qkv = scatter(*split_rows(dot(first_chip, d_proj, TN).astype(BF16)))
    grad_q = to_cores(grad_qkv[:, : 4 * d])
    grad_k = to_cores(grad_qkv[:, 4 * d : 6 * d])
    grad_v = to_cores(grad_qkv[:, 6 * d :])
    d_first = tensor_sum(core_sum(dot(d_proj, qkv_full, NT)))
    unused_in, norm_back_in = jax.vjp(rms_rows, tokens_wide, attn_gain)
    d_tokens_norm, grad_attn_local = norm_back_in(d_first)
    input_grad = d_middle + d_tokens_norm
    grad_attn_gain, grad_mlp_gain, grad_q_gain, grad_k_gain = lax.psum(
        (0.5 * grad_attn_local, 0.5 * grad_mlp_local, q_gain_local, k_gain_local),
        ("dp", "tensor"),
    )
    return (
        output,
        input_grad,
        grad_attn_gain,
        grad_q,
        grad_k,
        grad_v,
        grad_o,
        grad_q_gain,
        grad_k_gain,
        grad_mlp_gain,
        grad_gate,
        grad_up,
        grad_down,
    )


def solution(mesh):
    rows, weight = P("dp", None), P("dp", "tensor")
    placed = (
        (rows, rows) + (P(),) * 2 + (weight,) * 4 + (P(),) * 3 + (weight,) * 3
    )
    return jax.shard_map(
        local,
        mesh=mesh,
        in_specs=placed,
        out_specs=(rows, rows, P()) + (weight,) * 4 + (P(),) * 3 + (weight,) * 3,
        check_vma=False,
    )
```

time: 2550 us -> 1260 us (0.49)
  waiting for transfers between devices: 1700 us -> 254 us
  Pallas kernels: 0 us -> 501 us
  matrix products: 359 us -> 18.2 us
  starting transfers between devices: 136 us -> 244 us
  local copies, waits for them, and re-layouts: 120 us -> 73.6 us
  blocking collectives: 66.9 us -> 39.4 us
    reduce_scatter x7 -> x0, waiting for transfers between devices: 1040 us -> none  [the longest x1 249 us: local(): lax.psum_scatter(grad_up, 'dp', scatter_dimension=0, tiled=True)]
    pallas_call x0 -> x5, Pallas kernels: none -> 501 us  [the longest x1 368 us: forward(): pl.pallas_call(forward_kernel, in_specs=[vmem, hbm] + [vmem] * 7 + [hbm]...]
    all_gather x7 -> x0, waiting for transfers between devices: 352 us -> none  [the longest x1 98.3 us: local(): lax.all_gather(up_weight, 'dp', axis=0, tiled=True)]
    dot_general x84 -> x4, matrix products: 359 us -> 18.2 us  [dot(): return lax.dot_general(a, b, dims, preferred_element_type=F32)]
    psum x3 -> x0, waiting for transfers between devices: 189 us -> none  [the longest x1 90 us: local(): lax.psum(attn_part.astype(jnp.bfloat16), 'tensor').astype(jnp.float32)]
    ppermute x16 -> x62, waiting for transfers between devices: 113 us -> 254 us  [the longest x33 128 us: over_quads(): return lax.ppermute(value, 'dp', [(i, (i + 4 * by) % n) for i in range(n)])]
    ppermute x16 -> x62, starting transfers between devices: 135 us -> 244 us  [the longest x33 221 us: over_quads(): return lax.ppermute(value, 'dp', [(i, (i + 4 * by) % n) for i in range(n)])]
    psum x2 -> x1, blocking collectives: 66.9 us -> 39.4 us  [local(): lax.psum((0.5 * grad_attn_local, 0.5 * grad_mlp_local, q_gain_local, k_ga...]
  transfers between devices with their start and end apart: 33 -> 62, of which waited for: 31 -> 23; matrix products, arithmetic and copies ran while one was open for 12% -> 13% of each run, Pallas kernels for 0% -> 8%
where the time goes in v1:
time: 1260 us; the launch traced here: 1250 us
  Pallas kernels  501 us (40%)
  waiting for transfers between devices  254 us (20%)
  starting transfers between devices  244 us (19%)
  other arithmetic  114 us (9%)
  local copies, waits for them, and re-layouts  73.6 us (6%)
  blocking collectives  39.4 us (3%)
  matrix products  18.2 us (1%)
    pallas_call x1, Pallas kernels, forward(): pl.pallas_call(forward_kernel, in_specs=[vmem, hbm] + [vmem] * 7 + [hbm]...  368 us
    ppermute x33, starting transfers between devices, over_quads(): return lax.ppermute(value, 'dp', [(i, (i + 4 * by) % n) for i in range(n)])  221 us
    ppermute x33, waiting for transfers between devices, over_quads(): return lax.ppermute(value, 'dp', [(i, (i + 4 * by) % n) for i in range(n)])  128 us
    pallas_call x3, Pallas kernels, ffn_chunk(): pl.pallas_call(partial(ffn_kernel, n, block), grid_spec=pltpu.PrefetchSca...  107 us
    ppermute x13, waiting for transfers between devices, swap_x(): lax.ppermute(value, 'dp', [(i, i ^ 2) for i in range(lax.axis_size('dp'))])  107 us
    psum x1, blocking collectives, local(): lax.psum((0.5 * grad_attn_local, 0.5 * grad_mlp_local, q_gain_local, k_ga...  39.4 us
    pallas_call x1, Pallas kernels, attn_bwd(): pl.pallas_call(partial(attn_bwd_kernel, rows, blocks), grid_spec=pltpu.Pr...  25.6 us
  transfers between devices with their start and end apart: 62, of which 23 were waited for; matrix products, arithmetic and copies ran while one was open for 13% of the time, Pallas kernels for 8%

profile of v1, /device:TPU:0, one launch (start us, length us, event | category | flops | bytes accessed | tf_op | source)
XLA Modules:
  0.0 1253.4 jit_solution(16436477280667651146)
XLA Ops:
  8.0 368.1 %forward.1 = (bf16[1024,2048]{1,0:T(8,128)(2,1)}, bf16[1024,2048]{1,0:T(8,128)(2,1)}, f32[1024,1024]{1,0:T(8,128)}, bf16[2048,512]{1,0:T(8,128)(2,1)}, bf16[6144...) custom-call(bf16[512,2048]{1,0:T(8,128)(2,1)} %tokens.1, ...), custom_call_target="tpu_custom_call" | custom-call | tf_op jit(solution)/shard_map/forward/pallas_call | solution.py:637
  376.1 6.9 copy.118
  383.0 6.4 copy.119
  390.0 35.6 %ffn.5 = (f32[1024,2048]{1,0:T(8,128)}, f32[1024,2048]{1,0:T(8,128)}, bf16[4,256,512]{2,1,0:T(8,128)(2,1)}, bf16[4,256,512]{2,1,0:T(8,128)(2,1)}, bf16[4,256,512...) custom-call(s32[8]{0:T(128)} %stack.81.offs, ...), custom_call_target="tpu_custom_call" | custom-call | flops 19327352832 | bytes 10000000 | tf_op jit(solution)/shard_map/ffn/pallas_call | solution.py:207
  428.0 35.7 %ffn.4 = (f32[1024,2048]{1,0:T(8,128)}, f32[1024,2048]{1,0:T(8,128)}, bf16[4,256,512]{2,1,0:T(8,128)(2,1)}, bf16[4,256,512]{2,1,0:T(8,128)(2,1)}, bf16[4,256,512...) custom-call(s32[8]{0:T(128)} %stack.81.offs, ...), custom_call_target="tpu_custom_call" | custom-call | flops 19327352832 | bytes 10000000 | tf_op jit(solution)/shard_map/ffn/pallas_call | solution.py:207
  465.5 35.8 %ffn.3 = (f32[1024,2048]{1,0:T(8,128)}, f32[1024,2048]{1,0:T(8,128)}, bf16[4,256,512]{2,1,0:T(8,128)(2,1)}, bf16[4,256,512]{2,1,0:T(8,128)(2,1)}, bf16[4,256,512...) custom-call(s32[8]{0:T(128)} %stack.81.offs, ...), custom_call_target="tpu_custom_call" | custom-call | flops 19327352832 | bytes 10000000 | tf_op jit(solution)/shard_map/ffn/pallas_call | solution.py:207
  501.2 10.0 add_add_fusion
  511.3 3.4 copy-done.7
  533.1 9.6 add_add_fusion.1
  542.7 3.4 copy-done.6
  566.1 3.7 add_convert_fusion.1
  581.6 10.4 collective-permute-done.40
  595.6 18.9 %collective-permute-done.53 = bf16[4,256,512]{2,1,0:T(8,128)(2,1)S(1)} collective-permute-done((bf16[4,256,512]{2,1,0:T(8,128)(2,1)S(1)}, bf16[4,256,512]{2,1,0:T(8,128)(2,1)S(1)}, u32[]{:S(2)}, u32[]{:S(2)}) %collective-permute-start.53) | collective-permute-done | bytes 1048608 | tf_op jit(solution)/shard_map/ppermute | solution.py:42
  615.5 21.5 %collective-permute-done.23 = bf16[4,256,512]{2,1,0:T(8,128)(2,1)S(1)} collective-permute-done((bf16[4,256,512]{2,1,0:T(8,128)(2,1)S(1)}, bf16[4,256,512]{2,1,0:T(8,128)(2,1)S(1)}, u32[]{:S(2)}, u32[]{:S(2)}) %collective-permute-start.23) | collective-permute-done | bytes 1048608 | tf_op jit(solution)/shard_map/ppermute | solution.py:42
  637.0 41.1 %collective-permute-start.32 = (bf16[256,512]{1,0:T(8,128)(2,1)}, bf16[256,512]{1,0:T(8,128)(2,1)}, u32[]{:S(2)}, u32[]{:S(2)}) collective-permute-start(bf16[256,512]{1,0:T(8,128)(2,1)} %get-tuple-element.153), channel_id=1, source_target_pairs={{0,24},{2,26},{4,28},{6,30},{8,0},{10,2},{12,4},{14,6},{16,8},{18,... | collective-permute-start | bytes 786440 | tf_op jit(solution)/shard_map/ppermute | solution.py:31
  679.1 8.2 collective-permute-start.34
  687.5 44.0 %collective-permute-start.33 = (bf16[256,512]{1,0:T(8,128)(2,1)S(1)}, bf16[256,512]{1,0:T(8,128)(2,1)}, u32[]{:S(2)}, u32[]{:S(2)}) collective-permute-start(bf16[256,512]{1,0:T(8,128)(2,1)S(1)} %get-tuple-element.155), channel_id=1, source_target_pairs={{0,16},{2,18},{4,20},{6,22},{8,24},{10,26},{12,28},{14,30},{16,0},... | collective-permute-start | bytes 786440 | tf_op jit(solution)/shard_map/ppermute | solution.py:31
  740.2 8.0 collective-permute-done.45
  749.5 6.7 collective-permute-start.30
  756.2 10.6 collective-permute-done.46
  772.0 10.8 collective-permute-start.43
  782.8 6.5 collective-permute-done.29
  792.4 12.8 %collective-permute-start.26 = (bf16[256,512]{1,0:T(8,128)(2,1)S(1)}, bf16[256,512]{1,0:T(8,128)(2,1)S(1)}, u32[]{:S(2)}, u32[]{:S(2)}) collective-permute-start(bf16[256,512]{1,0:T(8,128)(2,1)S(1)} %copy-done.48), channel_id=1, source_target_pairs={{0,8},{2,10},{4,12},{6,14},{8,16},{10,18},{12,20},{14,22},{16,24},... | collective-permute-start | bytes 786440 | tf_op jit(solution)/shard_map/ppermute | solution.py:31
  805.2 6.6 collective-permute-done.42
  813.9 13.8 %collective-permute-start.39 = (bf16[256,512]{1,0:T(8,128)(2,1)S(1)}, bf16[256,512]{1,0:T(8,128)(2,1)S(1)}, u32[]{:S(2)}, u32[]{:S(2)}) collective-permute-start(bf16[256,512]{1,0:T(8,128)(2,1)S(1)} %get-tuple-element.139), channel_id=1, source_target_pairs={{0,8},{2,10},{4,12},{6,14},{8,16},{10,18},{12,20},{14,22},{16,24},... | collective-permute-start | bytes 786440 | tf_op jit(solution)/shard_map/ppermute | solution.py:31
  827.7 6.6 collective-permute-done.25
  836.4 13.8 %collective-permute-start.60 = (bf16[256,512]{1,0:T(8,128)(2,1)}, bf16[256,512]{1,0:T(8,128)(2,1)}, u32[]{:S(2)}, u32[]{:S(2)}) collective-permute-start(bf16[256,512]{1,0:T(8,128)(2,1)} %get-tuple-element.136), channel_id=1, source_target_pairs={{0,8},{2,10},{4,12},{6,14},{8,16},{10,18},{12,20},{14,22},{16,24},... | collective-permute-start | bytes 786440 | tf_op jit(solution)/shard_map/ppermute | solution.py:31
  850.2 6.6 collective-permute-done.38
  864.1 6.5 collective-permute-done.5
  870.6 6.7 collective-permute-start.54
  882.6 5.6 reduce_sum.139
  890.3 25.6 %attn_bwd.1 = (f32[2048,256]{1,0:T(8,128)}, f32[6144,128]{1,0:T(8,128)}, f32[6144,128]{1,0:T(8,128)}) custom-call(s32[4,12]{1,0:T(4,128)} %pad_add_fusion.info, bf16[2048,256]{1,0:T(8,128)(2,1)} %slice.327.q_ref, bf16[2048,256]{1,0:T(8,128)(2,1)} %get-tuple-element.116.g_ref, bf16[6144,128]{1,0:T(8,128)(2,1)} %get-tuple-element.70.k_ref, ...), custom_call_target="tpu_custom_call" | custom-call | flops 49999998976 | bytes 10000000 | tf_op jit(solution)/shard_map/attn_bwd/pallas_call | solution.py:141
  919.7 6.3 collective-permute-start.56
  926.0 28.0 %collective-permute-start.55 = (bf16[256,512]{1,0:T(8,128)(2,1)S(1)}, bf16[256,512]{1,0:T(8,128)(2,1)S(1)}, u32[]{:S(2)}, u32[]{:S(2)}) collective-permute-start(bf16[256,512]{1,0:T(8,128)(2,1)S(1)} %copy-done.43), channel_id=1, source_target_pairs={{0,16},{2,18},{4,20},{6,22},{8,24},{10,26},{12,28},{14,30},{16,0},... | collective-permute-start | bytes 786440 | tf_op jit(solution)/shard_map/ppermute | solution.py:31
  959.7 11.3 collective-permute-start.52
  974.3 15.1 %collective-permute-done.50 = bf16[256,512]{1,0:T(8,128)(2,1)S(1)} collective-permute-done((bf16[256,512]{1,0:T(8,128)(2,1)S(1)}, bf16[256,512]{1,0:T(8,128)(2,1)S(1)}, u32[]{:S(2)}, u32[]{:S(2)}) %collective-permute-start.50) | collective-permute-done | bytes 262176 | tf_op jit(solution)/shard_map/ppermute | solution.py:31
  989.4 8.5 collective-permute-done.52
  997.9 11.6 collective-permute-done.51
  1016.4 19.5 %collective-permute-done.7 = bf16[2048,256]{1,0:T(8,128)(2,1)S(1)} collective-permute-done((bf16[2048,256]{1,0:T(8,128)(2,1)S(1)}, bf16[2048,256]{1,0:T(8,128)(2,1)S(1)}, u32[]{:S(2)}, u32[]{:S(2)}) %collective-permute-start.7) | collective-permute-done | bytes 1048608 | tf_op jit(solution)/shard_map/ppermute | solution.py:36
  1044.6 17.8 %collective-permute-done.8 = bf16[1024,512]{1,0:T(8,128)(2,1)S(1)} collective-permute-done((bf16[1024,512]{1,0:T(8,128)(2,1)S(1)}, bf16[1024,512]{1,0:T(8,128)(2,1)S(1)}, u32[]{:S(2)}, u32[]{:S(2)}) %collective-permute-start.8) | collective-permute-done | bytes 1048608 | tf_op jit(solution)/shard_map/ppermute | solution.py:42
  1087.4 4.6 fusion.27
  1092.4 8.7 convolution_convert_fusion
  1108.3 3.8 add_convert_fusion.3
  1118.1 31.5 %collective-permute-done.11 = bf16[4,256,1024]{2,1,0:T(8,128)(2,1)S(1)} collective-permute-done((bf16[4,256,1024]{2,1,0:T(8,128)(2,1)S(1)}, bf16[4,256,1024]{2,1,0:T(8,128)(2,1)S(1)}, u32[]{:S(2)}, u32[]{:S(2)}) %collective-permute-start.11) | collective-permute-done | bytes 2097184 | tf_op jit(solution)/shard_map/ppermute | solution.py:42
  1155.3 20.2 %collective-permute-done.12 = bf16[256,1024]{1,0:T(8,128)(2,1)S(1)} collective-permute-done((bf16[256,1024]{1,0:T(8,128)(2,1)S(1)}, bf16[256,1024]{1,0:T(8,128)(2,1)S(1)}, u32[]{:S(2)}, u32[]{:S(2)}) %collective-permute-start.12) | collective-permute-done | bytes 524320 | tf_op jit(solution)/shard_map/ppermute | solution.py:31
  1175.5 21.5 %collective-permute-done.13 = bf16[256,1024]{1,0:T(8,128)(2,1)S(1)} collective-permute-done((bf16[256,1024]{1,0:T(8,128)(2,1)S(1)}, bf16[256,1024]{1,0:T(8,128)(2,1)S(1)}, u32[]{:S(2)}, u32[]{:S(2)}) %collective-permute-start.13) | collective-permute-done | bytes 524320 | tf_op jit(solution)/shard_map/ppermute | solution.py:31
  1203.2 39.4 %all-reduce.7 = (f32[2048]{0:T(1024)}, f32[128]{0:T(128)}, f32[128]{0:T(128)}, f32[2048]{0:T(1024)}) all-reduce(f32[2048]{0:T(1024)S(1)} %broadcast_multiply_fusion.5, f32[128]{0:T(128)S(1)} %get-tuple-element.103, f32[128]{0:T(128)S(1)} %get-tuple-element.105, ...), channel_id=1, replica_groups=mesh['dp'=16,'tensor'=2] {'dp','tensor'}, use_global_device_ids=true, to_apply=%region_13.14 | all-reduce | flops 4352 | bytes 34816 | tf_op jit(solution)/shard_map/psum | solution.py:888
  1242.7 10.5 fusion.1
  (373 shorter events, 175.4 us)
Async XLA Ops:
  425.6 144.3 %collective-permute-start.31 = (bf16[4,256,512]{2,1,0:T(8,128)(2,1)}, bf16[4,256,512]{2,1,0:T(8,128)(2,1)}, u32[]{:S(2)}, u32[]{:S(2)}) collective-permute-start(bf16[4,256,512]{2,1,0:T(8,128)(2,1)} %get-tuple-element.86), channel_id=1, source_target_pairs={{0,4},{2,6},{4,0},{6,2},{8,12},{10,14},{12,8},{14,10},{16,20},{18,... | collective-permute-start | bytes 3145736 | tf_op jit(solution)/shard_map/ppermute | solution.py:42
  426.0 145.5 %collective-permute-start.44 = (bf16[4,256,512]{2,1,0:T(8,128)(2,1)}, bf16[4,256,512]{2,1,0:T(8,128)(2,1)}, u32[]{:S(2)}, u32[]{:S(2)}) collective-permute-start(bf16[4,256,512]{2,1,0:T(8,128)(2,1)} %get-tuple-element.92), channel_id=1, source_target_pairs={{0,4},{2,6},{4,0},{6,2},{8,12},{10,14},{12,8},{14,10},{16,20},{18,... | collective-permute-start | bytes 3145736 | tf_op jit(solution)/shard_map/ppermute | solution.py:42
  427.7 147.5 %collective-permute-start.57 = (bf16[4,256,512]{2,1,0:T(8,128)(2,1)}, bf16[4,256,512]{2,1,0:T(8,128)(2,1)}, u32[]{:S(2)}, u32[]{:S(2)}) collective-permute-start(bf16[4,256,512]{2,1,0:T(8,128)(2,1)} %get-tuple-element.98), channel_id=1, source_target_pairs={{0,4},{2,6},{4,0},{6,2},{8,12},{10,14},{12,8},{14,10},{16,20},{18,... | collective-permute-start | bytes 3145736 | tf_op jit(solution)/shard_map/ppermute | solution.py:42
  463.7 114.2 %collective-permute-start.27 = (bf16[4,256,512]{2,1,0:T(8,128)(2,1)}, bf16[4,256,512]{2,1,0:T(8,128)(2,1)}, u32[]{:S(2)}, u32[]{:S(2)}) collective-permute-start(bf16[4,256,512]{2,1,0:T(8,128)(2,1)} %get-tuple-element.84), channel_id=1, source_target_pairs={{0,4},{2,6},{4,0},{6,2},{8,12},{10,14},{12,8},{14,10},{16,20},{18,... | collective-permute-start | bytes 3145736 | tf_op jit(solution)/shard_map/ppermute | solution.py:42
  516.2 49.5 %collective-permute-start.2 = (bf16[512,2048]{1,0:T(8,128)(2,1)}, bf16[512,2048]{1,0:T(8,128)(2,1)}, u32[]{:S(2)}, u32[]{:S(2)}) collective-permute-start(bf16[512,2048]{1,0:T(8,128)(2,1)} %dynamic-slice_convert_fusion.1), channel_id=1, source_target_pairs={{0,2},{2,0},{4,6},{6,4},{8,10},{10,8},{12,14},{14,12},{16,18},{18,... | collective-permute-start | bytes 6291464 | tf_op jit(solution)/shard_map/ppermute | solution.py:46
  565.7 26.3 %collective-permute-start.40 = (bf16[4,256,512]{2,1,0:T(8,128)(2,1)}, bf16[4,256,512]{2,1,0:T(8,128)(2,1)S(1)}, u32[]{:S(2)}, u32[]{:S(2)}) collective-permute-start(bf16[4,256,512]{2,1,0:T(8,128)(2,1)} %get-tuple-element.90), channel_id=1, source_target_pairs={{0,4},{2,6},{4,0},{6,2},{8,12},{10,14},{12,8},{14,10},{16,20},{18,... | collective-permute-start | bytes 3145736 | tf_op jit(solution)/shard_map/ppermute | solution.py:42
  569.9 44.6 %collective-permute-start.53 = (bf16[4,256,512]{2,1,0:T(8,128)(2,1)S(1)}, bf16[4,256,512]{2,1,0:T(8,128)(2,1)S(1)}, u32[]{:S(2)}, u32[]{:S(2)}) collective-permute-start(bf16[4,256,512]{2,1,0:T(8,128)(2,1)S(1)} %copy-done.71), channel_id=1, source_target_pairs={{0,4},{2,6},{4,0},{6,2},{8,12},{10,14},{12,8},{14,10},{16,20},{18,... | collective-permute-start | bytes 3145736 | tf_op jit(solution)/shard_map/ppermute | solution.py:42
  571.5 161.0 %collective-permute-start.3 = (bf16[512,2048]{1,0:T(8,128)(2,1)S(1)}, bf16[512,2048]{1,0:T(8,128)(2,1)S(1)}, u32[]{:S(2)}, u32[]{:S(2)}) collective-permute-start(bf16[512,2048]{1,0:T(8,128)(2,1)S(1)} %add_convert_fusion.1), channel_id=1, source_target_pairs={{0,1},{1,0},{2,3},{3,2},{4,5},{5,4},{6,7},{7,6},{8,9},{9,8},{10,11... | collective-permute-start | bytes 6291464 | tf_op jit(solution)/shard_map/ppermute | solution.py:50
  575.2 61.8 %collective-permute-start.23 = (bf16[4,256,512]{2,1,0:T(8,128)(2,1)S(1)}, bf16[4,256,512]{2,1,0:T(8,128)(2,1)S(1)}, u32[]{:S(2)}, u32[]{:S(2)}) collective-permute-start(bf16[4,256,512]{2,1,0:T(8,128)(2,1)S(1)} %copy-done.73), channel_id=1, source_target_pairs={{0,4},{2,6},{4,0},{6,2},{8,12},{10,14},{12,8},{14,10},{16,20},{18,... | collective-permute-start | bytes 3145736 | tf_op jit(solution)/shard_map/ppermute | solution.py:42
  577.9 101.2 %collective-permute-start.36 = (bf16[4,256,512]{2,1,0:T(8,128)(2,1)S(1)}, bf16[4,256,512]{2,1,0:T(8,128)(2,1)S(1)}, u32[]{:S(2)}, u32[]{:S(2)}) collective-permute-start(bf16[4,256,512]{2,1,0:T(8,128)(2,1)S(1)} %copy-done.72), channel_id=1, source_target_pairs={{0,4},{2,6},{4,0},{6,2},{8,12},{10,14},{12,8},{14,10},{16,20},{18,... | collective-permute-start | bytes 3145736 | tf_op jit(solution)/shard_map/ppermute | solution.py:42
  592.0 95.4 %collective-permute-start.49 = (bf16[4,256,512]{2,1,0:T(8,128)(2,1)S(1)}, bf16[4,256,512]{2,1,0:T(8,128)(2,1)S(1)}, u32[]{:S(2)}, u32[]{:S(2)}) collective-permute-start(bf16[4,256,512]{2,1,0:T(8,128)(2,1)S(1)} %copy-done.70), channel_id=1, source_target_pairs={{0,4},{2,6},{4,0},{6,2},{8,12},{10,14},{12,8},{14,10},{16,20},{18,... | collective-permute-start | bytes 3145736 | tf_op jit(solution)/shard_map/ppermute | solution.py:42
  614.5 493.8 %collective-permute-start = (bf16[512,2048]{1,0:T(8,128)(2,1)}, bf16[512,2048]{1,0:T(8,128)(2,1)}, u32[]{:S(2)}, u32[]{:S(2)}) collective-permute-start(bf16[512,2048]{1,0:T(8,128)(2,1)} %dynamic-slice_convert_fusion.2), channel_id=1, source_target_pairs={{0,2},{2,0},{4,6},{6,4},{8,10},{10,8},{12,14},{14,12},{16,18},{18,... | collective-permute-start | bytes 6291464 | tf_op jit(solution)/shard_map/ppermute | solution.py:46
  637.0 99.4 %collective-permute-start.32 = (bf16[256,512]{1,0:T(8,128)(2,1)}, bf16[256,512]{1,0:T(8,128)(2,1)}, u32[]{:S(2)}, u32[]{:S(2)}) collective-permute-start(bf16[256,512]{1,0:T(8,128)(2,1)} %get-tuple-element.153), channel_id=1, source_target_pairs={{0,24},{2,26},{4,28},{6,30},{8,0},{10,2},{12,4},{14,6},{16,8},{18,... | collective-permute-start | bytes 786440 | tf_op jit(solution)/shard_map/ppermute | solution.py:31
  679.1 59.2 %collective-permute-start.34 = (bf16[256,512]{1,0:T(8,128)(2,1)S(1)}, bf16[256,512]{1,0:T(8,128)(2,1)}, u32[]{:S(2)}, u32[]{:S(2)}) collective-permute-start(bf16[256,512]{1,0:T(8,128)(2,1)S(1)} %get-tuple-element.154), channel_id=1, source_target_pairs={{0,8},{2,10},{4,12},{6,14},{8,16},{10,18},{12,20},{14,22},{16,24},... | collective-permute-start | bytes 786440 | tf_op jit(solution)/shard_map/ppermute | solution.py:31
  687.5 51.3 %collective-permute-start.33 = (bf16[256,512]{1,0:T(8,128)(2,1)S(1)}, bf16[256,512]{1,0:T(8,128)(2,1)}, u32[]{:S(2)}, u32[]{:S(2)}) collective-permute-start(bf16[256,512]{1,0:T(8,128)(2,1)S(1)} %get-tuple-element.155), channel_id=1, source_target_pairs={{0,16},{2,18},{4,20},{6,22},{8,24},{10,26},{12,28},{14,30},{16,0},... | collective-permute-start | bytes 786440 | tf_op jit(solution)/shard_map/ppermute | solution.py:31
  738.2 28.6 %collective-permute-start.46 = (bf16[256,512]{1,0:T(8,128)(2,1)S(1)}, bf16[256,512]{1,0:T(8,128)(2,1)S(1)}, u32[]{:S(2)}, u32[]{:S(2)}) collective-permute-start(bf16[256,512]{1,0:T(8,128)(2,1)S(1)} %get-tuple-element.146), channel_id=1, source_target_pairs={{0,16},{2,18},{4,20},{6,22},{8,24},{10,26},{12,28},{14,30},{16,0},... | collective-permute-start | bytes 786440 | tf_op jit(solution)/shard_map/ppermute | solution.py:31
  738.8 119.3 %collective-permute-start.4 = (bf16[512,2048]{1,0:T(8,128)(2,1)S(1)}, bf16[512,2048]{1,0:T(8,128)(2,1)S(1)}, u32[]{:S(2)}, u32[]{:S(2)}) collective-permute-start(bf16[512,2048]{1,0:T(8,128)(2,1)S(1)} %fusion.97), channel_id=1, source_target_pairs={{0,2},{2,0},{4,6},{6,4},{8,10},{10,8},{12,14},{14,12},{16,18},{18,... | collective-permute-start | bytes 6291464 | tf_op jit(solution)/shard_map/ppermute | solution.py:46
  749.5 22.5 %collective-permute-start.30 = (bf16[256,512]{1,0:T(8,128)(2,1)}, bf16[256,512]{1,0:T(8,128)(2,1)S(1)}, u32[]{:S(2)}, u32[]{:S(2)}) collective-permute-start(bf16[256,512]{1,0:T(8,128)(2,1)} %get-tuple-element.151), channel_id=1, source_target_pairs={{0,8},{2,10},{4,12},{6,14},{8,16},{10,18},{12,20},{14,22},{16,24},... | collective-permute-start | bytes 786440 | tf_op jit(solution)/shard_map/ppermute | solution.py:31
  811.8 22.5 %collective-permute-start.25 = (bf16[256,512]{1,0:T(8,128)(2,1)S(1)}, bf16[256,512]{1,0:T(8,128)(2,1)S(1)}, u32[]{:S(2)}, u32[]{:S(2)}) collective-permute-start(bf16[256,512]{1,0:T(8,128)(2,1)S(1)} %get-tuple-element.149), channel_id=1, source_target_pairs={{0,16},{2,18},{4,20},{6,22},{8,24},{10,26},{12,28},{14,30},{16,0},... | collective-permute-start | bytes 786440 | tf_op jit(solution)/shard_map/ppermute | solution.py:31
  813.9 22.5 %collective-permute-start.39 = (bf16[256,512]{1,0:T(8,128)(2,1)S(1)}, bf16[256,512]{1,0:T(8,128)(2,1)S(1)}, u32[]{:S(2)}, u32[]{:S(2)}) collective-permute-start(bf16[256,512]{1,0:T(8,128)(2,1)S(1)} %get-tuple-element.139), channel_id=1, source_target_pairs={{0,8},{2,10},{4,12},{6,14},{8,16},{10,18},{12,20},{14,22},{16,24},... | collective-permute-start | bytes 786440 | tf_op jit(solution)/shard_map/ppermute | solution.py:31
  834.3 22.5 %collective-permute-start.38 = (bf16[256,512]{1,0:T(8,128)(2,1)S(1)}, bf16[256,512]{1,0:T(8,128)(2,1)S(1)}, u32[]{:S(2)}, u32[]{:S(2)}) collective-permute-start(bf16[256,512]{1,0:T(8,128)(2,1)S(1)} %get-tuple-element.140), channel_id=1, source_target_pairs={{0,16},{2,18},{4,20},{6,22},{8,24},{10,26},{12,28},{14,30},{16,0},... | collective-permute-start | bytes 786440 | tf_op jit(solution)/shard_map/ppermute | solution.py:31
  835.2 83.7 %collective-permute-start.58 = (bf16[256,512]{1,0:T(8,128)(2,1)}, bf16[256,512]{1,0:T(8,128)(2,1)}, u32[]{:S(2)}, u32[]{:S(2)}) collective-permute-start(bf16[256,512]{1,0:T(8,128)(2,1)} %get-tuple-element.135), channel_id=1, source_target_pairs={{0,24},{2,26},{4,28},{6,30},{8,0},{10,2},{12,4},{14,6},{16,8},{18,... | collective-permute-start | bytes 786440 | tf_op jit(solution)/shard_map/ppermute | solution.py:31
  836.4 89.6 %collective-permute-start.60 = (bf16[256,512]{1,0:T(8,128)(2,1)}, bf16[256,512]{1,0:T(8,128)(2,1)}, u32[]{:S(2)}, u32[]{:S(2)}) collective-permute-start(bf16[256,512]{1,0:T(8,128)(2,1)} %get-tuple-element.136), channel_id=1, source_target_pairs={{0,8},{2,10},{4,12},{6,14},{8,16},{10,18},{12,20},{14,22},{16,24},... | collective-permute-start | bytes 786440 | tf_op jit(solution)/shard_map/ppermute | solution.py:31
  856.8 97.2 %collective-permute-start.59 = (bf16[256,512]{1,0:T(8,128)(2,1)}, bf16[256,512]{1,0:T(8,128)(2,1)}, u32[]{:S(2)}, u32[]{:S(2)}) collective-permute-start(bf16[256,512]{1,0:T(8,128)(2,1)} %get-tuple-element.137), channel_id=1, source_target_pairs={{0,16},{2,18},{4,20},{6,22},{8,24},{10,26},{12,28},{14,30},{16,0},... | collective-permute-start | bytes 786440 | tf_op jit(solution)/shard_map/ppermute | solution.py:31
  870.6 86.1 %collective-permute-start.54 = (bf16[256,512]{1,0:T(8,128)(2,1)}, bf16[256,512]{1,0:T(8,128)(2,1)}, u32[]{:S(2)}, u32[]{:S(2)}) collective-permute-start(bf16[256,512]{1,0:T(8,128)(2,1)} %get-tuple-element.132), channel_id=1, source_target_pairs={{0,24},{2,26},{4,28},{6,30},{8,0},{10,2},{12,4},{14,6},{16,8},{18,... | collective-permute-start | bytes 786440 | tf_op jit(solution)/shard_map/ppermute | solution.py:31
  919.7 40.0 %collective-permute-start.56 = (bf16[256,512]{1,0:T(8,128)(2,1)S(1)}, bf16[256,512]{1,0:T(8,128)(2,1)S(1)}, u32[]{:S(2)}, u32[]{:S(2)}) collective-permute-start(bf16[256,512]{1,0:T(8,128)(2,1)S(1)} %copy-done.44), channel_id=1, source_target_pairs={{0,8},{2,10},{4,12},{6,14},{8,16},{10,18},{12,20},{14,22},{16,24},... | collective-permute-start | bytes 786440 | tf_op jit(solution)/shard_map/ppermute | solution.py:31
  926.0 45.1 %collective-permute-start.55 = (bf16[256,512]{1,0:T(8,128)(2,1)S(1)}, bf16[256,512]{1,0:T(8,128)(2,1)S(1)}, u32[]{:S(2)}, u32[]{:S(2)}) collective-permute-start(bf16[256,512]{1,0:T(8,128)(2,1)S(1)} %copy-done.43), channel_id=1, source_target_pairs={{0,16},{2,18},{4,20},{6,22},{8,24},{10,26},{12,28},{14,30},{16,0},... | collective-permute-start | bytes 786440 | tf_op jit(solution)/shard_map/ppermute | solution.py:31
  954.0 56.8 %collective-permute-start.6 = (bf16[2048,256]{1,0:T(8,128)(2,1)S(1)}, bf16[2048,256]{1,0:T(8,128)(2,1)S(1)}, u32[]{:S(2)}, u32[]{:S(2)}) collective-permute-start(bf16[2048,256]{1,0:T(8,128)(2,1)S(1)} %fusion.18), channel_id=1, source_target_pairs={{8,0},{10,2},{12,4},{14,6},{16,8},{18,10},{20,12},{22,14},{24,16},... | collective-permute-start | bytes 3145736 | tf_op jit(solution)/shard_map/ppermute | solution.py:36
  956.8 32.6 %collective-permute-start.50 = (bf16[256,512]{1,0:T(8,128)(2,1)S(1)}, bf16[256,512]{1,0:T(8,128)(2,1)S(1)}, u32[]{:S(2)}, u32[]{:S(2)}) collective-permute-start(bf16[256,512]{1,0:T(8,128)(2,1)S(1)} %copy-done.47), channel_id=1, source_target_pairs={{0,24},{2,26},{4,28},{6,30},{8,0},{10,2},{12,4},{14,6},{16,8},{18,... | collective-permute-start | bytes 786440 | tf_op jit(solution)/shard_map/ppermute | solution.py:31
  959.7 38.2 %collective-permute-start.52 = (bf16[256,512]{1,0:T(8,128)(2,1)S(1)}, bf16[256,512]{1,0:T(8,128)(2,1)S(1)}, u32[]{:S(2)}, u32[]{:S(2)}) collective-permute-start(bf16[256,512]{1,0:T(8,128)(2,1)S(1)} %copy-done.46), channel_id=1, source_target_pairs={{0,8},{2,10},{4,12},{6,14},{8,16},{10,18},{12,20},{14,22},{16,24},... | collective-permute-start | bytes 786440 | tf_op jit(solution)/shard_map/ppermute | solution.py:31
  971.1 38.4 %collective-permute-start.51 = (bf16[256,512]{1,0:T(8,128)(2,1)S(1)}, bf16[256,512]{1,0:T(8,128)(2,1)S(1)}, u32[]{:S(2)}, u32[]{:S(2)}) collective-permute-start(bf16[256,512]{1,0:T(8,128)(2,1)S(1)} %copy-done.45), channel_id=1, source_target_pairs={{0,16},{2,18},{4,20},{6,22},{8,24},{10,26},{12,28},{14,30},{16,0},... | collective-permute-start | bytes 786440 | tf_op jit(solution)/shard_map/ppermute | solution.py:31
  989.4 24.6 %collective-permute-start.35 = (f32[128,1536]{1,0:T(8,128)S(1)}, f32[128,1536]{1,0:T(8,128)S(1)}, u32[]{:S(2)}, u32[]{:S(2)}) collective-permute-start(f32[128,1536]{1,0:T(8,128)S(1)} %copy-done.39), channel_id=1, source_target_pairs={{0,2},{2,0},{4,6},{6,4},{8,10},{10,8},{12,14},{14,12},{16,18},{18,... | collective-permute-start | bytes 2359304 | tf_op jit(solution)/shard_map/ppermute | solution.py:46
  997.9 103.6 %collective-permute-start.48 = (f32[128,1536]{1,0:T(8,128)}, f32[128,1536]{1,0:T(8,128)}, u32[]{:S(2)}, u32[]{:S(2)}) collective-permute-start(f32[128,1536]{1,0:T(8,128)} %get-tuple-element.165), channel_id=1, source_target_pairs={{0,2},{2,0},{4,6},{6,4},{8,10},{10,8},{12,14},{14,12},{16,18},{18,... | collective-permute-start | bytes 2359304 | tf_op jit(solution)/shard_map/ppermute | solution.py:46
  1011.1 24.8 %collective-permute-start.7 = (bf16[2048,256]{1,0:T(8,128)(2,1)S(1)}, bf16[2048,256]{1,0:T(8,128)(2,1)S(1)}, u32[]{:S(2)}, u32[]{:S(2)}) collective-permute-start(bf16[2048,256]{1,0:T(8,128)(2,1)S(1)} %fusion.15), channel_id=1, source_target_pairs={{8,0},{10,2},{12,4},{14,6},{16,8},{18,10},{20,12},{22,14},{24,16},... | collective-permute-start | bytes 3145736 | tf_op jit(solution)/shard_map/ppermute | solution.py:36
  1014.0 91.5 %collective-permute-start.61 = (f32[128,1536]{1,0:T(8,128)}, f32[128,1536]{1,0:T(8,128)}, u32[]{:S(2)}, u32[]{:S(2)}) collective-permute-start(f32[128,1536]{1,0:T(8,128)} %get-tuple-element.163), channel_id=1, source_target_pairs={{0,2},{2,0},{4,6},{6,4},{8,10},{10,8},{12,14},{14,12},{16,18},{18,... | collective-permute-start | bytes 2359304 | tf_op jit(solution)/shard_map/ppermute | solution.py:46
  1036.3 26.2 %collective-permute-start.8 = (bf16[1024,512]{1,0:T(8,128)(2,1)S(1)}, bf16[1024,512]{1,0:T(8,128)(2,1)S(1)}, u32[]{:S(2)}, u32[]{:S(2)}) collective-permute-start(bf16[1024,512]{1,0:T(8,128)(2,1)S(1)} %fusion.10), channel_id=1, source_target_pairs={{0,4},{2,6},{4,0},{6,2},{8,12},{10,14},{12,8},{14,10},{16,20},{18,... | collective-permute-start | bytes 3145736 | tf_op jit(solution)/shard_map/ppermute | solution.py:42
  1043.0 69.1 %collective-permute-start.18 = (bf16[4,256,512]{2,1,0:T(8,128)(2,1)}, bf16[4,256,512]{2,1,0:T(8,128)(2,1)}, u32[]{:S(2)}, u32[]{:S(2)}) collective-permute-start(bf16[4,256,512]{2,1,0:T(8,128)(2,1)} %pad_maximum_fusion.6), channel_id=1, source_target_pairs={{0,4},{2,6},{4,0},{6,2},{8,12},{10,14},{12,8},{14,10},{16,20},{18,... | collective-permute-start | bytes 3145736 | tf_op jit(solution)/shard_map/ppermute | solution.py:42
  1092.3 23.3 %collective-permute-start.9 = (bf16[512,2048]{1,0:T(8,128)(2,1)S(1)}, bf16[512,2048]{1,0:T(8,128)(2,1)S(1)}, u32[]{:S(2)}, u32[]{:S(2)}) collective-permute-start(bf16[512,2048]{1,0:T(8,128)(2,1)S(1)} %dynamic-slice_convert_fusion), channel_id=1, source_target_pairs={{0,2},{2,0},{4,6},{6,4},{8,10},{10,8},{12,14},{14,12},{16,18},{18,... | collective-permute-start | bytes 6291464 | tf_op jit(solution)/shard_map/ppermute | solution.py:46
  1101.5 48.1 %collective-permute-start.11 = (bf16[4,256,1024]{2,1,0:T(8,128)(2,1)S(1)}, bf16[4,256,1024]{2,1,0:T(8,128)(2,1)S(1)}, u32[]{:S(2)}, u32[]{:S(2)}) collective-permute-start(bf16[4,256,1024]{2,1,0:T(8,128)(2,1)S(1)} %pad_maximum_fusion.2), channel_id=1, source_target_pairs={{0,4},{2,6},{4,0},{6,2},{8,12},{10,14},{12,8},{14,10},{16,20},{18,... | collective-permute-start | bytes 6291464 | tf_op jit(solution)/shard_map/ppermute | solution.py:42
  1113.5 36.9 %collective-permute-start.19 = (bf16[256,512]{1,0:T(8,128)(2,1)S(1)}, bf16[256,512]{1,0:T(8,128)(2,1)S(1)}, u32[]{:S(2)}, u32[]{:S(2)}) collective-permute-start(bf16[256,512]{1,0:T(8,128)(2,1)S(1)} %get-tuple-element.126), channel_id=1, source_target_pairs={{0,24},{2,26},{4,28},{6,30},{8,0},{10,2},{12,4},{14,6},{16,8},{18,... | collective-permute-start | bytes 786440 | tf_op jit(solution)/shard_map/ppermute | solution.py:31
  1113.5 38.8 %collective-permute-start.21 = (bf16[256,512]{1,0:T(8,128)(2,1)S(1)}, bf16[256,512]{1,0:T(8,128)(2,1)S(1)}, u32[]{:S(2)}, u32[]{:S(2)}) collective-permute-start(bf16[256,512]{1,0:T(8,128)(2,1)S(1)} %get-tuple-element.127), channel_id=1, source_target_pairs={{0,8},{2,10},{4,12},{6,14},{8,16},{10,18},{12,20},{14,22},{16,24},... | collective-permute-start | bytes 786440 | tf_op jit(solution)/shard_map/ppermute | solution.py:31
  1115.5 36.8 %collective-permute-start.20 = (bf16[256,512]{1,0:T(8,128)(2,1)S(1)}, bf16[256,512]{1,0:T(8,128)(2,1)S(1)}, u32[]{:S(2)}, u32[]{:S(2)}) collective-permute-start(bf16[256,512]{1,0:T(8,128)(2,1)S(1)} %get-tuple-element.128), channel_id=1, source_target_pairs={{0,16},{2,18},{4,20},{6,22},{8,24},{10,26},{12,28},{14,30},{16,0},... | collective-permute-start | bytes 786440 | tf_op jit(solution)/shard_map/ppermute | solution.py:31
  1116.3 85.2 %collective-permute-start.10 = (bf16[512,2048]{1,0:T(8,128)(2,1)S(1)}, bf16[512,2048]{1,0:T(8,128)(2,1)S(1)}, u32[]{:S(2)}, u32[]{:S(2)}) collective-permute-start(bf16[512,2048]{1,0:T(8,128)(2,1)S(1)} %add_convert_fusion), channel_id=1, source_target_pairs={{0,1},{1,0},{2,3},{3,2},{4,5},{5,4},{6,7},{7,6},{8,9},{9,8},{10,11... | collective-permute-start | bytes 6291464 | tf_op jit(solution)/shard_map/ppermute | solution.py:50
  1150.3 25.3 %collective-permute-start.12 = (bf16[256,1024]{1,0:T(8,128)(2,1)S(1)}, bf16[256,1024]{1,0:T(8,128)(2,1)S(1)}, u32[]{:S(2)}, u32[]{:S(2)}) collective-permute-start(bf16[256,1024]{1,0:T(8,128)(2,1)S(1)} %get-tuple-element.117), channel_id=1, source_target_pairs={{0,24},{2,26},{4,28},{6,30},{8,0},{10,2},{12,4},{14,6},{16,8},{18,... | collective-permute-start | bytes 1572872 | tf_op jit(solution)/shard_map/ppermute | solution.py:31
  1150.3 25.2 %collective-permute-start.14 = (bf16[256,1024]{1,0:T(8,128)(2,1)S(1)}, bf16[256,1024]{1,0:T(8,128)(2,1)S(1)}, u32[]{:S(2)}, u32[]{:S(2)}) collective-permute-start(bf16[256,1024]{1,0:T(8,128)(2,1)S(1)} %get-tuple-element.118), channel_id=1, source_target_pairs={{0,8},{2,10},{4,12},{6,14},{8,16},{10,18},{12,20},{14,22},{16,24},... | collective-permute-start | bytes 1572872 | tf_op jit(solution)/shard_map/ppermute | solution.py:31
  1152.3 44.6 %collective-permute-start.13 = (bf16[256,1024]{1,0:T(8,128)(2,1)S(1)}, bf16[256,1024]{1,0:T(8,128)(2,1)S(1)}, u32[]{:S(2)}, u32[]{:S(2)}) collective-permute-start(bf16[256,1024]{1,0:T(8,128)(2,1)S(1)} %get-tuple-element.119), channel_id=1, source_target_pairs={{0,16},{2,18},{4,20},{6,22},{8,24},{10,26},{12,28},{14,30},{16,0},... | collective-permute-start | bytes 1572872 | tf_op jit(solution)/shard_map/ppermute | solution.py:31
  1152.4 90.2 %collective-permute-start.1 = (bf16[512,2048]{1,0:T(8,128)(2,1)}, bf16[512,2048]{1,0:T(8,128)(2,1)}, u32[]{:S(2)}, u32[]{:S(2)}) collective-permute-start(bf16[512,2048]{1,0:T(8,128)(2,1)} %add_convert_fusion.3), channel_id=1, source_target_pairs={{0,1},{1,0},{2,3},{3,2},{4,5},{5,4},{6,7},{7,6},{8,9},{9,8},{10,11... | collective-permute-start | bytes 6291464 | tf_op jit(solution)/shard_map/ppermute | solution.py:50
  1175.5 22.8 %collective-permute-start.22 = (f32[128,512]{1,0:T(8,128)S(1)}, f32[128,512]{1,0:T(8,128)S(1)}, u32[]{:S(2)}, u32[]{:S(2)}) collective-permute-start(f32[128,512]{1,0:T(8,128)S(1)} %get-tuple-element.177), channel_id=1, source_target_pairs={{0,2},{2,0},{4,6},{6,4},{8,10},{10,8},{12,14},{14,12},{16,18},{18,... | collective-permute-start | bytes 786440 | tf_op jit(solution)/shard_map/ppermute | solution.py:46
  (90 other events, 2569.3 us)

commit v2 on v1

--- a/solution.py
+++ b/solution.py
@@ -81,145 +81,6 @@
     turn = position.astype(F32)[:, None] * freq[None, :]
     turn = jnp.concatenate([turn, turn], axis=-1)
     return (jnp.cos(turn), jnp.sin(turn))
-
-
-def attn_bwd_kernel(
-    rows, blocks, info, q_ref, g_ref, k_ref, v_ref, start_ref, l_ref, r_ref, dq_ref, dk_ref, dv_ref
-):
-    i = pl.program_id(0)
-    d = k_ref.shape[1]
-    scale = 1.0 / math.sqrt(d)
-
-    @pl.when(i == 0)
-    def _():
-        dk_ref[...] = jnp.zeros_like(dk_ref)
-        dv_ref[...] = jnp.zeros_like(dv_ref)
-
-    dq_ref[...] = jnp.zeros_like(dq_ref)
-    q2 = jnp.concatenate([q_ref[:, :d], q_ref[:, d:]], axis=0)
-    g2 = jnp.concatenate([g_ref[:, :d], g_ref[:, d:]], axis=0)
-    log_total = jnp.concatenate([l_ref[0:1, :], l_ref[1:2, :]], axis=1)
-    row_dot = jnp.concatenate([r_ref[0:1, :], r_ref[1:2, :]], axis=1)
-    q_block = info[0, i]
-
-    def step(j, carry):
-        k_block = info[1, j]
-        need = (k_block <= q_block) & (k_block >= 0) & (k_block * rows + rows - 1 >= info[2, i])
-        whole = (k_block < q_block) & (k_block * rows >= info[3, i])
-        at = pl.ds(pl.multiple_of(j * rows, rows), rows)
-
-        def part(masked):
-            k_now = k_ref[at, :]
-            score = dot(k_now, q2, NT)
-            prob = jnp.exp2(score * (scale * LOG2E) - log_total)
-            if masked:
-                k_pos = k_block * rows + lax.broadcasted_iota(jnp.int32, (rows, rows), 0)
-                q_pos = q_block * rows + lax.broadcasted_iota(jnp.int32, (rows, rows), 1)
-                keep = (k_pos <= q_pos) & (k_pos >= start_ref[...])
-                prob = jnp.where(jnp.concatenate([keep, keep], axis=1), prob, 0.0)
-            d_prob = dot(v_ref[at, :], g2, NT)
-            d_score = (prob * (d_prob - row_dot)).astype(BF16)
-            dv_ref[at, :] += dot(prob.astype(BF16), g2)
-            dk_ref[at, :] += dot(d_score, q2)
-            d_q = dot(d_score, k_now, TN)
-            dq_ref[:, :d] += d_q[:rows]
-            dq_ref[:, d:] += d_q[rows:]
-
-        pl.when(need & whole)(lambda: part(False))
-        pl.when(need & jnp.logical_not(whole))(lambda: part(True))
-        return carry
-
-    lax.fori_loop(0, blocks, step, 0)
-
-
-def attn_bwd(info, q, g, k, v, start, log_total, row_dot, rows):
-    n_q, width = q.shape[0] // rows, q.shape[1]
-    blocks = k.shape[0] // rows
-    whole = lambda i, s: (0, 0)
-    part = lambda i, s: (i, 0)
-    row = lambda i, s: (0, i)
-    return pl.pallas_call(
-        partial(attn_bwd_kernel, rows, blocks),
-        grid_spec=pltpu.PrefetchScalarGridSpec(
-            num_scalar_prefetch=1,
-            grid=(n_q,),
-            in_specs=[
-                pl.BlockSpec((rows, width), part),
-                pl.BlockSpec((rows, width), part),
-                pl.BlockSpec(k.shape, whole),
-                pl.BlockSpec(v.shape, whole),
-                pl.BlockSpec((1, rows), row),
-                pl.BlockSpec((2, rows), row),
-                pl.BlockSpec((2, rows), row),
-            ],
-            out_specs=[
-                pl.BlockSpec((rows, width), part),
-                pl.BlockSpec(k.shape, whole),
-                pl.BlockSpec(k.shape, whole),
-            ],
-        ),
-        out_shape=[
-            jax.ShapeDtypeStruct(q.shape, F32),
-            jax.ShapeDtypeStruct(k.shape, F32),
-            jax.ShapeDtypeStruct(k.shape, F32),
-        ],
-        compiler_params=pltpu.CompilerParams(vmem_limit_bytes=VMEM_LIMIT),
-        cost_estimate=pl.CostEstimate(flops=50 * 10**9, bytes_accessed=10**7, transcendentals=10**7),
-        name="attn_bwd",
-    )(info, q, g, k, v, start, log_total, row_dot)
-
-
-def ffn_kernel(pieces, block, offs, s_ref, g_ref, st_ref, gt_ref, w_gate, w_up, w_down, mlp_ref, ds_ref, *grads):
-    f = pl.program_id(0)
-
-    @pl.when(f == 0)
-    def _():
-        mlp_ref[...] = jnp.zeros_like(mlp_ref)
-        ds_ref[...] = jnp.zeros_like(ds_ref)
-
-    s, g = s_ref[...], g_ref[...]
-    gate = dot(s, w_gate[...])
-    up = dot(s, w_up[...])
-    d_act = dot(g, w_down[...])
-    sig = 1.0 / (1.0 + jnp.exp(-gate))
-    silu = gate * sig
-    act = (silu * up).astype(BF16)
-    d_gate = (d_act * up * sig * (1.0 + gate * (1.0 - sig))).astype(BF16)
-    d_up = (d_act * silu).astype(BF16)
-    mlp_ref[...] += dot(act, w_down[...], NT)
-    ds_ref[...] += dot(d_gate, w_gate[...], NT) + dot(d_up, w_up[...], NT)
-    half = pieces // 2
-    for k, (left, right) in enumerate(((st_ref, d_gate), (st_ref, d_up), (gt_ref, act))):
-        for j in range(pieces):
-            at = pl.ds(pl.multiple_of(offs[j], block), block)
-            grads[2 * k + j // half][j % half] = dot(left[at, :], right).astype(BF16)
-
-
-def ffn_chunk(offs, s, g, st, gt, full_w, block):
-    units = full_w.shape[1] // 3
-    ft = min(256, units)
-    n = offs.shape[0]
-    tokens, width = s.shape
-    steps = units // ft
-    whole = lambda a: pl.BlockSpec(a.shape, lambda f, o: (0, 0))
-    w_specs = [pl.BlockSpec((width, ft), lambda f, o, k=kind: (0, k * steps + f)) for kind in range(3)]
-    grad_spec = pl.BlockSpec((n // 2, block, ft), lambda f, o: (0, 0, f))
-    return pl.pallas_call(
-        partial(ffn_kernel, n, block),
-        grid_spec=pltpu.PrefetchScalarGridSpec(
-            num_scalar_prefetch=1,
-            grid=(steps,),
-            in_specs=[whole(a) for a in (s, g, st, gt)] + w_specs,
-            out_specs=[whole(s)] * 2 + [grad_spec] * 6,
-        ),
-        out_shape=[jax.ShapeDtypeStruct(s.shape, F32)] * 2
-        + [jax.ShapeDtypeStruct((n // 2, block, units), BF16)] * 6,
-        compiler_params=pltpu.CompilerParams(vmem_limit_bytes=VMEM_LIMIT),
-        cost_estimate=pl.CostEstimate(
-            flops=18 * tokens * width * units, bytes_accessed=10**7, transcendentals=tokens * units
-        ),
-        name="ffn",
-    )(offs, s, g, st, gt, full_w, full_w, full_w)
 
 
 class Net:
@@ -232,6 +93,9 @@
         self.quads = lax.axis_size("dp") // 4
         self.sems, self.used = sems, 0
         self.pending = []
+        self.to_core = self.at(core=1 - self.core)
+        self.to_x = self.at(x=1 - self.x)
+        self.to_tensor = self.at(tensor=1 - self.tensor)
 
     def sem(self):
         self.used += 1
@@ -245,13 +109,13 @@
         return (quad * 4 + x * 2 + core, tensor)
 
     def other_core(self):
-        return self.at(core=1 - self.core)
+        return self.to_core
 
     def other_x(self):
-        return self.at(x=1 - self.x)
+        return self.to_x
 
     def other_tensor(self):
-        return self.at(tensor=1 - self.tensor)
+        return self.to_tensor
 
     def greet(self):
         targets = [self.other_core(), self.other_x(), self.other_tensor()]
@@ -380,9 +244,7 @@
     second_out,
     qkv_full,
     o_full,
-    ff0,
-    ff1,
-    ff2,
+    ff_full,
     sems,
     first,
     w_qkv,
@@ -407,7 +269,7 @@
     rows, width = tokens.shape
     d = q_gain.shape[1]
     shard = wq.shape[0]
-    units = ff0.shape[1] // 3
+    units = ff_full.shape[2] // 3
     my_rows = pl.ds(pl.multiple_of(n.core * rows, rows), rows)
     chip_rows = pl.ds(pl.multiple_of(n.x * 2 * rows, 2 * rows), 2 * rows)
     back = kx.shape[0] - 1
@@ -418,11 +280,11 @@
     ff = [
         Gather(
             n,
-            full,
+            ff_full.at[i],
             shard,
             [(wg, i * units, units, 0), (wu, i * units, units, units), (wd, i * units, units, 2 * units)],
         )
-        for i, full in enumerate((ff0, ff1, ff2))
+        for i in range(ff_full.shape[0])
     ]
     qkv.start()
     o_w.start()
@@ -637,7 +499,7 @@
     return pl.pallas_call(
         forward_kernel,
         in_specs=[vmem, hbm] + [vmem] * 7 + [hbm] * 7,
-        out_specs=[hbm] * 16,
+        out_specs=[hbm] * 14,
         out_shape=[
             shape((2 * rows, width), BF16),
             shape((2 * rows, width), BF16),
@@ -652,8 +514,8 @@
             shape((2 * rows, width), BF16),
             shape((width, 8 * d), BF16),
             shape((width, 4 * d), BF16),
-        ]
-        + [shape((width, 3 * units), BF16)] * 3,
+            shape((3, width, 3 * units), BF16),
+        ],
         scratch_shapes=[
             pltpu.SemaphoreType.DMA((80 + 5 * (2 * quads + 3),)),
             pltpu.VMEM((2 * rows, width), BF16),
@@ -693,6 +555,777 @@
     )
 
 
+class Scatter:
+    def __init__(self, net, keep, send, x_land, z_land, loaded, added, slot):
+        self.net, self.keep, self.send, self.x_land, self.z_land = net, keep, send, x_land, z_land
+        self.loaded, self.added, self.slot = loaded, added, slot
+        self.own_waited = False
+        self.x_sent, self.x_got, self.z_sent, self.z_got, self.own, self.tmp = [net.sem() for _ in range(6)]
+
+    def start(self):
+        n = self.net
+        n.copy(self.send, self.x_land, n.other_x(), self.x_sent, self.x_got).start()
+
+    def add(self):
+        n = self.net
+        pieces, shard, cols = self.keep.shape
+        total = self.added.at[self.slot, :, :, pl.ds(0, cols)]
+        other = self.loaded.at[:, :, pl.ds(0, cols)]
+        first = pltpu.make_async_copy(self.keep, total, self.tmp)
+        first.start()
+        wait_bytes(self.x_land, self.x_got)
+        second = pltpu.make_async_copy(self.x_land, other, self.own)
+        second.start()
+        first.wait()
+        second.wait()
+
+        def one(i, carry):
+            total[i] = (total[i].astype(F32) + other[i].astype(F32)).astype(BF16)
+            return carry
+
+        lax.fori_loop(0, pieces, one, 0)
+        pltpu.make_async_copy(total.at[n.core], self.z_land.at[n.core], self.own).start()
+        n.copy(
+            total.at[1 - n.core], self.z_land.at[n.core], n.other_core(), self.z_sent, self.z_got
+        ).start()
+        for s in range(1, n.quads):
+            to = lax.rem(n.quad + n.quads - s, n.quads)
+            for c in range(2):
+                n.copy(
+                    total.at[2 * s + c],
+                    self.z_land.at[2 * s + n.core],
+                    n.at(quad=to, core=c),
+                    self.z_sent,
+                    self.z_got,
+                ).start()
+
+    def sent(self):
+        pieces = self.keep.shape[0]
+        wait_bytes(self.send, self.x_sent)
+        wait_bytes(self.z_land.at[pl.ds(0, pieces - 1)], self.z_sent)
+        self.own_done()
+
+    def own_done(self):
+        if not self.own_waited:
+            wait_bytes(self.z_land.at[0], self.own)
+        self.own_waited = True
+
+    def final(self, out, write):
+        pieces, shard, cols = self.keep.shape
+        wait_bytes(self.z_land.at[pl.ds(0, pieces - 1)], self.z_got)
+        self.own_done()
+        got = self.loaded.at[:, :, pl.ds(0, cols)]
+        load = pltpu.make_async_copy(self.z_land, got, self.tmp)
+        load.start()
+        load.wait()
+        for c in range(2):
+            total = got[c].astype(F32)
+            for s in range(1, pieces // 2):
+                total = total + got[2 * s + c].astype(F32)
+            out[c, :, pl.ds(0, cols)] = total
+        copies = []
+        for c in range(2):
+            for at, wide, dst, col in write(c):
+                k = pltpu.make_async_copy(
+                    out.at[c, :, pl.ds(at, wide)], dst.at[:, pl.ds(col, wide)], self.tmp
+                )
+                k.start()
+                copies.append((at, wide))
+        wait_bytes(out.at[:, :, pl.ds(0, cols)], self.tmp)
+
+
+def norm_back(values, gain, grad):
+    scale = lax.rsqrt(jnp.mean(values * values, axis=-1, keepdims=True) + EPS)
+    scaled = grad * gain
+    inner = jnp.mean(scaled * values, axis=-1, keepdims=True)
+    gain_part = jnp.sum(grad * values * scale, axis=0, keepdims=True)
+    return scale * scaled - values * (scale * scale * scale * inner), gain_part
+
+
+def backward_kernel(*refs):
+    (
+        tokens,
+        attn_gain,
+        mlp_gain,
+        q_gain,
+        k_gain,
+        cosine,
+        sine,
+        start,
+        first_t_in,
+        grad_in,
+        grad_t_in,
+        second_in,
+        second_t_in,
+        proj_in,
+        plane_in,
+        k_in,
+        v_in,
+        heads_in,
+        stat_in,
+        attn_in,
+        middle_in,
+        qkv_full,
+        o_full,
+        ff_full,
+        output,
+        input_grad,
+        gain_out,
+        g_q,
+        g_k,
+        g_v,
+        g_o,
+        g_gate,
+        g_up,
+        g_down,
+        ff_keep,
+        ff_send,
+        ff_xland,
+        ff_zland,
+        at_keep,
+        at_send,
+        at_xland,
+        at_zland,
+        core_land,
+        low_land,
+        mlp_own,
+        mlp_low,
+        da_land,
+        heads_land,
+        kv_land,
+        back_land,
+        sems,
+        loaded,
+        added,
+        summed,
+        low_send,
+        gains,
+        gains_land,
+    ) = refs
+    n = Net(sems)
+    rows, width = tokens.shape
+    d = q_gain.shape[1]
+    pieces, shard, ff_cols = ff_keep.shape[1:]
+    tiles = ff_keep.shape[0]
+    ft = ff_cols // 3
+    per_chunk = tiles // ff_full.shape[0]
+    units = ff_full.shape[2] // 3
+    half_ff = tiles * ft
+    quads = n.quads
+    block = 2 * shard
+    my_at = pl.multiple_of(n.core * rows, rows)
+    their_at = pl.multiple_of((1 - n.core) * rows, rows)
+    my_chip = pl.ds(pl.multiple_of(n.x * 2 * rows, 2 * rows), 2 * rows)
+    other_chip = pl.ds(pl.multiple_of((1 - n.x) * 2 * rows, 2 * rows), 2 * rows)
+    n.greet()
+    step, tall = 128, 256
+    steps = rows // step
+    low_sent = [n.sem() for _ in range(steps)]
+    low_got = [n.sem() for _ in range(steps)]
+
+    ff = [
+        Scatter(n, ff_keep.at[f], ff_send.at[f], ff_xland.at[f], ff_zland.at[f], loaded, added, f % 2)
+        for f in range(tiles)
+    ]
+    at_groups = [
+        Scatter(n, at_keep.at[f], at_send.at[f], at_xland.at[f], at_zland.at[f], loaded, added, f % 2)
+        for f in range(3)
+    ]
+
+    def ff_write(f):
+        def places(c):
+            col = c * half_ff + f * ft
+            return [(k * ft, ft, dst, col) for k, dst in enumerate((g_gate, g_up, g_down))]
+
+        return places
+
+    def row_block(xr, s):
+        quad = lax.rem(n.quad + quads - s, quads)
+        x = n.x if xr == 0 else 1 - n.x
+        return pl.multiple_of((quad * 4 + 2 * x) * shard, block)
+
+    def load(pairs):
+        copies = [pltpu.make_async_copy(s, t, n.sem()) for s, t in pairs]
+        for c in copies:
+            c.start()
+        return copies
+
+    def ffn_phase(s, g, st, gt, w, mlp, ds, acts, stage, w_sem, stage_sem):
+        first = load([(second_in, s), (grad_in, g), (second_t_in, st), (grad_t_in, gt)])
+
+        def fetch(f, slot):
+            chunk, sub = lax.div(f, per_chunk), lax.rem(f, per_chunk)
+            for k in range(3):
+                col = pl.multiple_of(k * units + sub * ft, ft)
+                pltpu.make_async_copy(
+                    ff_full.at[chunk, :, pl.ds(col, ft)], w.at[slot, k], w_sem.at[slot]
+                ).start()
+
+        fetch(0, 0)
+        mlp[...] = jnp.zeros_like(mlp)
+        ds[...] = jnp.zeros_like(ds)
+        for c in first:
+            c.wait()
+
+        def staged(f):
+            for k, dst in enumerate((ff_keep, ff_send)):
+                yield pltpu.make_async_copy(stage.at[k], dst.at[f], stage_sem.at[k])
+
+        def tile(f, carry):
+            slot = lax.rem(f, 2)
+
+            @pl.when(f + 1 < tiles)
+            def _():
+                fetch(f + 1, 1 - slot)
+
+            wait_bytes(w.at[slot], w_sem.at[slot])
+            def some_rows(i, inner):
+                at = pl.ds(pl.multiple_of(i * rows, rows), rows)
+                gate = dot(s[at, :], w[slot, 0])
+                up = dot(s[at, :], w[slot, 1])
+                d_act = dot(g[at, :], w[slot, 2])
+                sig = 1.0 / (1.0 + jnp.exp(-gate))
+                silu = gate * sig
+                acts[at, pl.ds(2 * ft, ft)] = (silu * up).astype(BF16)
+                acts[at, pl.ds(0, ft)] = (d_act * up * sig * (1.0 + gate * (1.0 - sig))).astype(BF16)
+                acts[at, pl.ds(ft, ft)] = (d_act * silu).astype(BF16)
+                mlp[at, :] += dot(acts[at, pl.ds(2 * ft, ft)], w[slot, 2], NT)
+                ds[at, :] += dot(acts[at, pl.ds(0, ft)], w[slot, 0], NT) + dot(
+                    acts[at, pl.ds(ft, ft)], w[slot, 1], NT
+                )
+                return inner
+
+            lax.fori_loop(0, 2, some_rows, 0)
+
+            @pl.when(f >= 1)
+            def _():
+                for c in staged(f - 1):
+                    c.wait()
+
+            for k in range(1, tiles):
+
+                @pl.when(f == k)
+                def _(k=k):
+                    if k - 1 < 4:
+                        ff[k - 1].start()
+
+            for xr in range(2):
+                for q in range(quads):
+                    at = pl.ds(row_block(xr, q), block)
+                    left = dot(st[at, :], acts[:, pl.ds(0, 2 * ft)]).astype(BF16)
+                    right = dot(gt[at, :], acts[:, pl.ds(2 * ft, ft)]).astype(BF16)
+                    for c in range(2):
+                        cut = slice(c * shard, (c + 1) * shard)
+                        stage[xr, 2 * q + c, :, pl.ds(0, 2 * ft)] = left[cut]
+                        stage[xr, 2 * q + c, :, pl.ds(2 * ft, ft)] = right[cut]
+            for c in staged(f):
+                c.start()
+            for k in range(3, tiles):
+
+                @pl.when(f == k)
+                def _(k=k):
+                    if k >= 5:
+                        ff[k - 5].sent()
+                    ff[k - 3].add()
+
+            return carry
+
+        lax.fori_loop(0, tiles, tile, 0)
+        core_copies = []
+        for i in range(rows // step):
+            at = pl.ds(i * step, step)
+            g[at, :] = ds[pl.ds(their_at + i * step, step), :].astype(BF16)
+            core_copies.append(n.copy(g.at[at], core_land.at[0, at], n.other_core()))
+            core_copies[-1].start()
+        for c in staged(tiles - 1):
+            c.wait()
+
+        def to_low(i, carry):
+            at = pl.ds(pl.multiple_of(i * step, step), step)
+            s[at, :] = mlp[at, :].astype(BF16)
+            return carry
+
+        lax.fori_loop(0, 2 * rows // step, to_low, 0)
+        mlp_copy = n.copy(s.at[pl.ds(their_at, rows)], core_land.at[1], n.other_core())
+        mlp_copy.start()
+        mlp_keep = pltpu.make_async_copy(s.at[pl.ds(my_at, rows)], mlp_own, n.sem())
+        mlp_keep.start()
+        for i in range(rows // step):
+            at = pl.ds(i * step, step)
+            core_copies[i].wait_recv()
+            take = pltpu.make_async_copy(core_land.at[0, at], g.at[pl.ds(rows + i * step, step)], n.sem())
+            take.start()
+            take.wait()
+            low_send[at, :] = (
+                ds[pl.ds(my_at + i * step, step), :] + g[pl.ds(rows + i * step, step), :].astype(F32)
+            ).astype(BF16)
+            n.copy(
+                low_send.at[at], low_land.at[0, at], n.other_tensor(), low_sent[i], low_got[i]
+            ).start()
+        for c in core_copies:
+            c.wait_send()
+        mlp_copy.wait_send()
+        mlp_copy.wait_recv()
+        mlp_keep.wait()
+
+    bf = lambda *shape: pltpu.VMEM(shape, BF16)
+    f32 = lambda *shape: pltpu.VMEM(shape, F32)
+    pl.run_scoped(
+        ffn_phase,
+        bf(2 * rows, width),
+        bf(2 * rows, width),
+        bf(width, 2 * rows),
+        bf(width, 2 * rows),
+        bf(2, 3, width, ft),
+        f32(2 * rows, width),
+        f32(2 * rows, width),
+        bf(2 * rows, ff_cols),
+        bf(2, pieces, shard, ff_cols),
+        pltpu.SemaphoreType.DMA((2,)),
+        pltpu.SemaphoreType.DMA((2,)),
+    )
+
+    def rest(
+        big,
+        big_t,
+        d_middle,
+        tmp,
+        tmp_low,
+        w_o,
+        plane,
+        kx,
+        vx,
+        heads,
+        stat,
+        attn,
+        d_out,
+        d_q,
+        d_kv,
+        kv_low,
+        d_low,
+        d_proj,
+        stage,
+        proj,
+    ):
+        def load_now(pairs):
+            for c in load(pairs):
+                c.wait()
+
+        loads = load(
+            [
+                (o_full, w_o),
+                (plane_in, plane),
+                (k_in, kx),
+                (v_in, vx),
+                (heads_in, heads),
+                (stat_in, stat.at[pl.ds(0, 2)]),
+                (attn_in, attn),
+            ]
+        )
+        gains[...] = jnp.zeros_like(gains)
+        ff[1].sent()
+        ff[3].add()
+        ff[0].final(summed, ff_write(0))
+
+        for i in range(steps):
+            at = pl.ds(i * step, step)
+            load_now([(mlp_own.at[at], tmp_low.at[0]), (core_land.at[1, at], tmp_low.at[1])])
+            tmp_low[0] = (tmp_low[0].astype(F32) + tmp_low[1].astype(F32)).astype(BF16)
+            load_now([(tmp_low.at[0], mlp_low.at[at])])
+
+        da_copies = []
+        for i in range(steps):
+            at = pl.ds(i * step, step)
+            to = pl.ds(my_at + i * step, step)
+            wait_bytes(low_land.at[0, at], low_got[i])
+            load_now(
+                [
+                    (low_land.at[0, at], tmp_low.at[0]),
+                    (middle_in.at[at], tmp),
+                    (grad_in.at[to], tmp_low.at[1]),
+                ]
+            )
+            d_second = low_send[at, :].astype(F32) + tmp_low[0].astype(F32)
+            back, part = norm_back(tmp[...], mlp_gain[...], d_second)
+            gains[1:2, :] += part
+            d_mid = tmp_low[1].astype(F32) + back
+            d_middle[at, :] = d_mid
+            big[to, :] = d_mid.astype(BF16)
+            da_copies.append(n.copy(big.at[to], da_land.at[at], n.other_core()))
+            da_copies[-1].start()
+        mlp_copy = n.send(mlp_low, low_land.at[1], n.other_tensor())
+        for i in range(steps):
+            wait_bytes(low_send.at[pl.ds(i * step, step)], low_sent[i])
+        for c in loads:
+            c.wait()
+        for c in da_copies:
+            c.wait()
+        load_now([(da_land, big.at[pl.ds(their_at, rows)])])
+
+        def head_grads(i, carry):
+            at = pl.ds(pl.multiple_of(i * tall, tall), tall)
+            got = dot(big[at, :], w_o[...]).astype(BF16)
+            d_low[0, at, pl.ds(0, 2 * d)] = got[:, : 2 * d]
+            d_low[1, at, pl.ds(0, 2 * d)] = got[:, 2 * d :]
+            return carry
+
+        lax.fori_loop(0, 2 * rows // tall, head_grads, 0)
+        heads_copy = n.copy(d_low.at[1 - n.x, :, pl.ds(0, 2 * d)], heads_land, n.other_x())
+        heads_copy.start()
+        ff[4].start()
+        ff[5].start()
+        d_out[my_chip, :] = d_low[n.x, :, pl.ds(0, 2 * d)]
+        d_q[...] = jnp.zeros_like(d_q)
+
+        def flip(i, carry):
+            at = pl.ds(pl.multiple_of(i * tall, tall), tall)
+            big_t[at, :] = big[:, at].T
+            return carry
+
+        lax.fori_loop(0, width // tall, flip, 0)
+        both_halves = jnp.concatenate([attn[0], attn[1]], axis=1)
+
+        def weight_pieces(right, into):
+            for xr in range(2):
+                for q in range(quads):
+                    got = dot(big_t[pl.ds(row_block(xr, q), block), :], right).astype(BF16)
+                    for k in range(got.shape[1] // (4 * d)):
+                        for c in range(2):
+                            stage[into + k, xr, 2 * q + c] = got[
+                                c * shard : (c + 1) * shard, k * 4 * d : (k + 1) * 4 * d
+                            ]
+
+        def stage_out(k, g):
+            return load([(stage.at[k, 0], at_keep.at[g]), (stage.at[k, 1], at_send.at[g])])
+
+        weight_pieces(both_halves, 0)
+        o_stage = stage_out(0, 0)
+        heads_copy.wait_recv()
+        load_now([(heads_land, d_out.at[other_chip])])
+        for c in o_stage:
+            c.wait()
+        at_groups[0].start()
+
+        for g in range(2):
+            for i in range(4):
+                at = pl.ds(i * rows, rows)
+                cols = pl.ds(g * d, d)
+                prod = d_out[at, cols].astype(F32) * heads[at, cols]
+                stat[2 + g : 3 + g, at] = jnp.sum(prod.T, axis=0, keepdims=True)
+        scale = 1.0 / math.sqrt(d)
+
+        def attend_back(h, i, j):
+            q_at = pl.ds(pl.multiple_of(i * rows, rows), rows)
+            k_at = pl.ds(pl.multiple_of(j * rows, rows), rows)
+            kv_at = pl.ds(pl.multiple_of(h * 4 * rows + j * rows, rows), rows)
+            q2 = jnp.concatenate([plane[q_at, pl.ds(0, d)], plane[q_at, pl.ds(d, d)]], axis=0)
+            g2 = jnp.concatenate([d_out[q_at, pl.ds(0, d)], d_out[q_at, pl.ds(d, d)]], axis=0)
+            log_total = jnp.concatenate([stat[0:1, q_at], stat[1:2, q_at]], axis=1)
+            row_dot = jnp.concatenate([stat[2:3, q_at], stat[3:4, q_at]], axis=1)
+            k_now = kx[kv_at, :]
+            prob = jnp.exp2(dot(k_now, q2, NT) * (scale * LOG2E) - log_total)
+            k_pos = (4 * (n.quad - h) + j) * rows + lax.broadcasted_iota(jnp.int32, (rows, rows), 0)
+            keep = k_pos >= start[:, q_at]
+            if h == 0:
+                q_pos = (4 * n.quad + i) * rows + lax.broadcasted_iota(jnp.int32, (rows, rows), 1)
+                keep = keep & (k_pos <= q_pos)
+            prob = jnp.where(jnp.concatenate([keep, keep], axis=1), prob, 0.0)
+            d_prob = dot(vx[kv_at, :], g2, NT)
+            d_score = (prob * (d_prob - row_dot)).astype(BF16)
+            d_kv[k_at, pl.ds(d, d)] += dot(prob.astype(BF16), g2)
+            d_kv[k_at, pl.ds(0, d)] += dot(d_score, q2)
+            got = dot(d_score, k_now, TN)
+            d_q[q_at, pl.ds(0, d)] += got[:rows]
+            d_q[q_at, pl.ds(d, d)] += got[rows:]
+
+        def plane_back(h, lo, hi):
+            d_kv[...] = jnp.zeros_like(d_kv)
+
+            def over_i(i, carry):
+                def over_j(j, inner):
+                    attend_back(h, i, j)
+                    return inner
+
+                lax.fori_loop(lo(i), hi(i), over_j, 0)
+                return carry
+
+            lax.fori_loop(0, 4, over_i, 0)
+            d_kv[:, pl.ds(0, d)] = d_kv[:, pl.ds(0, d)] * scale
+
+        behind = n.at(quad=jnp.maximum(n.quad - 1, 0))
+        ranges = {
+            0: (lambda i: 0, lambda i: i + 1),
+            1: (lambda i: 0, lambda i: 4),
+            2: (lambda i: i, lambda i: 4),
+        }
+        top = kv_low.shape[0]
+        hops = [n.copy(kv_low.at[k], kv_land.at[k], behind) for k in range(top)]
+        kv_sem = n.sem()
+
+        def add_landed(k):
+            hops[k].wait_recv()
+            for part in range(2):
+                at = pl.ds(part * 2 * rows, 2 * rows)
+                c = pltpu.make_async_copy(
+                    kv_land.at[k, at], d_low.at[part, :, pl.ds(0, 2 * d)], kv_sem
+                )
+                c.start()
+                c.wait()
+                d_kv[at, :] += d_low[part, :, pl.ds(0, 2 * d)].astype(F32)
+
+        heads_copy.wait_send()
+        for h in range(top, 0, -1):
+
+            @pl.when(n.quad >= h)
+            def _(h=h):
+                plane_back(h, *ranges[h])
+                if h < top:
+
+                    @pl.when(n.quad < quads - 1)
+                    def _():
+                        add_landed(top - h - 1)
+
+                kv_low[top - h] = d_kv[...].astype(BF16)
+                hops[top - h].start()
+
+            if h == top:
+                ff[1].final(summed, ff_write(1))
+                ff[2].sent()
+                ff[4].add()
+                ff[2].final(summed, ff_write(2))
+        plane_back(0, *ranges[0])
+        ff[3].sent()
+        ff[5].add()
+        ff[3].final(summed, ff_write(3))
+
+        @pl.when(n.quad < quads - 1)
+        def _():
+            add_landed(top - 1)
+
+        def put_back(x):
+            def body(i, carry):
+                at = pl.ds(pl.multiple_of(i * tall, tall), tall)
+                src = pl.ds(pl.multiple_of(x * 2 * rows + i * tall, tall), tall)
+                d_low[x, at, pl.ds(0, 2 * d)] = (d_q[src, :] * scale).astype(BF16)
+                d_low[x, at, pl.ds(2 * d, 2 * d)] = d_kv[src, :].astype(BF16)
+                return carry
+
+            lax.fori_loop(0, 2 * rows // tall, body, 0)
+
+        put_back(1 - n.x)
+        back_copy = n.copy(d_low.at[1 - n.x], back_land, n.other_x())
+        back_copy.start()
+        put_back(n.x)
+        late = load([(qkv_full, big_t)])
+        ff[4].sent()
+        at_groups[0].add()
+        ff[4].final(summed, ff_write(4))
+        back_copy.wait_send()
+        back_copy.wait_recv()
+        load_now([(back_land, d_low.at[1 - n.x])])
+
+        def prep_back(i, carry):
+            at = pl.ds(pl.multiple_of(i * step, step), step)
+            got = pltpu.make_async_copy(proj_in.at[at], proj, kv_sem)
+            got.start()
+            got.wait()
+            cos, sin = cosine[at, :], sine[at, :]
+
+            def back(col, h, src, gain, row):
+                grad = d_low[h, at, pl.ds(src, d)].astype(F32)
+                turned = grad * cos + pltpu.roll(grad * sin, d // 2, 1)
+                res, part = norm_back(proj[:, pl.ds(col, d)], gain[...], turned)
+                gains[pl.ds(row, 1), pl.ds(0, d)] += part
+                d_proj[at, pl.ds(col, d)] = res.astype(BF16)
+
+            for h in range(2):
+                for g in range(2):
+                    back((2 * h + g) * d, h, g * d, q_gain, 2)
+                back((4 + h) * d, h, 2 * d, k_gain, 3)
+                d_proj[at, pl.ds((6 + h) * d, d)] = d_low[h, at, pl.ds(3 * d, d)]
+            return carry
+
+        lax.fori_loop(0, 2 * rows // step, prep_back, 0)
+        for c in late:
+            c.wait()
+
+        core_copies, low_copies = [], []
+        for i in range(steps):
+            at = pl.ds(i * step, step)
+            big[at, :] = dot(d_proj[pl.ds(their_at + i * step, step), :], big_t[...], NT).astype(BF16)
+            core_copies.append(n.send(big.at[at], core_land.at[2, at], n.other_core()))
+        for i in range(steps):
+            at = pl.ds(i * step, step)
+            part = dot(d_proj[pl.ds(my_at + i * step, step), :], big_t[...], NT)
+            core_copies[i].wait_recv()
+            load_now([(core_land.at[2, at], tmp_low.at[0])])
+            low_send[at, :] = (part + tmp_low[0].astype(F32)).astype(BF16)
+            low_copies.append(n.send(low_send.at[at], low_land.at[2, at], n.other_tensor()))
+
+        load_now([(first_t_in, big_t)])
+        weight_pieces(d_proj[...], 0)
+        for c in stage_out(0, 1) + stage_out(1, 2):
+            c.wait()
+        at_groups[1].start()
+        at_groups[2].start()
+        ff[5].final(summed, ff_write(5))
+
+        mlp_copy.wait_recv()
+        for i in range(steps):
+            at = pl.ds(i * step, step)
+            load_now(
+                [
+                    (low_land.at[1, at], tmp_low.at[0]),
+                    (mlp_low.at[at], tmp_low.at[1]),
+                    (middle_in.at[at], tmp),
+                ]
+            )
+            tmp_low[0] = (tmp[...] + (tmp_low[1].astype(F32) + tmp_low[0].astype(F32))).astype(BF16)
+            load_now([(tmp_low.at[0], output.at[at])])
+        for i in range(steps):
+            at = pl.ds(i * step, step)
+            low_copies[i].wait_recv()
+            load_now([(low_land.at[2, at], tmp_low.at[0]), (tokens.at[at], tmp_low.at[1])])
+            d_first = low_send[at, :].astype(F32) + tmp_low[0].astype(F32)
+            back, part = norm_back(tmp_low[1].astype(F32), attn_gain[...], d_first)
+            gains[0:1, :] += part
+            d_middle[at, :] = d_middle[at, :] + back
+            n.keep(d_middle.at[at], input_grad.at[at])
+
+        for k, to in enumerate((n.other_core(), n.other_x(), n.other_tensor())):
+            c = n.copy(gains, gains_land.at[k], to)
+            c.start()
+            c.wait()
+            if k < 2:
+                gains[...] += gains_land[k]
+            else:
+                gains[2:4, :] += gains_land[k, 2:4, :]
+        gains_land[3 + n.quad] = gains[...]
+        quad_copies = []
+        for s in range(1, quads):
+            to = n.at(quad=lax.rem(n.quad + s, quads))
+            quad_copies.append(n.copy(gains, gains_land.at[3 + n.quad], to))
+            quad_copies[-1].start()
+        for c in quad_copies:
+            c.wait()
+        total = gains_land[3]
+        for k in range(1, quads):
+            total = total + gains_land[3 + k]
+        gains[...] = total
+        n.keep(gains, gain_out)
+
+        ff[5].sent()
+        at_groups[1].add()
+
+        def simple(places):
+            return lambda c: [(at, wide, dst, c * wide) for at, wide, dst in places]
+
+        at_groups[0].final(summed, simple([(0, 4 * d, g_o)]))
+        at_groups[0].sent()
+        at_groups[2].add()
+        at_groups[1].final(summed, simple([(0, 4 * d, g_q)]))
+        at_groups[2].final(summed, simple([(0, 2 * d, g_k), (2 * d, 2 * d, g_v)]))
+        at_groups[1].sent()
+        at_groups[2].sent()
+        for k in range(top):
+
+            @pl.when(n.quad >= top - k)
+            def _(k=k):
+                hops[k].wait_send()
+
+        n.finish()
+
+    top = kv_land.shape[0]
+    pl.run_scoped(
+        rest,
+        bf(2 * rows, width),
+        bf(width, 2 * rows),
+        f32(rows, width),
+        f32(128, width),
+        bf(2, 128, width),
+        bf(width, 4 * d),
+        bf(4 * rows, 4 * d),
+        bf(4 * rows * (top + 1), d),
+        bf(4 * rows * (top + 1), d),
+        f32(4 * rows, 2 * d),
+        f32(4, 4 * rows),
+        bf(2, 2 * rows, 2 * d),
+        bf(4 * rows, 2 * d),
+        f32(4 * rows, 2 * d),
+        f32(4 * rows, 2 * d),
+        bf(top, 4 * rows, 2 * d),
+        bf(2, 2 * rows, 4 * d),
+        bf(2 * rows, 8 * d),
+        bf(2, 2, pieces, shard, 4 * d),
+        f32(128, 8 * d),
+    )
+
+
+def backward(tokens, attn_gain, mlp_gain, q_gain, k_gain, cosine, sine, start, *arrays):
+    rows, width = tokens.shape
+    d = q_gain.shape[0]
+    ff_full = arrays[-1]
+    quads = lax.axis_size("dp") // 4
+    shard = width // (4 * quads)
+    chunks, half_ff = ff_full.shape[0], ff_full.shape[0] * ff_full.shape[2] // 3
+    tiles = 2 * chunks
+    cols = 3 * half_ff // tiles
+    top = REACH // 4
+    vmem = pl.BlockSpec(memory_space=pltpu.VMEM)
+    hbm = pl.BlockSpec(memory_space=pl.ANY)
+    shape = jax.ShapeDtypeStruct
+    out_shape = [
+        shape((rows, width), BF16),
+        shape((rows, width), F32),
+        shape((4, width), F32),
+        shape((shard, 8 * d), F32),
+        shape((shard, 4 * d), F32),
+        shape((shard, 4 * d), F32),
+        shape((shard, 8 * d), F32),
+        shape((shard, 2 * half_ff), F32),
+        shape((shard, 2 * half_ff), F32),
+        shape((shard, 2 * half_ff), F32),
+    ]
+    out_shape += [shape((tiles, 2 * quads, shard, cols), BF16)] * 4
+    out_shape += [shape((3, 2 * quads, shard, 4 * d), BF16)] * 4
+    out_shape += [shape((3, rows, width), BF16)] * 2
+    out_shape += [shape((rows, width), BF16)] * 3
+    out_shape += [
+        shape((2 * rows, 2 * d), BF16),
+        shape((top, 4 * rows, 2 * d), BF16),
+        shape((2 * rows, 4 * d), BF16),
+    ]
+    return pl.pallas_call(
+        backward_kernel,
+        in_specs=[hbm] + [vmem] * 7 + [hbm] * len(arrays),
+        out_specs=[hbm] * len(out_shape),
+        out_shape=out_shape,
+        scratch_shapes=[
+            pltpu.SemaphoreType.DMA((260,)),
+            pltpu.VMEM((2 * quads, shard, max(cols, 4 * d)), BF16),
+            pltpu.VMEM((2, 2 * quads, shard, max(cols, 4 * d)), BF16),
+            pltpu.VMEM((2, shard, max(cols, 4 * d)), F32),
+            pltpu.VMEM((rows, width), BF16),
+            pltpu.VMEM((4, width), F32),
+            pltpu.VMEM((3 + quads, 4, width), F32),
+        ],
+        compiler_params=pltpu.CompilerParams(
+            collective_id=1, has_side_effects=True, vmem_limit_bytes=VMEM_LIMIT
+        ),
+        name="backward",
+    )(
+        tokens,
+        attn_gain[None],
+        mlp_gain[None],
+        q_gain[None],
+        k_gain[None],
+        cosine,
+        sine,
+        start,
+        *arrays,
+    )[:10]
+
+
 def local(
     tokens,
     out_grad,
@@ -709,46 +1342,15 @@
     up_weight,
     down_weight,
 ):
-    rows, width = tokens.shape
+    rows = tokens.shape[0]
     d = q_gain.shape[0]
-    devices = lax.axis_size("dp")
-    quads = devices // 4
     me = lax.axis_index("dp")
-    quad, x, core = me // 4, (me // 2) % 2, me % 2
-    shard = q_weight.shape[0]
-    block = 2 * shard
-    kv_here = key_matrix.shape[1] // d
-    group = q_weight.shape[1] // key_matrix.shape[1]
-    assert kv_here == 4 and group == 2
-
-    def pick(arr, index, count, axis):
-        size = arr.shape[axis] // count
-        return lax.dynamic_slice_in_dim(arr, index * size, size, axis)
-
-    def ordered(mine, other, flag, axis):
-        return jnp.where(
-            flag == 0,
-            jnp.concatenate([mine, other], axis),
-            jnp.concatenate([other, mine], axis),
-        )
-
-    offs = jnp.stack(
-        [
-            ((quad - s) % quads) * 2 * block + jnp.where(xr == 0, x, 1 - x) * block
-            for xr in range(2)
-            for s in range(quads)
-        ]
-    ).astype(jnp.int32)
-
-    def both(mine_rows):
-        return ordered(mine_rows, swap_core(mine_rows), core, 0)
-
+    assert key_matrix.shape[1] == 4 * d and q_weight.shape[1] == 8 * d
     chip_index = (me // 2) * 2 * rows + jnp.arange(2 * rows, dtype=jnp.int32)
     cosine, sine_vals = angles(chip_index - starts_of(chip_index, lengths), d)
     sine_signed = jnp.concatenate([-sine_vals[:, : d // 2], sine_vals[:, d // 2 :]], 1)
-    q_index = quad * 4 * rows + jnp.arange(4 * rows, dtype=jnp.int32)
+    q_index = (me // 4) * 4 * rows + jnp.arange(4 * rows, dtype=jnp.int32)
     q_start = starts_of(q_index, lengths)
-    tokens_wide = tokens.astype(F32)
     (
         first_chip,
         grad_chip,
@@ -763,7 +1365,7 @@
         second_chip,
         qkv_full,
         o_full,
-        *ff_full,
+        ff_full,
     ) = forward(
         tokens,
         out_grad,
@@ -782,127 +1384,46 @@
         up_weight,
         down_weight,
     )
-    q_plane = plane[:, : group * d]
-    attn_low = jnp.concatenate([attn_halves[0], attn_halves[1]], 1)
-    back_hops = REACH // 4
-    q_blocks = 4 * quad + jnp.arange(4)
-    k_blocks = jnp.concatenate([q_blocks - 4 * h for h in range(back_hops + 1)])
-    by_block = q_start.reshape(-1, rows)
-    lanes = k_blocks.shape[0]
-    info = jnp.stack(
-        [
-            jnp.pad(v, (0, lanes - v.shape[0]))
-            for v in (q_blocks, k_blocks, by_block[:, 0], by_block[:, -1])
-        ]
-    ).astype(jnp.int32)
-
-    def prep_q(p, gain):
-        return head_prep(p.reshape(2 * rows, 2 * group, d), gain, cosine, sine_vals)
-
-    def prep_k(p, gain):
-        return head_prep(p.reshape(2 * rows, 2, d), gain, cosine, sine_vals)
-
-    q_in, k_in = proj[:, : 4 * d], proj[:, 4 * d : 6 * d]
-
-    def core_sum(part):
-        low_part = pick(part, 1 - core, 2, 0).astype(BF16)
-        return pick(part, core, 2, 0) + swap_core(low_part).astype(F32)
-
-    second_t, grad_t = second_chip.T, grad_chip.T
-
-    def scatter(keep, send):
-        got = swap_x(send)
-        sums = [
-            (keep[s].astype(F32) + got[s].astype(F32)).astype(BF16) for s in range(quads)
-        ]
-        total = sums[0].astype(F32)
-        for s in range(1, quads):
-            total = total + over_quads(sums[s], -s).astype(F32)
-        return total
-
-    def to_cores(total):
-        own = pick(total, core, 2, 0)
-        return ordered(own, swap_core(pick(total, 1 - core, 2, 0)), core, 1)
-
-    ff_grads = [[], [], []]
-    mlp_part, d_second_part = 0.0, 0.0
-    for full_w in ff_full:
-        got = ffn_chunk(offs, second_chip, grad_chip, second_t, grad_t, full_w, block)
-        mlp_part, d_second_part = mlp_part + got[0], d_second_part + got[1]
-        for n in range(3):
-            ff_grads[n].append(scatter(got[2 + 2 * n], got[3 + 2 * n]))
-    grad_gate, grad_up, grad_down = (to_cores(jnp.concatenate(g, 1)) for g in ff_grads)
-
-    d_second = tensor_sum(core_sum(d_second_part))
-    mlp_out = tensor_sum(core_sum(mlp_part))
-    output = (middle + mlp_out).astype(BF16)
-    unused_mid, norm_back_mid = jax.vjp(rms_rows, middle, mlp_gain)
-    d_middle_norm, grad_mlp_local = norm_back_mid(d_second)
-    d_middle = out_grad.astype(F32) + d_middle_norm
-    d_attn = both(d_middle.astype(BF16))
-
-    def split_rows(grad):
-        by = grad.reshape(quads, 2, block, -1)
-        order = (quad - jnp.arange(quads)) % quads
-        keep = lax.dynamic_index_in_dim(by, x, 1, False)
-        send = lax.dynamic_index_in_dim(by, 1 - x, 1, False)
-
-        def rel(a):
-            return [lax.dynamic_index_in_dim(a, order[s], 0, False) for s in range(quads)]
-
-        return jnp.stack(rel(keep)), jnp.stack(rel(send))
-
-    grad_o = to_cores(scatter(*split_rows(dot(d_attn, attn_low, TN).astype(BF16))))
-    d_heads = dot(d_attn, o_full).astype(BF16)
-    d_heads_plane = ordered(pick(d_heads, x, 2, 1), swap_x(pick(d_heads, 1 - x, 2, 1)), x, 0)
-    row_dot = jnp.sum(
-        (d_heads_plane.astype(F32) * heads_out).reshape(4 * rows, group, d), axis=-1
-    ).T
-    d_q, d_k, d_v = attn_bwd(
-        info, q_plane, d_heads_plane, k_all, v_all, q_start[None, :], log_total, row_dot, rows
-    )
-    scale = 1.0 / math.sqrt(d)
-    d_kv = jnp.concatenate([d_k * scale, d_v], 1).reshape(back_hops + 1, 4 * rows, 2 * d)
-    carried = d_kv[back_hops]
-    for h in reversed(range(back_hops)):
-        carried = d_kv[h] + shift_quads(carried.astype(BF16), -1).astype(F32)
-    d_plane = jnp.concatenate([d_q * scale, carried], 1)
-    d_mine = pick(d_plane, x, 2, 0)
-    d_back = swap_x(pick(d_plane, 1 - x, 2, 0).astype(BF16)).astype(F32)
-    d_low = jnp.where(x == 0, jnp.stack([d_mine, d_back], 1), jnp.stack([d_back, d_mine], 1))
-    unused_q, q_back = jax.vjp(prep_q, q_in, q_gain)
-    d_q_proj, q_gain_local = q_back(d_low[:, :, : group * d].reshape(2 * rows, 2 * group, d))
-    unused_k, k_back = jax.vjp(prep_k, k_in, k_gain)
-    d_k_proj, k_gain_local = k_back(d_low[:, :, group * d : (group + 1) * d])
-    d_proj = jnp.concatenate(
-        [d_q_proj, d_k_proj, d_low[:, :, (group + 1) * d :].reshape(2 * rows, -1)], 1
-    ).astype(BF16)
-    grad_qkv = scatter(*split_rows(dot(first_chip, d_proj, TN).astype(BF16)))
-    grad_q = to_cores(grad_qkv[:, : 4 * d])
-    grad_k = to_cores(grad_qkv[:, 4 * d : 6 * d])
-    grad_v = to_cores(grad_qkv[:, 6 * d :])
-    d_first = tensor_sum(core_sum(dot(d_proj, qkv_full, NT)))
-    unused_in, norm_back_in = jax.vjp(rms_rows, tokens_wide, attn_gain)
-    d_tokens_norm, grad_attn_local = norm_back_in(d_first)
-    input_grad = d_middle + d_tokens_norm
-    grad_attn_gain, grad_mlp_gain, grad_q_gain, grad_k_gain = lax.psum(
-        (0.5 * grad_attn_local, 0.5 * grad_mlp_local, q_gain_local, k_gain_local),
-        ("dp", "tensor"),
+    output, input_grad, gains, g_q, g_k, g_v, g_o, g_gate, g_up, g_down = backward(
+        tokens,
+        attn_gain,
+        mlp_gain,
+        q_gain,
+        k_gain,
+        cosine,
+        sine_signed,
+        q_start[None, :],
+        first_chip.T,
+        grad_chip,
+        grad_chip.T,
+        second_chip,
+        second_chip.T,
+        proj,
+        plane,
+        k_all,
+        v_all,
+        heads_out,
+        log_total,
+        attn_halves,
+        middle,
+        qkv_full,
+        o_full,
+        ff_full,
     )
     return (
         output,
         input_grad,
-        grad_attn_gain,
-        grad_q,
-        grad_k,
-        grad_v,
-        grad_o,
-        grad_q_gain,
-        grad_k_gain,
-        grad_mlp_gain,
-        grad_gate,
-        grad_up,
-        grad_down,
+        gains[0],
+        g_q,
+        g_k,
+        g_v,
+        g_o,
+        gains[2, :d],
+        gains[3, :d],
+        gains[1],
+        g_gate,
+        g_up,
+        g_down,
     )
 
 

time: 1260 us -> 959 us (0.76)
  Pallas kernels: 501 us -> 908 us
  waiting for transfers between devices: 254 us -> 0 us
  starting transfers between devices: 244 us -> 0 us
  other arithmetic: 114 us -> 5.83 us
  blocking collectives: 39.4 us -> 0 us
  local copies, waits for them, and re-layouts: 73.6 us -> 35.4 us
  matrix products: 18.2 us -> 0 us
    pallas_call x4 -> x1, Pallas kernels: 133 us -> 540 us  [backward(): pl.pallas_call(backward_kernel, in_specs=[hbm] + [vmem] * 7 + [hbm] * len...]
    ppermute x62 -> x0, waiting for transfers between devices: 254 us -> none  [the longest x33 128 us: over_quads(): return lax.ppermute(value, 'dp', [(i, (i + 4 * by) % n) for i in range(n)])]
    ppermute x62 -> x0, starting transfers between devices: 244 us -> none  [the longest x33 221 us: over_quads(): return lax.ppermute(value, 'dp', [(i, (i + 4 * by) % n) for i in range(n)])]
    add x17 -> x1, other arithmetic: 39.9 us -> 0.01 us  [local(): q_index = me // 4 * 4 * rows + jnp.arange(4 * rows, dtype=jnp.int32)]
    psum x1 -> x0, blocking collectives: 39.4 us -> none  [local(): lax.psum((0.5 * grad_attn_local, 0.5 * grad_mlp_local, q_gain_local, k_ga...]
    convert_element_type x17 -> x0, other arithmetic: 25 us -> none  [the longest x11 14.9 us: scatter(): (keep[s].astype(F32) + got[s].astype(F32)).astype(BF16)]
    dot_general x4 -> x0, matrix products: 18.2 us -> none  [dot(): return lax.dot_general(a, b, dims, preferred_element_type=F32)]
    slice x12 -> x1, local copies, waits for them, and re-layouts: 19.6 us -> 1.45 us  [local(): gains[1]]
  transfers between devices with their start and end apart: 62 -> 0, of which waited for: 23 -> 0; matrix products, arithmetic and copies ran while one was open for 13% -> 0% of each run, Pallas kernels for 8% -> 0%
where the time goes in v2:
time: 959 us; the launch traced here: 950 us
  Pallas kernels  908 us (95%)
  local copies, waits for them, and re-layouts  35.4 us (4%)
    pallas_call x1, Pallas kernels, backward(): pl.pallas_call(backward_kernel, in_specs=[hbm] + [vmem] * 7 + [hbm] * len...  540 us
    pallas_call x1, Pallas kernels, forward(): pl.pallas_call(forward_kernel, in_specs=[vmem, hbm] + [vmem] * 7 + [hbm]...  368 us
    pallas_call x3, local copies, waits for them, and re-layouts, forward(): pl.pallas_call(forward_kernel, in_specs=[vmem, hbm] + [vmem] * 7 + [hbm]...  19.5 us

profile of v2, /device:TPU:0, one launch (start us, length us, event | category | flops | bytes accessed | tf_op | source)
XLA Modules:
  0.0 950.1 jit_solution(14303275449502270613)
XLA Ops:
  0.7 0.8 reduce-window.8
  1.5 0.7 bitcast_subtract_fusion
  2.2 0.1 select_reduce_fusion.1
  2.3 0.1 select_reduce_fusion
  2.4 0.0 copy-start.8
  2.4 0.2 broadcast_multiply_fusion
  2.6 2.7 fusion
  5.3 0.2 slice_negate_fusion
  5.5 1.0 pad_maximum_fusion.1.sine.refs_6_
  6.5 1.3 copy.34.start
  7.9 0.0 copy-done.8
  7.9 368.1 %forward.1 = (bf16[1024,2048]{1,0:T(8,128)(2,1)}, bf16[1024,2048]{1,0:T(8,128)(2,1)}, f32[1024,1024]{1,0:T(8,128)}, bf16[2048,512]{1,0:T(8,128)(2,1)}, bf16[6144...) custom-call(bf16[512,2048]{1,0:T(8,128)(2,1)} %refs_0_.1, ...), custom_call_target="tpu_custom_call" | custom-call | tf_op jit(solution)/shard_map/forward/pallas_call | solution.py:499
  376.0 6.7 copy.35
  382.7 6.4 copy.36
  389.1 6.4 copy.37
  395.5 539.7 %backward.1 = (bf16[512,2048]{1,0:T(8,128)(2,1)}, f32[512,2048]{1,0:T(8,128)}, f32[4,2048]{1,0:T(4,128)}, f32[128,1024]{1,0:T(8,128)}, f32[128,512]{1,0:T(8,128)...) custom-call(bf16[512,2048]{1,0:T(8,128)(2,1)} %refs_0_.1, ...), custom_call_target="tpu_custom_call" | custom-call | tf_op jit(solution)/shard_map/backward/pallas_call | solution.py:1298
  935.1 0.0 copy-start
  935.2 1.3 slice_bitcast_fusion
  936.5 1.4 fusion.2
  937.9 3.2 copy.47
  941.1 0.0 copy-done
  941.1 0.0 copy-start.5
  941.1 0.0 copy-start.7
  941.1 0.0 copy-start.6
  941.1 0.0 copy-start.4
  941.1 0.0 copy-start.3
  941.1 2.1 copy.48
  943.3 0.0 copy-done.5
  943.3 0.0 copy-start.2
  943.3 0.8 copy.49
  944.1 0.0 copy-done.7
  944.1 0.7 copy.50
  944.8 0.0 copy-done.6
  944.8 0.7 copy.51
  945.5 0.0 copy-done.4
  945.5 0.8 copy.52
  946.3 0.0 copy-done.3
  946.3 0.0 copy-start.1
  946.3 1.1 copy.53
  947.4 0.0 copy-done.2
  947.4 1.1 copy.54
  948.6 0.0 copy-done.1
  948.6 1.1 copy.55
  (4 shorter events, 0.0 us)
Async XLA Ops:
  2.4 5.5 copy-start.8
  935.1 6.0 copy-start
  941.1 2.2 copy-start.5
  941.1 3.0 copy-start.7
  941.1 3.7 copy-start.6
  941.1 4.4 copy-start.4
  941.1 5.2 copy-start.3
  943.3 4.2 copy-start.2
  946.3 2.3 copy-start.1

commit v3 on v0

v3 whole, which is shorter than its diff:
```python
from functools import partial
import math

import jax
import jax.numpy as jnp
from jax import lax
from jax.experimental import pallas as pl
from jax.experimental.pallas import tpu as pltpu
from jax.sharding import PartitionSpec as P

REACH = 8
EPS = 1e-06
THETA = 1000000.0
LOG2E = 1.4426950408889634
F32 = jnp.float32
BF16 = jnp.bfloat16
VMEM_LIMIT = 62 * 1024 * 1024

NT = (((1,), (1,)), ((), ()))
NN = (((1,), (0,)), ((), ()))
TN = (((0,), (0,)), ((), ()))
MESH = pl.DeviceIdType.MESH


def dot(a, b, dims=NN):
    return lax.dot_general(a, b, dims, preferred_element_type=F32)


def over_quads(value, by):
    n = lax.axis_size("dp")
    return lax.ppermute(value, "dp", [(i, (i + 4 * by) % n) for i in range(n)])


def shift_quads(value, by):
    n = lax.axis_size("dp")
    return lax.ppermute(
        value, "dp", [(i, i + 4 * by) for i in range(n) if 0 <= i + 4 * by < n]
    )


def swap_x(value):
    return lax.ppermute(value, "dp", [(i, i ^ 2) for i in range(lax.axis_size("dp"))])


def swap_core(value):
    return lax.ppermute(value, "dp", [(i, i ^ 1) for i in range(lax.axis_size("dp"))])


def swap_tensor(value):
    return lax.ppermute(value, "tensor", [(0, 1), (1, 0)])


def tensor_sum(part):
    low = part.astype(BF16)
    return low.astype(F32) + swap_tensor(low).astype(F32)


def rms_rows(values, gain_vec):
    return values * lax.rsqrt(jnp.mean(values * values, axis=-1, keepdims=True) + EPS) * gain_vec


def rotate(values):
    half_size = values.shape[-1] // 2
    return jnp.concatenate([-values[..., half_size:], values[..., :half_size]], axis=-1)


def head_prep(heads_view, gain_vec, cosine, sine_vals):
    normed = rms_rows(heads_view, gain_vec)
    return normed * cosine[:, None, :] + rotate(normed) * sine_vals[:, None, :]


def starts_of(index, lengths):
    ends = jnp.cumsum(lengths)
    starts = ends - lengths
    inside = (index[:, None] >= starts[None, :]) & (index[:, None] < ends[None, :])
    return jnp.sum(jnp.where(inside, starts[None, :], 0), axis=1)


def angles(position, head_dim):
    freq = THETA ** (-(jnp.arange(0, head_dim, 2, dtype=F32) / head_dim))
    turn = position.astype(F32)[:, None] * freq[None, :]
    turn = jnp.concatenate([turn, turn], axis=-1)
    return (jnp.cos(turn), jnp.sin(turn))


class Net:
    def __init__(self, sems):
        me = lax.axis_index("dp")
        self.me, self.tensor = me, lax.axis_index("tensor")
        self.core = lax.rem(me, 2)
        self.x = lax.rem(lax.div(me, 2), 2)
        self.quad = lax.div(me, 4)
        self.quads = lax.axis_size("dp") // 4
        self.sems, self.used = sems, 0
        self.pending = []
        self.to_core = self.at(core=1 - self.core)
        self.to_x = self.at(x=1 - self.x)
        self.to_tensor = self.at(tensor=1 - self.tensor)

    def sem(self):
        self.used += 1
        return self.sems.at[self.used - 1]

    def at(self, quad=None, x=None, core=None, tensor=None):
        quad = self.quad if quad is None else quad
        x = self.x if x is None else x
        core = self.core if core is None else core
        tensor = self.tensor if tensor is None else tensor
        return (quad * 4 + x * 2 + core, tensor)

    def flipped(self, bits):
        quad, bit = self.quad, 1
        while bit <= bits:
            if bits & bit:
                quad = quad + bit * (1 - 2 * lax.rem(lax.div(self.quad, bit), 2))
            bit *= 2
        return quad

    def other_core(self):
        return self.to_core

    def other_x(self):
        return self.to_x

    def other_tensor(self):
        return self.to_tensor

    def greet(self):
        targets = [self.other_core(), self.other_x(), self.other_tensor()]
        for s in range(1, self.quads):
            for c in range(2):
                targets.append(self.at(quad=lax.rem(self.quad + s, self.quads), core=c))
        barrier = pltpu.get_barrier_semaphore()
        for t in targets:
            pl.semaphore_signal(barrier, inc=1, device_id=t, device_id_type=MESH)
        pl.semaphore_wait(barrier, len(targets))

    def copy(self, src, dst, to, send=None, recv=None):
        return pltpu.make_async_remote_copy(
            src_ref=src,
            dst_ref=dst,
            send_sem=self.sem() if send is None else send,
            recv_sem=self.sem() if recv is None else recv,
            device_id=to,
            device_id_type=MESH,
        )

    def send(self, src, dst, to):
        c = self.copy(src, dst, to)
        c.start()
        self.pending.append(c.wait_send)
        return c

    def keep(self, src, dst):
        c = pltpu.make_async_copy(src, dst, self.sem())
        c.start()
        self.pending.append(c.wait)
        return c

    def finish(self):
        for wait in self.pending:
            wait()
        self.pending = []


def wait_bytes(ref, sem):
    pltpu.make_async_copy(ref, ref, sem).wait()


class Gather:
    def __init__(self, net, full, shard, kinds, paired=False):
        self.net, self.full, self.shard, self.kinds, self.paired = net, full, shard, kinds, paired
        self.z_rows = (4 if paired else 2) * shard
        rounds = range(net.quads)
        self.z_got = [[net.sem() for _ in rounds[1:]] for _ in range(2)]
        self.x_got = [[net.sem() for _ in rounds[1:]] for _ in range(2)]
        self.z_sent = [net.sem(), net.sem()]
        self.x_own, self.x_sent, self.own, self.core_got, self.core_sent = [net.sem() for _ in range(5)]

    def rows(self, quad, x):
        at = (quad * 4 + 2 * x) * self.shard
        return self.full.at[pl.ds(pl.multiple_of(at, self.shard), 2 * self.shard)]

    def z_block(self, quad):
        if self.paired:
            return self.full.at[pl.ds(pl.multiple_of(quad * self.z_rows, self.z_rows), self.z_rows)]
        return self.rows(quad, self.net.x)

    def start(self):
        n = self.net
        mine = pl.ds(pl.multiple_of(n.me * self.shard, self.shard), self.shard)
        for arr, first, wide, into in self.kinds:
            half = arr.shape[1] // 2
            there = self.full.at[mine, pl.ds(into, wide)]

            def cut(core):
                return arr.at[:, pl.ds(pl.multiple_of(core * half + first, 128), wide)]

            pltpu.make_async_copy(cut(n.core), there, self.own).start()
            n.copy(cut(1 - n.core), there, n.other_core(), self.core_sent, self.core_got).start()

    def sides(self, r):
        n = self.net
        for side, way in enumerate((1, -1)):
            quad = n.quad - way * r
            near = n.quad + way
            last = n.quads - 1
            here = (quad >= 0) & (quad <= last)
            on = here & (near >= 0) & (near <= last)
            yield side, here, jnp.clip(quad, 0, last), on, jnp.clip(near, 0, last)

    def z(self, r):
        n = self.net
        if r == 0:
            if self.paired:
                wait_bytes(self.rows(n.quad, 1 - n.x), self.x_own)
            else:
                self.own_here()
        for side, here, quad, on, near in self.sides(r):
            if r > 0:

                @pl.when(here)
                def _():
                    wait_bytes(self.z_block(quad), self.z_got[side][r - 1])

            if r < n.quads - 1:

                @pl.when(on)
                def _():
                    block = self.z_block(quad)
                    n.copy(block, block, n.at(quad=near), self.z_sent[side], self.z_got[side][r]).start()

    def own_here(self):
        half = self.full.at[pl.ds(0, self.shard)]
        wait_bytes(half, self.own)
        wait_bytes(half, self.core_got)

    def x(self, r):
        n = self.net
        if r == 0:
            if self.paired:
                self.own_here()
            block = self.rows(n.quad, n.x)
            n.copy(block, block, n.other_x(), self.x_sent, self.x_own).start()
            return
        if self.paired:
            return
        for side, here, quad, on, near in self.sides(r):

            @pl.when(here)
            def _():
                block = self.rows(quad, n.x)
                n.copy(block, block, n.other_x(), self.x_sent, self.x_got[side][r - 1]).start()

    def arrived(self):
        n = self.net
        if self.paired:
            return
        wait_bytes(self.rows(n.quad, 1 - n.x), self.x_own)
        for r in range(1, n.quads):
            for side, here, quad, on, near in self.sides(r):

                @pl.when(here)
                def _():
                    wait_bytes(self.rows(quad, 1 - n.x), self.x_got[side][r - 1])

    def finish(self):
        n = self.net
        wait_bytes(self.full.at[pl.ds(0, self.shard)], self.core_sent)
        wait_bytes(self.full.at[pl.ds(0, 2 * (1 if self.paired else n.quads) * self.shard)], self.x_sent)
        for k in range(n.quads):

            @pl.when(n.quad == k)
            def _():
                for side, count in enumerate((k + 1, n.quads - k)):
                    if count < n.quads:
                        wait_bytes(self.full.at[pl.ds(0, count * self.z_rows)], self.z_sent[side])


class Scatter:
    def __init__(self, net, keep, send, x_land, z_land, loaded, added, slot):
        self.net, self.keep, self.send, self.x_land, self.z_land = net, keep, send, x_land, z_land
        self.loaded, self.added, self.slot = loaded, added, slot
        self.shard = keep.shape[0] // (2 * net.quads)
        self.stages = net.quads.bit_length() - 1
        self.own_waited = False
        self.z_got = [net.sem() for _ in range(self.stages)]
        self.z_sent = [net.sem() for _ in range(self.stages)]
        self.x_sent, self.x_got, self.own, self.tmp = [net.sem() for _ in range(4)]

    def start(self):
        n = self.net
        n.copy(self.send, self.x_land, n.other_x(), self.x_sent, self.x_got).start()

    def left(self, stage):
        return self.keep.shape[0] >> stage

    def landing(self, stage):
        rows = self.keep.shape[0]
        return self.z_land.at[pl.ds(rows - self.left(stage), self.left(stage + 1))]

    def last(self, far, core, count=1):
        at = self.keep.shape[0] + (2 * far + core) * self.shard
        at = at if isinstance(at, int) else pl.multiple_of(at, self.shard)
        return self.z_land.at[pl.ds(at, count * self.shard)]

    def total(self):
        return self.added.at[self.slot, :, pl.ds(0, self.keep.shape[1])]

    def add_in(self, rows):
        total, other = self.total(), self.loaded.at[:, pl.ds(0, self.keep.shape[1])]

        def one(i, carry):
            at = pl.ds(pl.multiple_of(i * 128, 128), 128)
            total[at, :] = (total[at, :].astype(F32) + other[at, :].astype(F32)).astype(BF16)
            return carry

        lax.fori_loop(0, rows // 128, one, 0)

    def add(self):
        first = pltpu.make_async_copy(self.keep, self.total(), self.tmp)
        first.start()
        wait_bytes(self.x_land, self.x_got)
        second = pltpu.make_async_copy(
            self.x_land, self.loaded.at[:, pl.ds(0, self.keep.shape[1])], self.own
        )
        second.start()
        first.wait()
        second.wait()
        self.add_in(self.keep.shape[0])
        self.send_half(0)

    def pass_on(self):
        for stage in range(1, self.stages):
            rows = self.left(stage)
            wait_bytes(self.landing(stage - 1), self.z_got[stage - 1])
            load = pltpu.make_async_copy(
                self.landing(stage - 1),
                self.loaded.at[pl.ds(0, rows), pl.ds(0, self.keep.shape[1])],
                self.tmp,
            )
            load.start()
            load.wait()
            self.add_in(rows)
            self.send_half(stage)

    def send_half(self, stage):
        n, total = self.net, self.total()
        quad = n.flipped(1 << stage)
        sent, got = self.z_sent[stage], self.z_got[stage]
        if stage < self.stages - 1:
            half = total.at[pl.ds(self.left(stage + 1), self.left(stage + 1))]
            n.copy(half, self.landing(stage), n.at(quad=quad), sent, got).start()
            return

        def rows(far, core):
            at = (2 * far + core) * self.shard
            at = at if isinstance(at, int) else pl.multiple_of(at, self.shard)
            return total.at[pl.ds(at, self.shard)]

        for c in range(2):
            n.copy(rows(1, c), self.last(1, n.core), n.at(quad=quad, core=c), sent, got).start()
        n.copy(rows(0, 1 - n.core), self.last(0, n.core), n.other_core(), sent, got).start()
        pltpu.make_async_copy(rows(0, n.core), self.last(0, n.core), self.own).start()

    def sent(self):
        wait_bytes(self.send, self.x_sent)
        for stage in range(self.stages - 1):
            wait_bytes(self.landing(stage), self.z_sent[stage])
        wait_bytes(self.last(0, 0, 3), self.z_sent[-1])
        self.own_done()

    def own_done(self):
        if not self.own_waited:
            wait_bytes(self.last(0, 0), self.own)
        self.own_waited = True

    def final(self, out, write):
        shard, cols = self.shard, self.keep.shape[1]
        wait_bytes(self.last(0, 0, 3), self.z_got[-1])
        self.own_done()
        got = self.loaded.at[pl.ds(0, 4 * shard), pl.ds(0, cols)]
        load = pltpu.make_async_copy(self.last(0, 0, 4), got, self.tmp)
        load.start()
        load.wait()
        for c in range(2):
            near, far = pl.ds(c * shard, shard), pl.ds((2 + c) * shard, shard)
            out[c, :, pl.ds(0, cols)] = got[near, :].astype(F32) + got[far, :].astype(F32)
        for c in range(2):
            for at, wide, dst, col in write(c):
                pltpu.make_async_copy(
                    out.at[c, :, pl.ds(at, wide)], dst.at[:, pl.ds(col, wide)], self.tmp
                ).start()
        wait_bytes(out.at[:, :, pl.ds(0, cols)], self.tmp)


def norm_back(values, gain, grad):
    scale = lax.rsqrt(jnp.mean(values * values, axis=-1, keepdims=True) + EPS)
    scaled = grad * gain
    inner = jnp.mean(scaled * values, axis=-1, keepdims=True)
    gain_part = jnp.sum(grad * values * scale, axis=0, keepdims=True)
    return scale * scaled - values * (scale * scale * scale * inner), gain_part


SLOTS = 3
MID = {0: 3, 1: 2, 2: 1}
PAIRED = (4, 5)
SCHEDULE = {
    "G": (
        ("z", 0, 0),
        ("z", 6, 0),
    ),
    "P0": (
        ("z", 3, 0),
        ("z", 1, 0),
        ("z", 0, 1),
    ),
    "P1": (
        ("x", 0, 0),
        ("z", 6, 1),
    ),
    "P1b": (
        ("x", 6, 1),
        ("x", 0, 1),
        ("z", 6, 2),
    ),
    "P2": (
        ("x", 5, 0),
    ),
    "P3": (
        ("x", 4, 0),
        ("z", 1, 1),
        ("x", 6, 0),
        ("z", 6, 3),
    ),
    "P3b": (
        ("x", 6, 3),
        ("x", 1, 1),
        ("x", 6, 2),
        ("z", 1, 2),
    ),
    "P4": (
        ("z", 1, 3),
        ("z", 0, 2),
        ("x", 0, 2),
    ),
    "P5": (
        ("z", 3, 1),
    ),
    "P6": (
        ("z", 0, 3),
        ("z", 2, 0),
    ),
    "P7": (
        ("x", 0, 3),
        ("x", 1, 0),
        ("z", 3, 2),
        ("z", 2, 1),
    ),
    "P8": (
        ("x", 2, 0),
        ("x", 3, 0),
        ("z", 2, 2),
        ("x", 1, 2),
        ("x", 1, 3),
        ("x", 2, 1),
    ),
    "P8b": (
        ("z", 4, 0),
        ("x", 3, 2),
        ("z", 4, 1),
        ("z", 2, 3),
    ),
    "P9": (
        ("x", 2, 3),
        ("z", 5, 0),
        ("x", 2, 2),
    ),
    "F0b": (
        ("z", 3, 3),
    ),
    "F1a": (
        ("x", 3, 3),
        ("x", 3, 1),
    ),
    "F1b": (
        ("z", 4, 2),
        ("s", 0),
    ),
    "F2a": (
        ("z", 5, 1),
    ),
    "F2b": (
        ("z", 5, 2),
    ),
    "F3a": (
        ("z", 4, 3),
        ("s", 1),
    ),
    "F4a": (
        ("z", 5, 3),
    ),
    "F5a": (
        ("a", 0),
        ("s", 2),
    ),
    "B0": (
        ("a", 1),
    ),
    "B1": (
        ("p", 0),
        ("s", 3),
    ),
    "B2": (
        ("a", 2),
    ),
    "B3": (
        ("p", 1),
        ("f", 0),
        ("s", 4),
        ("a", 3),
    ),
    "B4": (
        ("p", 2),
    ),
    "C2": (
        ("s", 5),
    ),
    "C1e": (
        ("s", 6),
    ),
    "C0": (
        ("a", 4),
    ),
    "D0": (
        ("p", 3),
        ("a", 5),
        ("f", 1),
    ),
    "D1": (
        ("f", 2),
    ),
    "D2": (
        ("p", 4),
        ("a", 6),
    ),
    "D3": (
        ("p", 5),
        ("f", 3),
        ("a", 7),
        ("f", 4),
    ),
    "D4": (
        ("p", 6),
        ("p", 7),
        ("a", 8),
    ),
    "D5": (
        ("p", 8),
        ("f", 5),
        ("f", 6),
        ("f", 7),
        ("f", 8),
    ),
}


def layer_kernel(*refs):
    (
        tokens,
        out_grad,
        attn_gain,
        mlp_gain,
        q_gain,
        k_gain,
        cosine,
        sine,
        start_in,
        start_row,
        wq,
        wk,
        wv,
        wo,
        wg,
        wu,
        wd,
        output,
        input_grad,
        gain_out,
        g_q,
        g_k,
        g_v,
        g_o,
        g_gate,
        g_up,
        g_down,
        qkv_full,
        o_full,
        ff_full,
        grad_full,
        first_t,
        proj_s,
        plane_s,
        k_s,
        v_s,
        heads_s,
        stat_s,
        middle_s,
        ff_keep,
        ff_send,
        ff_xland,
        ff_zland,
        at_keep,
        at_send,
        at_xland,
        at_zland,
        core_land,
        low_land,
        mlp_own,
        mlp_low,
        da_land,
        heads_land,
        kv_land,
        back_land,
        sems,
        xa,
        sa,
        ta,
        tb,
        attn,
        loaded,
        added,
        summed,
        low_send,
        gains,
        gains_land,
    ) = refs
    n = Net(sems)
    rows, width = tokens.shape
    d = q_gain.shape[1]
    shard = wq.shape[0]
    block = 2 * shard
    quads = n.quads
    tiles, _, ff_cols = ff_keep.shape
    ft = ff_cols // 3
    half_ff = tiles * ft
    top = kv_land.shape[0]
    step, tall = 128, 256
    steps = rows // step
    my_at = pl.multiple_of(n.core * rows, rows)
    their_at = pl.multiple_of((1 - n.core) * rows, rows)
    my_rows = pl.ds(my_at, rows)
    my_chip = pl.ds(pl.multiple_of(n.x * 2 * rows, 2 * rows), 2 * rows)
    other_chip = pl.ds(pl.multiple_of((1 - n.x) * 2 * rows, 2 * rows), 2 * rows)
    scale = 1.0 / math.sqrt(d)
    bf = lambda *shape: pltpu.VMEM(shape, BF16)
    f32 = lambda *shape: pltpu.VMEM(shape, F32)

    def load(pairs):
        copies = [pltpu.make_async_copy(s, t, n.sem()) for s, t in pairs]
        for c in copies:
            c.start()
        return copies

    def load_now(pairs):
        for c in load(pairs):
            c.wait()

    def loop(count, fn):
        def body(i, carry):
            fn(i)
            return carry

        lax.fori_loop(0, count, body, 0)

    def part(i, size):
        return pl.ds(pl.multiple_of(i * size, size), size)

    n.greet()

    qkv = Gather(n, qkv_full, shard, [(wq, 0, 4 * d, 0), (wk, 0, 2 * d, 4 * d), (wv, 0, 2 * d, 6 * d)])
    o_w = Gather(n, o_full, shard, [(wo, 0, 4 * d, 0)])
    ffw = [
        Gather(
            n,
            ff_full.at[f],
            shard,
            [(arr, f * ft, ft, kind * ft) for kind, arr in enumerate((wg, wu, wd))],
            paired=f in PAIRED,
        )
        for f in range(tiles)
    ]
    ff = [
        Scatter(n, ff_keep.at[f], ff_send.at[f], ff_xland.at[f], ff_zland.at[f], loaded, added, f % SLOTS)
        for f in range(tiles)
    ]
    at_groups = [
        Scatter(n, at_keep.at[f], at_send.at[f], at_xland.at[f], at_zland.at[f], loaded, added, (tiles + f) % SLOTS)
        for f in range(3)
    ]

    def ff_write(f):
        def places(c):
            col = c * half_ff + f * ft
            return [(k * ft, ft, dst, col) for k, dst in enumerate((g_gate, g_up, g_down))]

        return places

    def simple(places):
        return lambda c: [(at, wide, dst, c * wide) for at, wide, dst in places]

    groups = ffw + [o_w]
    sums = ff + at_groups
    writes = [ff_write(f) for f in range(tiles)] + [
        simple([(0, 4 * d, g_o)]),
        simple([(0, 4 * d, g_q)]),
        simple([(0, 2 * d, g_k), (2 * d, 2 * d, g_v)]),
    ]
    planned = 1 + max(step[2] for steps_at in SCHEDULE.values() for step in steps_at if step[0] in "zx")

    def tick(name):
        for what, g, *r in SCHEDULE.get(name, ()):
            if what in "zx":
                if r[0] < quads:
                    getattr(groups[g], what)(r[0])
            elif what == "s":
                sums[g].start()
            elif what == "a":
                if g >= SLOTS:
                    sums[g - SLOTS].sent()
                sums[g].add()
            elif what == "p":
                sums[g].pass_on()
            else:
                sums[g].final(summed, writes[g])

    def need(g):
        for r in range(planned, quads):
            groups[g].z(r)
            groups[g].x(r)
        groups[g].arrived()

    def tick_within(h, sweeps, name):
        flags = [s.own_waited for s in sums]
        pl.when(n.quad >= h)(lambda: sweeps(lambda: tick(name)))
        for s, flag in zip(sums, flags):
            s.own_waited = flag
        pl.when(n.quad < h)(lambda: tick(name))

    plane = ta.at[:, pl.ds(0, 4 * d)]
    keys = [tb.at[:, pl.ds(h * d, d)] for h in range(top + 1)]
    vals = [ta.at[:, pl.ds(4 * d, 2 * d)], ta.at[:, pl.ds(6 * d, 2 * d)], tb.at[:, pl.ds(3 * d, 2 * d)]]
    ones = [ta.at[:, pl.ds(5 * d, d)], ta.at[:, pl.ds(7 * d, d)], tb.at[:, pl.ds(4 * d, d)]]

    def core_then_tensor(product, sending, k, tmp_low):
        core_copies, low_copies = [], []
        for i in range(rows // tall):
            at = pl.ds(i * tall, tall)
            sending[at, :] = product(pl.ds(their_at + i * tall, tall)).astype(BF16)
            core_copies.append(n.send(sending.at[at], core_land.at[k, at], n.other_core()))
        for i in range(rows // tall):
            got = product(pl.ds(my_at + i * tall, tall))
            core_copies[i].wait_recv()
            for p in range(tall // step):
                at = pl.ds(i * tall + p * step, step)
                load_now([(core_land.at[k, at], tmp_low.at[0])])
                low_send[at, :] = (got[p * step : (p + 1) * step] + tmp_low[0].astype(F32)).astype(BF16)
                low_copies.append(n.send(low_send.at[at], low_land.at[k, at], n.other_tensor()))
        return low_copies

    def forward(w_qkv, proj, low, acc, heads, stat, w_o, core_send, tmp, tmp_low, start_col):
        qkv.start()
        o_w.start()
        qkv.z(0)
        qkv.x(0)
        for g in ffw:
            g.start()

        def norm_first(i):
            load_tok = pltpu.make_async_copy(tokens.at[part(i, step)], tmp_low.at[0], tok_sem)
            load_tok.start()
            load_tok.wait()
            to = pl.ds(pl.multiple_of(n.core * rows + i * step, step), step)
            xa[to, :] = rms_rows(tmp_low[0].astype(F32), attn_gain[...]).astype(BF16)

        tok_sem = n.sem()
        loop(steps, norm_first)
        first_copy = n.send(xa.at[my_rows], xa.at[my_rows], n.other_core())
        for r in range(1, quads):
            qkv.z(r)
            qkv.x(r)
        tick("G")
        grad_copy = n.send(out_grad, grad_full.at[my_rows], n.other_core())
        grad_keep = n.keep(out_grad, grad_full.at[my_rows])
        start_load = load([(start_in, start_col)])
        for o in ones:
            o[...] = jnp.ones((4 * rows, d), BF16)
        acc[...] = jnp.zeros_like(acc)
        first_copy.wait_recv()
        qkv.arrived()
        load_now([(qkv_full, w_qkv)])

        def project(i):
            at = part(i, tall)
            proj[at, :] = dot(xa[at, :], w_qkv[...])
            cos, sin = cosine[at, :], sine[at, :]

            def prep(col, gain):
                u = rms_rows(proj[at, pl.ds(col, d)], gain[...])
                return (u * cos + pltpu.roll(u, d // 2, 1) * sin).astype(BF16)

            for h in range(2):
                for g in range(2):
                    low[h, at, pl.ds(g * d, d)] = prep((2 * h + g) * d, q_gain)
                low[h, at, pl.ds(2 * d, d)] = prep((4 + h) * d, k_gain)
                low[h, at, pl.ds(3 * d, d)] = proj[at, pl.ds((6 + h) * d, d)].astype(BF16)

        loop(2 * rows // tall, project)
        head_copy = n.copy(low.at[1 - n.x], plane.at[my_chip], n.other_x())
        head_copy.start()
        n.keep(proj, proj_s)
        plane[my_chip, :] = low[n.x]
        tick("P0")

        def flip_first(i):
            at = part(i, tall)
            w_qkv[at, :] = xa[:, at].T

        loop(width // tall, flip_first)
        n.keep(w_qkv, first_t)
        head_copy.wait()
        keys[0][...] = plane[:, pl.ds(2 * d, d)]
        vals[0][:, pl.ds(0, d)] = plane[:, pl.ds(3 * d, d)]

        ahead = n.at(quad=jnp.minimum(n.quad + 1, quads - 1))
        hops = [
            [
                n.copy(keys[h], keys[h + 1], ahead),
                n.copy(vals[h].at[:, pl.ds(0, d)], vals[h + 1].at[:, pl.ds(0, d)], ahead),
            ]
            for h in range(top)
        ]

        def hop_start(h):
            @pl.when((n.quad >= h) & (n.quad < quads - 1))
            def _():
                for c in hops[h]:
                    c.start()

        def hop_sent(h):
            @pl.when((n.quad >= h) & (n.quad < quads - 1))
            def _():
                for c in hops[h]:
                    c.wait_send()

        def hop_arrived(h):
            @pl.when(n.quad >= h + 1)
            def _():
                for c in hops[h]:
                    c.wait_recv()

        def attend(h, i, j):
            q_at, k_at = part(i, rows), part(j, rows)
            q2 = jnp.concatenate([plane[q_at, pl.ds(0, d)], plane[q_at, pl.ds(d, d)]], axis=0)
            prob = jnp.exp2(dot(q2, keys[h][k_at, :], NT) * (scale * LOG2E))
            k_pos = (4 * (n.quad - h) + j) * rows + lax.broadcasted_iota(jnp.int32, (rows, rows), 1)
            keep = k_pos >= start_col[q_at, :]
            if h == 0:
                q_pos = (4 * n.quad + i) * rows + lax.broadcasted_iota(jnp.int32, (rows, rows), 0)
                keep = keep & (k_pos <= q_pos)
            prob = jnp.where(jnp.concatenate([keep, keep], axis=0), prob, 0.0)
            acc[i] += dot(prob.astype(BF16), vals[h][k_at, :])

        def sweep(h, lo, hi, mid):
            def over_i(i, carry):
                pl.when(i == MID[h])(mid)

                def over_j(j, inner):
                    attend(h, i, j)
                    return inner

                lax.fori_loop(lo(i), hi(i), over_j, 0)
                return carry

            lax.fori_loop(0, 4, over_i, 0)

        start_load[0].wait()
        hop_start(0)
        tick("P1")
        sweep(0, *ranges[0], lambda: tick("P1b"))
        tick("P2")
        hop_arrived(0)
        hop_start(1)
        tick("P3")

        tick_within(1, lambda mid: sweep(1, *ranges[1], mid), "P3b")

        tick("P4")
        need(tiles)
        load_o = load([(o_full, w_o)])
        saves = load([(plane, plane_s)])
        hop_arrived(1)
        tick("P5")

        @pl.when(n.quad >= 2)
        def _():
            sweep(2, *ranges[2], lambda: None)

        for i in range(4):
            at = pl.ds(i * rows, rows)
            total = acc[i, :, d:]
            done = acc[i, :, :d] / total
            heads[at, pl.ds(0, d)] = done[:rows]
            heads[at, pl.ds(d, d)] = done[rows:]
            logs = jnp.log2(total)
            stat[0:1, at] = logs[:rows].T[0:1]
            stat[1:2, at] = logs[rows:].T[0:1]
        low[0, :, pl.ds(0, 2 * d)] = heads[other_chip, :].astype(BF16)
        attn_copy = n.send(low.at[0, :, pl.ds(0, 2 * d)], attn.at[n.x], n.other_x())
        tick("P6")
        attn[n.x] = heads[my_chip, :].astype(BF16)
        n.keep(heads, heads_s)
        n.keep(stat, stat_s)
        for h in range(top + 1):
            at = pl.ds(h * 4 * rows, 4 * rows)
            saves += load([(keys[h], k_s.at[at]), (vals[h].at[:, pl.ds(0, d)], v_s.at[at])])
        for h in range(top):
            hop_sent(h)
        grad_copy.wait_recv()
        grad_keep.wait()
        n.pending.remove(grad_keep.wait)
        first_copy.wait_send()
        n.pending.remove(first_copy.wait_send)
        g_load = load([(grad_full, xa)])
        for c in load_o + saves:
            c.wait()
        attn_copy.wait_recv()
        tick("P7")

        def o_rows(at):
            return dot(attn[0, at, :], w_o[:, : 2 * d], NT) + dot(attn[1, at, :], w_o[:, 2 * d :], NT)

        second_copies = []
        low_copies = core_then_tensor(o_rows, core_send, 3, tmp_low)
        tick("P8")
        for c in g_load:
            c.wait()

        def flip_grad(i):
            at = part(i, tall)
            tb[at, :] = xa[:, at].T

        loop(width // tall, flip_grad)
        tick("P8b")
        for i in range(steps):
            at = pl.ds(i * step, step)
            low_copies[i].wait_recv()
            load_now([(low_land.at[3, at], tmp_low.at[0]), (tokens.at[at], tmp_low.at[1])])
            mid = tmp_low[1].astype(F32) + (low_send[at, :].astype(F32) + tmp_low[0].astype(F32))
            tmp[...] = mid
            mid_copy = load([(tmp, middle_s.at[at])])
            to = pl.ds(my_at + i * step, step)
            sa[to, :] = rms_rows(mid, mlp_gain[...]).astype(BF16)
            second_copies.append(n.send(sa.at[to], sa.at[to], n.other_core()))
            ta[:, to] = sa[to, :].T
            mid_copy[0].wait()
        for i in range(steps):
            second_copies[i].wait_recv()
            to = pl.ds(their_at + i * step, step)
            ta[:, to] = sa[to, :].T
        tick("P9")
        n.finish()

    ranges = {
        0: (lambda i: 0, lambda i: i + 1),
        1: (lambda i: 0, lambda i: 4),
        2: (lambda i: i, lambda i: 4),
    }
    pl.run_scoped(
        forward,
        bf(width, 8 * d),
        f32(2 * rows, 8 * d),
        bf(2, 2 * rows, 4 * d),
        f32(4, 2 * rows, 2 * d),
        f32(4 * rows, 2 * d),
        f32(2, 4 * rows),
        bf(width, 4 * d),
        bf(rows, width),
        f32(step, width),
        bf(2, step, width),
        pltpu.VMEM((4 * rows, 1), jnp.int32),
    )

    def row_block(xr, s):
        bits = quads.bit_length() - 1
        quad = n.flipped(sum(((s >> b) & 1) << (bits - 1 - b) for b in range(bits)))
        x = n.x if xr == 0 else 1 - n.x
        return pl.multiple_of((quad * 4 + 2 * x) * shard, block)

    low_sent = [n.sem() for _ in range(steps)]
    low_got = [n.sem() for _ in range(steps)]

    def feed_forward(w, mlp, ds, acts, stage, w_sem, stage_sem):
        def fetch(f, slot):
            pltpu.make_async_copy(ff_full.at[f], w.at[slot], w_sem.at[slot]).start()

        tick("F0a")
        need(0)
        fetch(0, 0)
        mlp[...] = jnp.zeros_like(mlp)
        ds[...] = jnp.zeros_like(ds)

        def staged(f):
            for k, dst in enumerate((ff_keep, ff_send)):
                yield pltpu.make_async_copy(stage.at[k], dst.at[f], stage_sem.at[k])

        def at_tile(f, k, fn):
            pl.when(f == k)(fn)

        def tile(f, carry):
            slot = lax.rem(f, 2)

            def before(c):
                if c > 0:
                    tick("F%da" % c)
                if c + 1 < tiles:
                    need(c + 1)

            for c in range(tiles):
                at_tile(f, c, partial(before, c))

            @pl.when(f + 1 < tiles)
            def _():
                fetch(f + 1, 1 - slot)

            wait_bytes(w.at[slot], w_sem.at[slot])

            def some_rows(i):
                at = part(i, rows)
                gate = dot(sa[at, :], w[slot, :, pl.ds(0, ft)])
                up = dot(sa[at, :], w[slot, :, pl.ds(ft, ft)])
                d_act = dot(xa[at, :], w[slot, :, pl.ds(2 * ft, ft)])
                sig = 1.0 / (1.0 + jnp.exp(-gate))
                silu = gate * sig
                acts[at, pl.ds(2 * ft, ft)] = (silu * up).astype(BF16)
                acts[at, pl.ds(0, ft)] = (d_act * up * sig * (1.0 + gate * (1.0 - sig))).astype(BF16)
                acts[at, pl.ds(ft, ft)] = (d_act * silu).astype(BF16)
                mlp[at, :] += dot(acts[at, pl.ds(2 * ft, ft)], w[slot, :, pl.ds(2 * ft, ft)], NT)
                ds[at, :] += dot(acts[at, pl.ds(0, ft)], w[slot, :, pl.ds(0, ft)], NT) + dot(
                    acts[at, pl.ds(ft, ft)], w[slot, :, pl.ds(ft, ft)], NT
                )

            loop(2, some_rows)

            @pl.when(f >= 1)
            def _():
                for c in staged(f - 1):
                    c.wait()

            for c in range(tiles):
                at_tile(f, c, partial(tick, "F%db" % c))
            for xr in range(2):
                for q in range(quads):
                    at = pl.ds(row_block(xr, q), block)
                    to = pl.ds(q * block, block)
                    stage[xr, to, pl.ds(0, 2 * ft)] = dot(ta[at, :], acts[:, pl.ds(0, 2 * ft)]).astype(BF16)
                    stage[xr, to, pl.ds(2 * ft, ft)] = dot(tb[at, :], acts[:, pl.ds(2 * ft, ft)]).astype(BF16)
            for c in staged(f):
                c.start()

            return carry

        lax.fori_loop(0, tiles, tile, 0)
        core_copies = []
        for i in range(steps):
            at = pl.ds(i * step, step)
            xa[at, :] = ds[pl.ds(their_at + i * step, step), :].astype(BF16)
            core_copies.append(n.copy(xa.at[at], core_land.at[0, at], n.other_core()))
            core_copies[-1].start()
        for c in staged(tiles - 1):
            c.wait()
        for i in range(steps):
            at = pl.ds(i * step, step)
            core_copies[i].wait_recv()
            spare = xa.at[pl.ds(rows + i * step, step)]
            load_now([(core_land.at[0, at], spare)])
            low_send[at, :] = (ds[pl.ds(my_at + i * step, step), :] + spare[...].astype(F32)).astype(BF16)
            n.copy(
                low_send.at[at], low_land.at[0, at], n.other_tensor(), low_sent[i], low_got[i]
            ).start()

        tick("B0")
        def to_low(i):
            at = part(i, step)
            sa[at, :] = mlp[at, :].astype(BF16)

        loop(2 * rows // step, to_low)
        mlp_copy = n.copy(sa.at[pl.ds(their_at, rows)], core_land.at[1], n.other_core())
        mlp_copy.start()
        mlp_keep = load([(sa.at[my_rows], mlp_own)])
        for c in core_copies:
            c.wait_send()
        mlp_copy.wait()
        mlp_keep[0].wait()

    pl.run_scoped(
        feed_forward,
        bf(2, width, ff_cols),
        f32(2 * rows, width),
        f32(2 * rows, width),
        bf(2 * rows, ff_cols),
        bf(2, 2 * rows, ff_cols),
        pltpu.SemaphoreType.DMA((2,)),
        pltpu.SemaphoreType.DMA((2,)),
    )

    def backward(
        d_middle, tmp, tmp_low, vx, heads, stat, d_out, d_q, d_kv, kv_low, d_low, d_proj
    ):
        loads = load(
            [(o_full, ta.at[:, pl.ds(0, 4 * d)]), (plane_s, tb.at[:, pl.ds(0, 4 * d)]), (v_s, vx), (heads_s, heads)]
            + [(stat_s, stat.at[pl.ds(0, 2)])]
            + [
                (k_s.at[pl.ds(h * 4 * rows, 4 * rows)], tb.at[:, pl.ds((4 + h) * d, d)])
                for h in range(top + 1)
            ]
        )
        early = load([(middle_s, d_middle), (out_grad, xa.at[my_rows])])
        gains[...] = jnp.zeros_like(gains)

        tick("B1")
        for i in range(steps):
            at = pl.ds(i * step, step)
            load_now([(mlp_own.at[at], tmp_low.at[0]), (core_land.at[1, at], tmp_low.at[1])])
            tmp_low[0] = (tmp_low[0].astype(F32) + tmp_low[1].astype(F32)).astype(BF16)
            load_now([(tmp_low.at[0], mlp_low.at[at])])

        tick("B2")
        for c in early:
            c.wait()
        da_copies = []
        for i in range(steps):
            at = pl.ds(i * step, step)
            to = pl.ds(my_at + i * step, step)
            wait_bytes(low_land.at[0, at], low_got[i])
            load_now([(low_land.at[0, at], tmp_low.at[0])])
            d_second = low_send[at, :].astype(F32) + tmp_low[0].astype(F32)
            back, gain_part = norm_back(d_middle[at, :], mlp_gain[...], d_second)
            gains[1:2, :] += gain_part
            d_mid = xa[to, :].astype(F32) + back
            d_middle[at, :] = d_mid
            xa[to, :] = d_mid.astype(BF16)
            da_copies.append(n.copy(xa.at[to], da_land.at[at], n.other_core()))
            da_copies[-1].start()
        mlp_copy = n.send(mlp_low, low_land.at[1], n.other_tensor())
        for i in range(steps):
            wait_bytes(low_send.at[pl.ds(i * step, step)], low_sent[i])
        for c in loads:
            c.wait()
        for c in da_copies:
            c.wait()
        load_now([(da_land, xa.at[pl.ds(their_at, rows)])])

        def head_grads(i):
            at = part(i, tall)
            got = dot(xa[at, :], ta[:, pl.ds(0, 4 * d)]).astype(BF16)
            d_low[0, at, pl.ds(0, 2 * d)] = got[:, : 2 * d]
            d_low[1, at, pl.ds(0, 2 * d)] = got[:, 2 * d :]

        loop(2 * rows // tall, head_grads)
        heads_copy = n.copy(d_low.at[1 - n.x, :, pl.ds(0, 2 * d)], heads_land, n.other_x())
        heads_copy.start()
        tick("B3")
        d_out[my_chip, :] = d_low[n.x, :, pl.ds(0, 2 * d)]
        d_q[...] = jnp.zeros_like(d_q)

        def flip(i):
            at = part(i, tall)
            ta[at, :] = xa[:, at].T

        loop(width // tall, flip)

        def weight_pieces(right, k):
            for xr in range(2):
                for q in range(quads):
                    sa[pl.ds(q * block, block), pl.ds((2 * k + xr) * 4 * d, 4 * d)] = dot(
                        ta[pl.ds(row_block(xr, q), block), :], right
                    ).astype(BF16)

        def stage_out(k, g):
            return load(
                [
                    (sa.at[:, pl.ds((2 * k + xr) * 4 * d, 4 * d)], dst.at[g])
                    for xr, dst in enumerate((at_keep, at_send))
                ]
            )

        weight_pieces(jnp.concatenate([attn[0], attn[1]], axis=1), 0)
        o_stage = stage_out(0, 0)
        heads_copy.wait()
        load_now([(heads_land, d_out.at[other_chip])])
        for c in o_stage:
            c.wait()
        tick("B4")

        for g in range(2):
            for i in range(4):
                at = pl.ds(i * rows, rows)
                cols = pl.ds(g * d, d)
                prod = d_out[at, cols].astype(F32) * heads[at, cols]
                stat[2 + g : 3 + g, at] = jnp.sum(prod.T, axis=0, keepdims=True)
        q_proj = load(
            [
                (proj_s.at[:, pl.ds(h * 2 * d, 2 * d)], heads.at[pl.ds(h * 2 * rows, 2 * rows)])
                for h in range(2)
            ]
        )

        def attend_back(h, i, j):
            q_at, k_at = part(i, rows), part(j, rows)
            q2 = jnp.concatenate([tb[q_at, pl.ds(0, d)], tb[q_at, pl.ds(d, d)]], axis=0)
            g2 = jnp.concatenate([d_out[q_at, pl.ds(0, d)], d_out[q_at, pl.ds(d, d)]], axis=0)
            log_total = jnp.concatenate([stat[0:1, q_at], stat[1:2, q_at]], axis=1)
            row_dot = jnp.concatenate([stat[2:3, q_at], stat[3:4, q_at]], axis=1)
            k_now = tb[k_at, pl.ds((4 + h) * d, d)]
            v_now = vx[pl.ds(pl.multiple_of(h * 4 * rows + j * rows, rows), rows), :]
            prob = jnp.exp2(dot(k_now, q2, NT) * (scale * LOG2E) - log_total)
            k_pos = (4 * (n.quad - h) + j) * rows + lax.broadcasted_iota(jnp.int32, (rows, rows), 0)
            keep = k_pos >= start_row[:, q_at]
            if h == 0:
                q_pos = (4 * n.quad + i) * rows + lax.broadcasted_iota(jnp.int32, (rows, rows), 1)
                keep = keep & (k_pos <= q_pos)
            prob = jnp.where(jnp.concatenate([keep, keep], axis=1), prob, 0.0)
            d_prob = dot(v_now, g2, NT)
            d_score = (prob * (d_prob - row_dot)).astype(BF16)
            d_kv[k_at, pl.ds(d, d)] += dot(prob.astype(BF16), g2)
            d_kv[k_at, pl.ds(0, d)] += dot(d_score, q2)
            got = dot(d_score, k_now, TN)
            d_q[q_at, pl.ds(0, d)] += got[:rows]
            d_q[q_at, pl.ds(d, d)] += got[rows:]

        def plane_back(h, lo, hi, mid):
            d_kv[...] = jnp.zeros_like(d_kv)

            def over_i(i, carry):
                pl.when(i == MID[h])(mid)

                def over_j(j, inner):
                    attend_back(h, i, j)
                    return inner

                lax.fori_loop(lo(i), hi(i), over_j, 0)
                return carry

            lax.fori_loop(0, 4, over_i, 0)
            d_kv[:, pl.ds(0, d)] = d_kv[:, pl.ds(0, d)] * scale

        behind = n.at(quad=jnp.maximum(n.quad - 1, 0))
        hops = [n.copy(kv_low.at[k], kv_land.at[k], behind) for k in range(top)]
        kv_sem = n.sem()

        def add_landed(k):
            hops[k].wait_recv()
            for p in range(2):
                at = pl.ds(p * 2 * rows, 2 * rows)
                c = pltpu.make_async_copy(kv_land.at[k, at], d_low.at[p, :, pl.ds(2 * d, 2 * d)], kv_sem)
                c.start()
                c.wait()
                d_kv[at, :] += d_low[p, :, pl.ds(2 * d, 2 * d)].astype(F32)

        for h in range(top, 0, -1):

            def one_plane(mid, h=h):
                plane_back(h, *ranges[h], mid)
                if h < top:

                    @pl.when(n.quad < quads - 1)
                    def _():
                        add_landed(top - h - 1)

                kv_low[top - h] = d_kv[...].astype(BF16)
                hops[top - h].start()

            tick_within(h, one_plane, "C%d" % h)
            tick("C%de" % h)
        plane_back(0, *ranges[0], lambda: tick("C0"))

        def put_back(x, first, source, factor):
            def body(i):
                at = part(i, tall)
                src = pl.ds(pl.multiple_of(x * 2 * rows + i * tall, tall), tall)
                d_low[x, at, pl.ds(first, 2 * d)] = (source[src, :] * factor).astype(BF16)

            loop(2 * rows // tall, body)

        q_cols, kv_cols = pl.ds(0, 2 * d), pl.ds(2 * d, 2 * d)
        put_back(1 - n.x, 0, d_q, scale)
        q_back = n.copy(d_low.at[1 - n.x, :, q_cols], back_land.at[:, q_cols], n.other_x())
        q_back.start()
        put_back(n.x, 0, d_q, scale)
        k_proj = load([(proj_s.at[:, pl.ds(4 * d, 2 * d)], d_q.at[pl.ds(0, 2 * rows)])])
        late = load([(first_t, ta), (qkv_full, tb)])

        tick("D0")
        @pl.when(n.quad < quads - 1)
        def _():
            add_landed(top - 1)

        put_back(1 - n.x, 2 * d, d_kv, 1.0)
        kv_back = n.copy(d_low.at[1 - n.x, :, kv_cols], back_land.at[:, kv_cols], n.other_x())
        kv_back.start()
        put_back(n.x, 2 * d, d_kv, 1.0)
        tick("D1")
        q_back.wait()
        load_now([(back_land.at[:, q_cols], d_low.at[1 - n.x, :, q_cols])])

        def prep_back(cols):
            def body(i):
                at = part(i, tall)
                cos, sin = cosine[at, :], sine[at, :]
                for col, h, src, gain, row, read in cols:
                    grad = d_low[h, at, pl.ds(src, d)]
                    if gain is not None:
                        grad = grad.astype(F32)
                        grad = grad * cos + pltpu.roll(grad * sin, d // 2, 1)
                        grad, gain_part = norm_back(read(i), gain[...], grad)
                        gains[pl.ds(row, 1), pl.ds(0, d)] += gain_part
                    d_proj[at, pl.ds(col, d)] = grad.astype(BF16)

            loop(2 * rows // tall, body)

        def q_read(h, g):
            return lambda i: heads[
                pl.ds(pl.multiple_of(h * 2 * rows + i * tall, tall), tall), pl.ds(g * d, d)
            ]

        def k_read(h):
            return lambda i: d_q[part(i, tall), pl.ds(h * d, d)]

        for c in q_proj:
            c.wait()
        prep_back(
            [
                ((2 * h + g) * d, h, g * d, q_gain, 2, q_read(h, g))
                for h in range(2)
                for g in range(2)
            ]
        )
        for c in late:
            c.wait()
        weight_pieces(d_proj[:, pl.ds(0, 4 * d)], 0)
        for c in stage_out(0, 1):
            c.wait()
        at_groups[1].start()
        tick("D2")
        kv_back.wait()
        load_now([(back_land.at[:, kv_cols], d_low.at[1 - n.x, :, kv_cols])])
        for c in k_proj:
            c.wait()
        prep_back(
            [((4 + h) * d, h, 2 * d, k_gain, 3, k_read(h)) for h in range(2)]
            + [((6 + h) * d, h, 3 * d, None, None, None) for h in range(2)]
        )

        low_copies = core_then_tensor(
            lambda at: dot(d_proj[at, :], tb[...], NT), xa.at[pl.ds(0, rows)], 2, tmp_low
        )

        weight_pieces(d_proj[:, pl.ds(4 * d, 4 * d)], 1)
        for c in stage_out(1, 2):
            c.wait()
        at_groups[2].start()
        tick("D3")

        mlp_copy.wait_recv()
        for i in range(steps):
            at = pl.ds(i * step, step)
            load_now(
                [
                    (low_land.at[1, at], tmp_low.at[0]),
                    (mlp_low.at[at], tmp_low.at[1]),
                    (middle_s.at[at], tmp),
                ]
            )
            tmp_low[0] = (tmp[...] + (tmp_low[1].astype(F32) + tmp_low[0].astype(F32))).astype(BF16)
            load_now([(tmp_low.at[0], output.at[at])])
        tick("D4")
        for i in range(steps):
            at = pl.ds(i * step, step)
            low_copies[i].wait_recv()
            load_now([(low_land.at[2, at], tmp_low.at[0]), (tokens.at[at], tmp_low.at[1])])
            d_first = low_send[at, :].astype(F32) + tmp_low[0].astype(F32)
            back, gain_part = norm_back(tmp_low[1].astype(F32), attn_gain[...], d_first)
            gains[0:1, :] += gain_part
            d_middle[at, :] = d_middle[at, :] + back
            n.keep(d_middle.at[at], input_grad.at[at])

        for k, to in enumerate((n.other_core(), n.other_x(), n.other_tensor())):
            c = n.copy(gains, gains_land.at[k], to)
            c.start()
            c.wait()
            if k < 2:
                gains[...] += gains_land[k]
            else:
                gains[2:4, :] += gains_land[k, 2:4, :]
        gains_land[3 + n.quad] = gains[...]
        quad_copies = []
        for s in range(1, quads):
            to = n.at(quad=lax.rem(n.quad + s, quads))
            quad_copies.append(n.copy(gains, gains_land.at[3 + n.quad], to))
            quad_copies[-1].start()
        for c in quad_copies:
            c.wait()
        total = gains_land[3]
        for k in range(1, quads):
            total = total + gains_land[3 + k]
        gains[...] = total
        n.keep(gains, gain_out)
        tick("D5")
        for g in (ff + at_groups)[-SLOTS:]:
            g.sent()
        for k in range(top):

            @pl.when(n.quad >= top - k)
            def _(k=k):
                hops[k].wait_send()

        n.finish()
        for g in [qkv, o_w] + ffw:
            g.finish()
        assert n.used <= sems.shape[0], n.used


    pl.run_scoped(
        backward,
        f32(rows, width),
        f32(step, width),
        bf(2, step, width),
        bf(4 * rows * (top + 1), d),
        f32(4 * rows, 2 * d),
        f32(4, 4 * rows),
        bf(4 * rows, 2 * d),
        f32(4 * rows, 2 * d),
        f32(4 * rows, 2 * d),
        bf(top, 4 * rows, 2 * d),
        bf(2, 2 * rows, 4 * d),
        bf(2 * rows, 8 * d),
    )


def whole_layer(tokens, out_grad, attn_gain, mlp_gain, q_gain, k_gain, *arrays):
    rows, width = tokens.shape
    d = q_gain.shape[0]
    wg = arrays[-1]
    shard = wg.shape[0]
    quads = lax.axis_size("dp") // 4
    tiles, half_ff = 6, wg.shape[1] // 2
    cols = 3 * half_ff // tiles
    top = REACH // 4
    widest = max(cols, 4 * d)
    assert top == 2 and width == 4 * rows and 2 * rows == 8 * d
    vmem = pl.BlockSpec(memory_space=pltpu.VMEM)
    hbm = pl.BlockSpec(memory_space=pl.ANY)

    def bf(*shape):
        return jax.ShapeDtypeStruct(shape, BF16)

    def f32(*shape):
        return jax.ShapeDtypeStruct(shape, F32)

    out_shape = [bf(rows, width), f32(rows, width), f32(4, width)]
    out_shape += [f32(shard, 8 * d), f32(shard, 4 * d), f32(shard, 4 * d), f32(shard, 8 * d)]
    out_shape += [f32(shard, 2 * half_ff)] * 3
    out_shape += [bf(width, 8 * d), bf(width, 4 * d), bf(tiles, width, cols)]
    out_shape += [bf(2 * rows, width), bf(width, 2 * rows), f32(2 * rows, 8 * d), bf(4 * rows, 4 * d)]
    out_shape += [bf(4 * rows * (top + 1), d)] * 2
    out_shape += [f32(4 * rows, 2 * d), f32(2, 4 * rows), f32(rows, width)]
    out_shape += [bf(tiles, width // 2, cols)] * 3 + [bf(tiles, width // 2 + 4 * shard, cols)]
    out_shape += [bf(3, width // 2, 4 * d)] * 3 + [bf(3, width // 2 + 4 * shard, 4 * d)]
    out_shape += [bf(4, rows, width)] * 2
    out_shape += [bf(rows, width)] * 3
    out_shape += [bf(2 * rows, 2 * d), bf(top, 4 * rows, 2 * d), bf(2 * rows, 4 * d)]
    return pl.pallas_call(
        layer_kernel,
        in_specs=[hbm] * 2 + [vmem] * 6 + [hbm, vmem] + [hbm] * 7,
        out_specs=[hbm] * len(out_shape),
        out_shape=out_shape,
        scratch_shapes=[
            pltpu.SemaphoreType.DMA((330 + 36 * quads,)),
            pltpu.VMEM((2 * rows, width), BF16),
            pltpu.VMEM((2 * rows, width), BF16),
            pltpu.VMEM((width, 2 * rows), BF16),
            pltpu.VMEM((width, 2 * rows), BF16),
            pltpu.VMEM((2, 2 * rows, 2 * d), BF16),
            pltpu.VMEM((width // 2, widest), BF16),
            pltpu.VMEM((SLOTS, width // 2, widest), BF16),
            pltpu.VMEM((2, shard, widest), F32),
            pltpu.VMEM((rows, width), BF16),
            pltpu.VMEM((4, width), F32),
            pltpu.VMEM((3 + quads, 4, width), F32),
        ],
        compiler_params=pltpu.CompilerParams(
            collective_id=0, has_side_effects=True, vmem_limit_bytes=VMEM_LIMIT
        ),
        name="layer",
    )(
        tokens,
        out_grad,
        attn_gain[None],
        mlp_gain[None],
        q_gain[None],
        k_gain[None],
        *arrays,
    )[:10]


def local(
    tokens,
    out_grad,
    lengths,
    attn_gain,
    q_weight,
    key_matrix,
    value_matrix,
    o_weight,
    q_gain,
    k_gain,
    mlp_gain,
    gate_weight,
    up_weight,
    down_weight,
):
    rows = tokens.shape[0]
    d = q_gain.shape[0]
    me = lax.axis_index("dp")
    assert key_matrix.shape[1] == 4 * d and q_weight.shape[1] == 8 * d
    chip_index = (me // 2) * 2 * rows + jnp.arange(2 * rows, dtype=jnp.int32)
    cosine, sine_vals = angles(chip_index - starts_of(chip_index, lengths), d)
    sine_signed = jnp.concatenate([-sine_vals[:, : d // 2], sine_vals[:, d // 2 :]], 1)
    q_index = (me // 4) * 4 * rows + jnp.arange(4 * rows, dtype=jnp.int32)
    q_start = starts_of(q_index, lengths)
    output, input_grad, gains, g_q, g_k, g_v, g_o, g_gate, g_up, g_down = whole_layer(
        tokens,
        out_grad,
        attn_gain,
        mlp_gain,
        q_gain,
        k_gain,
        cosine,
        sine_signed,
        q_start[:, None],
        q_start[None, :],
        q_weight,
        key_matrix,
        value_matrix,
        o_weight,
        gate_weight,
        up_weight,
        down_weight,
    )
    return (
        output,
        input_grad,
        gains[0],
        g_q,
        g_k,
        g_v,
        g_o,
        gains[2, :d],
        gains[3, :d],
        gains[1],
        g_gate,
        g_up,
        g_down,
    )


def solution(mesh):
    rows, weight = P("dp", None), P("dp", "tensor")
    placed = (
        (rows, rows) + (P(),) * 2 + (weight,) * 4 + (P(),) * 3 + (weight,) * 3
    )
    return jax.shard_map(
        local,
        mesh=mesh,
        in_specs=placed,
        out_specs=(rows, rows, P()) + (weight,) * 4 + (P(),) * 3 + (weight,) * 3,
        check_vma=False,
    )
```

time: 2550 us -> 676 us (0.27)
  waiting for transfers between devices: 1700 us -> 0 us
  Pallas kernels: 0 us -> 638 us
  matrix products: 359 us -> 0 us
  starting transfers between devices: 136 us -> 0 us
  other arithmetic: 121 us -> 5.83 us
  local copies, waits for them, and re-layouts: 120 us -> 16.7 us
  blocking collectives: 66.9 us -> 0 us
    reduce_scatter x7 -> x0, waiting for transfers between devices: 1040 us -> none  [the longest x1 249 us: local(): lax.psum_scatter(grad_up, 'dp', scatter_dimension=0, tiled=True)]
    pallas_call x0 -> x1, Pallas kernels: none -> 638 us  [whole_layer(): pl.pallas_call(layer_kernel, in_specs=[hbm] * 2 + [vmem] * 6 + [hbm, vmem...]
    dot_general x84 -> x0, matrix products: 359 us -> none  [the longest x9 53.9 us: value_step(): jnp.einsum('nlcu,une->cnle', prob_reduced, retained_rows[1], preferred_el...]
    all_gather x7 -> x0, waiting for transfers between devices: 352 us -> none  [the longest x1 98.3 us: local(): lax.all_gather(up_weight, 'dp', axis=0, tiled=True)]
    psum x3 -> x0, waiting for transfers between devices: 189 us -> none  [the longest x1 90 us: local(): lax.psum(attn_part.astype(jnp.bfloat16), 'tensor').astype(jnp.float32)]
    ppermute x16 -> x0, starting transfers between devices: 135 us -> none  [shifted(): return lax.ppermute(value, axis, pairs)]
    ppermute x16 -> x0, waiting for transfers between devices: 113 us -> none  [shifted(): return lax.ppermute(value, axis, pairs)]
    psum x2 -> x0, blocking collectives: 66.9 us -> none  [the longest x1 62 us: local(): lax.psum((grad_attn_local, q_gain_local, k_gain_local, grad_mlp_gain), 'dp')]
  transfers between devices with their start and end apart: 33 -> 0, of which waited for: 31 -> 0; matrix products, arithmetic and copies ran while one was open for 12% -> 0% of each run, Pallas kernels for 0% -> 0%
where the time goes in v3:
time: 676 us; the launch traced here: 662 us
  Pallas kernels  638 us (94%)
  local copies, waits for them, and re-layouts  16.7 us (2%)
    pallas_call x1, Pallas kernels, whole_layer(): pl.pallas_call(layer_kernel, in_specs=[hbm] * 2 + [vmem] * 6 + [hbm, vmem...  638 us

profile of v3, /device:TPU:0, one launch (start us, length us, event | category | flops | bytes accessed | tf_op | source)
XLA Modules:
  0.0 662.2 jit_solution(9090824650308728993)
XLA Ops:
  0.7 0.8 reduce-window.8
  1.5 0.7 bitcast_subtract_fusion
  2.2 0.1 select_reduce_fusion.1
  2.3 0.1 select_reduce_fusion
  2.4 0.0 copy-start.8
  2.4 0.2 broadcast_multiply_fusion
  2.6 2.7 fusion
  5.3 0.2 slice_negate_fusion
  5.5 1.0 pad_maximum_fusion.1.refs_7_
  6.5 0.0 copy-done.8
  6.5 1.3 copy.28.refs_8_
  7.9 638.5 %layer.1 = (bf16[512,2048]{1,0:T(8,128)(2,1)}, f32[512,2048]{1,0:T(8,128)}, f32[4,2048]{1,0:T(4,128)}, f32[128,1024]{1,0:T(8,128)}, f32[128,512]{1,0:T(8,128)}, ...) custom-call(bf16[512,2048]{1,0:T(8,128)(2,1)} %refs_0_.1, ...), custom_call_target="tpu_custom_call" | custom-call | tf_op jit(solution)/shard_map/layer/pallas_call | solution.py:1483
  646.4 1.3 slice_bitcast_fusion
  647.6 1.4 fusion.2
  649.1 0.0 copy-start
  649.1 3.3 copy.38
  652.4 0.0 copy-done
  652.4 0.0 copy-start.5
  652.4 0.0 copy-start.7
  652.4 0.0 copy-start.6
  652.4 0.0 copy-start.4
  652.4 2.0 copy.39
  654.4 0.0 copy-done.5
  654.4 0.0 copy-start.3
  654.4 0.8 copy.40
  655.2 0.0 copy-done.7
  655.2 0.7 copy.41
  655.9 0.0 copy-done.6
  655.9 0.7 copy.42
  656.6 0.0 copy-done.4
  656.7 0.0 copy-start.2
  656.7 0.8 copy.43
  657.4 0.0 copy-done.3
  657.5 1.1 copy.44
  658.6 0.0 copy-done.2
  658.6 0.0 copy-start.1
  658.6 1.1 copy.45
  659.7 0.8 copy-done.1
  660.6 1.1 copy.46
  (4 shorter events, 0.0 us)
Async XLA Ops:
  2.4 4.2 copy-start.8
  649.1 3.3 copy-start
  652.4 2.0 copy-start.5
  652.4 2.8 copy-start.7
  652.4 3.5 copy-start.6
  652.4 4.2 copy-start.4
  654.4 3.0 copy-start.3
  656.7 1.9 copy-start.2
  658.6 2.0 copy-start.1

commit v4 on v3

--- a/solution.py
+++ b/solution.py
@@ -407,45 +407,44 @@
 PAIRED = (4, 5)
 SCHEDULE = {
     "G": (
+        ("z", 6, 0),
+    ),
+    "P0": (
+        ("z", 1, 0),
+        ("z", 6, 1),
+        ("z", 6, 2),
+        ("z", 1, 1),
+    ),
+    "P1": (
+        ("x", 6, 2),
+        ("x", 6, 1),
+    ),
+    "P1b": (
+        ("x", 1, 0),
+        ("x", 5, 0),
+        ("x", 1, 1),
+    ),
+    "P2": (
+        ("z", 1, 2),
+        ("z", 1, 3),
+        ("x", 6, 0),
+        ("x", 1, 2),
         ("z", 0, 0),
-        ("z", 6, 0),
-    ),
-    "P0": (
-        ("z", 3, 0),
-        ("z", 1, 0),
-        ("z", 0, 1),
-    ),
-    "P1": (
-        ("x", 0, 0),
-        ("z", 6, 1),
-    ),
-    "P1b": (
-        ("x", 6, 1),
-        ("x", 0, 1),
-        ("z", 6, 2),
-    ),
-    "P2": (
-        ("x", 5, 0),
+        ("z", 6, 3),
     ),
     "P3": (
         ("x", 4, 0),
-        ("z", 1, 1),
-        ("x", 6, 0),
-        ("z", 6, 3),
+        ("z", 0, 1),
     ),
     "P3b": (
+        ("x", 1, 3),
         ("x", 6, 3),
-        ("x", 1, 1),
-        ("x", 6, 2),
-        ("z", 1, 2),
-    ),
-    "P4": (
-        ("z", 1, 3),
+        ("z", 5, 0),
         ("z", 0, 2),
-        ("x", 0, 2),
     ),
     "P5": (
-        ("z", 3, 1),
+        ("z", 3, 0),
+        ("x", 0, 0),
     ),
     "P6": (
         ("z", 0, 3),
@@ -453,54 +452,51 @@
     ),
     "P7": (
         ("x", 0, 3),
-        ("x", 1, 0),
+        ("x", 0, 1),
+    ),
+    "P8": (
+        ("z", 2, 1),
+        ("x", 0, 2),
+        ("z", 2, 2),
+        ("z", 4, 0),
+        ("x", 2, 1),
+        ("x", 2, 2),
+    ),
+    "P8b": (
+        ("x", 2, 0),
+        ("z", 3, 1),
         ("z", 3, 2),
-        ("z", 2, 1),
-    ),
-    "P8": (
-        ("x", 2, 0),
+        ("x", 3, 1),
+        ("z", 2, 3),
         ("x", 3, 0),
-        ("z", 2, 2),
-        ("x", 1, 2),
-        ("x", 1, 3),
-        ("x", 2, 1),
-    ),
-    "P8b": (
-        ("z", 4, 0),
+    ),
+    "P9": (
+        ("z", 5, 1),
+        ("x", 2, 3),
+        ("z", 3, 3),
+    ),
+    "F0a": (
+        ("z", 4, 1),
+    ),
+    "F1a": (
         ("x", 3, 2),
-        ("z", 4, 1),
-        ("z", 2, 3),
-    ),
-    "P9": (
-        ("x", 2, 3),
-        ("z", 5, 0),
-        ("x", 2, 2),
-    ),
-    "F0b": (
-        ("z", 3, 3),
-    ),
-    "F1a": (
         ("x", 3, 3),
-        ("x", 3, 1),
     ),
     "F1b": (
+        ("s", 0),
+    ),
+    "F2a": (
         ("z", 4, 2),
-        ("s", 0),
-    ),
-    "F2a": (
-        ("z", 5, 1),
-    ),
-    "F2b": (
+    ),
+    "F3a": (
+        ("s", 1),
         ("z", 5, 2),
-    ),
-    "F3a": (
         ("z", 4, 3),
-        ("s", 1),
     ),
     "F4a": (
         ("z", 5, 3),
     ),
-    "F5a": (
+    "F5b": (
         ("a", 0),
         ("s", 2),
     ),
@@ -516,50 +512,52 @@
     ),
     "B3": (
         ("p", 1),
-        ("f", 0),
+        ("a", 3),
         ("s", 4),
-        ("a", 3),
     ),
     "B4": (
         ("p", 2),
-    ),
-    "C2": (
+        ("s", 6),
+    ),
+    "C2e": (
+        ("f", 1),
+    ),
+    "C1": (
         ("s", 5),
     ),
     "C1e": (
-        ("s", 6),
+        ("p", 3),
     ),
     "C0": (
         ("a", 4),
     ),
     "D0": (
-        ("p", 3),
+        ("f", 3),
+        ("f", 0),
         ("a", 5),
-        ("f", 1),
     ),
     "D1": (
         ("f", 2),
     ),
     "D2": (
+        ("a", 6),
         ("p", 4),
-        ("a", 6),
     ),
     "D3": (
         ("p", 5),
-        ("f", 3),
         ("a", 7),
-        ("f", 4),
     ),
     "D4": (
         ("p", 6),
+        ("a", 8),
         ("p", 7),
-        ("a", 8),
+        ("f", 4),
     ),
     "D5": (
         ("p", 8),
         ("f", 5),
+        ("f", 7),
         ("f", 6),
-        ("f", 7),
         ("f", 8),
     ),
 }
@@ -962,12 +960,9 @@
             to = pl.ds(my_at + i * step, step)
             sa[to, :] = rms_rows(mid, mlp_gain[...]).astype(BF16)
             second_copies.append(n.send(sa.at[to], sa.at[to], n.other_core()))
-            ta[:, to] = sa[to, :].T
             mid_copy[0].wait()
         for i in range(steps):
             second_copies[i].wait_recv()
-            to = pl.ds(their_at + i * step, step)
-            ta[:, to] = sa[to, :].T
         tick("P9")
         n.finish()
 
@@ -1017,6 +1012,10 @@
         def at_tile(f, k, fn):
             pl.when(f == k)(fn)
 
+        def flip_second(i):
+            at = part(i, step)
+            ta[:, at] = sa[at, :].T
+
         def tile(f, carry):
             slot = lax.rem(f, 2)
 
@@ -1059,6 +1058,10 @@
 
             for c in range(tiles):
                 at_tile(f, c, partial(tick, "F%db" % c))
+            @pl.when(f == 0)
+            def _():
+                loop(2 * rows // step, flip_second)
+
             for xr in range(2):
                 for q in range(quads):
                     at = pl.ds(row_block(xr, q), block)
@@ -1372,6 +1375,7 @@
         at_groups[2].start()
         tick("D3")
 
+        tok_load = load([(tokens, xa.at[pl.ds(rows, rows)])])
         mlp_copy.wait_recv()
         for i in range(steps):
             at = pl.ds(i * step, step)
@@ -1385,12 +1389,13 @@
             tmp_low[0] = (tmp[...] + (tmp_low[1].astype(F32) + tmp_low[0].astype(F32))).astype(BF16)
             load_now([(tmp_low.at[0], output.at[at])])
         tick("D4")
+        tok_load[0].wait()
         for i in range(steps):
             at = pl.ds(i * step, step)
             low_copies[i].wait_recv()
-            load_now([(low_land.at[2, at], tmp_low.at[0]), (tokens.at[at], tmp_low.at[1])])
+            load_now([(low_land.at[2, at], tmp_low.at[0])])
             d_first = low_send[at, :].astype(F32) + tmp_low[0].astype(F32)
-            back, gain_part = norm_back(tmp_low[1].astype(F32), attn_gain[...], d_first)
+            back, gain_part = norm_back(xa[pl.ds(rows + i * step, step), :].astype(F32), attn_gain[...], d_first)
             gains[0:1, :] += gain_part
             d_middle[at, :] = d_middle[at, :] + back
             n.keep(d_middle.at[at], input_grad.at[at])

time: 676 us -> 685 us (1.013)
  Pallas kernels: 638 us -> 648 us
    pallas_call x1, Pallas kernels: 638 us -> 648 us  [whole_layer(): pl.pallas_call(layer_kernel, in_specs=[hbm] * 2 + [vmem] * 6 + [hbm, vmem...]
where the time goes in v4:
time: 685 us; the launch traced here: 672 us
  Pallas kernels  648 us (95%)
  local copies, waits for them, and re-layouts  16.7 us (2%)
    pallas_call x1, Pallas kernels, whole_layer(): pl.pallas_call(layer_kernel, in_specs=[hbm] * 2 + [vmem] * 6 + [hbm, vmem...  648 us

profile of v4, /device:TPU:0, one launch (start us, length us, event | category | flops | bytes accessed | tf_op | source)
XLA Modules:
  0.0 671.5 jit_solution(8456047715188113121)
XLA Ops:
  0.7 0.8 reduce-window.8
  1.5 0.7 bitcast_subtract_fusion
  2.2 0.1 select_reduce_fusion.1
  2.3 0.1 select_reduce_fusion
  2.4 0.0 copy-start.8
  2.4 0.2 broadcast_multiply_fusion
  2.6 2.7 fusion
  5.3 0.2 slice_negate_fusion
  5.5 1.0 pad_maximum_fusion.1.refs_7_
  6.5 0.0 copy-done.8
  6.5 1.3 copy.28.refs_8_
  7.9 647.9 %layer.1 = (bf16[512,2048]{1,0:T(8,128)(2,1)}, f32[512,2048]{1,0:T(8,128)}, f32[4,2048]{1,0:T(4,128)}, f32[128,1024]{1,0:T(8,128)}, f32[128,512]{1,0:T(8,128)}, ...) custom-call(bf16[512,2048]{1,0:T(8,128)(2,1)} %refs_0_.1, ...), custom_call_target="tpu_custom_call" | custom-call | tf_op jit(solution)/shard_map/layer/pallas_call | solution.py:1488
  655.8 1.3 slice_bitcast_fusion
  657.0 1.4 fusion.2
  658.5 0.0 copy-start
  658.5 3.3 copy.38
  661.8 0.0 copy-done
  661.8 0.0 copy-start.5
  661.8 0.0 copy-start.7
  661.8 0.0 copy-start.6
  661.8 0.0 copy-start.4
  661.8 2.0 copy.39
  663.8 0.0 copy-done.5
  663.8 0.0 copy-start.3
  663.8 0.8 copy.40
  664.6 0.0 copy-done.7
  664.6 0.7 copy.41
  665.3 0.0 copy-done.6
  665.3 0.7 copy.42
  666.0 0.0 copy-done.4
  666.0 0.0 copy-start.2
  666.0 0.8 copy.43
  666.8 0.0 copy-done.3
  666.8 1.1 copy.44
  668.0 0.0 copy-done.2
  668.0 0.0 copy-start.1
  668.0 1.1 copy.45
  669.1 0.8 copy-done.1
  670.0 1.1 copy.46
  (4 shorter events, 0.0 us)
Async XLA Ops:
  2.4 4.2 copy-start.8
  658.5 3.3 copy-start
  661.8 2.0 copy-start.5
  661.8 2.8 copy-start.7
  661.8 3.5 copy-start.6
  661.8 4.2 copy-start.4
  663.8 3.0 copy-start.3
  666.0 1.9 copy-start.2
  668.0 2.0 copy-start.1
